TPU v7x, 32 devices: a whole 2x2x4 slice. The times are simulated.
32 devices in a mesh: wide: 8 (over z, y), seq: 4 (over x, core).
Axes of the slice: x: 2, y: 2, z: 4, core: 2. Of those that a mesh axis runs over, the one named last changes fastest.
Arguments:
- tokens: bfloat16 [48, 580, 512], P('wide', 'seq'), may hold values from -6 to 6
- key_mask: int32 [48, 580], P('wide'), may hold values from 0 to 1, as said below
- expert_ids: int32 [48, 580, 2], P('wide', 'seq'), may hold values from 0 to 3, as said below
- ln1_gain: bfloat16 [512], P('wide'), may hold values from 0.5 to 1.5
- ln1_bias: bfloat16 [512], P('wide'), may hold values from -4 to 4
- qkv_weight: bfloat16 [512, 1536], P('wide'), may hold values from -0.25 to 0.25
- proj_weight: bfloat16 [512, 512], P('wide'), may hold values from -6 to 6
- ln2_gain: bfloat16 [512], P('wide'), may hold values from 0.5 to 1.5
- ln2_bias: bfloat16 [512], P('wide'), may hold values from -4 to 4
- router_weight: bfloat16 [512, 4], P('wide'), may hold values from -0.1875 to 0.1875
- up_weight: bfloat16 [4, 512, 2048], P(None, 'wide'), may hold values from -0.25 to 0.25
- down_weight: bfloat16 [4, 2048, 512], P(None, 'wide'), may hold values from -0.375 to 0.375
- cotangent: bfloat16 [48, 580, 512], P('wide', 'seq'), may hold values from -6 to 6
Outputs:
- layer_out: bfloat16 [48, 580, 512], P('wide', 'seq')
- input_grad: float32 [48, 580, 512], P('wide', 'seq')
- grad_ln1_gain: float32 [512], P('wide')
- grad_ln1_bias: float32 [512], P('wide')
- grad_qkv: float32 [512, 1536], P('wide')
- grad_proj: float32 [512, 512], P('wide')
- grad_ln2_gain: float32 [512], P('wide')
- grad_ln2_bias: float32 [512], P('wide')
- grad_router: float32 [512, 4], P('wide')
- grad_up: float32 [4, 512, 2048], P(None, 'wide')
- grad_down: float32 [4, 2048, 512], P(None, 'wide')
Inputs may be any that keep to these rules, and one draw needn't show every extreme that they name: `key_mask`: position 0 of every image is 1, the last 3 positions are 0. `expert_ids`: the two numbers of a token differ. Among the 290 tokens that one device holds of one micro-batch (images m * 2 to (m + 1) * 2 - 1 of its images, all its positions), every expert is named by exactly 145 tokens.
All inputs are finite; a program needn't handle non-finite values.
Results may differ from a plain program's by a relative error of at most 0.0093.
Values may be sent and summed in bfloat16 or wider, within the bound.
No kernel may reach another device: no remote copies, remote signals or barrier semaphores. Data moves between devices by JAX's collectives and lax.ppermute only.
A program may use at most 136 MiB of HBM per device.

v0:
```python
import math

import jax
import jax.numpy as jnp
from jax import lax
from jax.sharding import PartitionSpec as P

H = 8
E = 4
IMG_MB = 2


EPSILON = 1e-06


def layer_norm(values, gain, offset):
    center = values - jnp.mean(values, axis=-1, keepdims=True)
    spread = jnp.mean(center * center, axis=-1, keepdims=True)
    return center * lax.rsqrt(spread + EPSILON) * gain + offset


def gelu_exact(values):
    return jax.nn.gelu(values, approximate=False)


def shards(
    tokens,
    key_mask,
    expert_ids,
    ln1_gain,
    ln1_bias,
    qkv_weight,
    proj_weight,
    ln2_gain,
    ln2_bias,
    router_weight,
    up_weight,
    down_weight,
    cotangent,
):
    n_seq = lax.axis_size("seq")
    images, quarter, width = tokens.shape
    length = key_mask.shape[1]
    batch_size = IMG_MB
    micro_count = images // batch_size
    head_dim = width // H
    local_heads = H // n_seq
    group_width = local_heads * head_dim
    scaling = 1.0 / math.sqrt(head_dim)
    row_count = batch_size * quarter
    capacity = row_count // 2
    expert_range = jnp.arange(E, dtype=jnp.int32)

    def masked_scores(queries, key_rows, valid):
        raw_scores = (
            jnp.einsum("bqhd,bkhd->bhqk", queries, key_rows, preferred_element_type=jnp.float32)
            * scaling
        )
        return jnp.where(valid[:, None, None, :], raw_scores, -1e30)

    gathered = None
    layer_parts = []
    input_parts = []
    totals = None
    for micro in range(micro_count):
        gathered = (
            lax.all_gather(ln1_gain, "wide", axis=0, tiled=True),
            lax.all_gather(ln1_bias, "wide", axis=0, tiled=True),
            lax.all_gather(qkv_weight, "wide", axis=0, tiled=True),
            lax.all_gather(proj_weight, "wide", axis=0, tiled=True),
            lax.all_gather(ln2_gain, "wide", axis=0, tiled=True),
            lax.all_gather(ln2_bias, "wide", axis=0, tiled=True),
            lax.all_gather(router_weight, "wide", axis=0, tiled=True),
            lax.all_gather(up_weight, "wide", axis=1, tiled=True),
            lax.all_gather(down_weight, "wide", axis=1, tiled=True),
        )
        (
            gain_one,
            offset_one,
            qkv_full,
            proj_full,
            gain_two,
            offset_two,
            router_full,
            up_full,
            down_full,
        ) = gathered
        first_image = micro * batch_size
        last_image = first_image + batch_size
        inputs = tokens[first_image:last_image].astype(jnp.float32).reshape(row_count, width)
        normed_one, norm_back_one = jax.vjp(
            layer_norm, inputs, gain_one.astype(jnp.float32), offset_one.astype(jnp.float32)
        )
        hidden_one = normed_one.astype(jnp.bfloat16)
        packed = jnp.dot(hidden_one, qkv_full, preferred_element_type=jnp.float32).astype(
            jnp.bfloat16
        )
        packed = packed.reshape(batch_size, quarter, 3, n_seq, group_width)
        by_heads = lax.all_to_all(packed, "seq", split_axis=3, concat_axis=1, tiled=True).reshape(
            batch_size, length, 3, local_heads, head_dim
        )
        micro_queries = by_heads[:, :, 0]
        micro_key_rows = by_heads[:, :, 1]
        value_rows = by_heads[:, :, 2]
        micro_valid = key_mask[first_image:last_image] > 0
        scores = masked_scores(micro_queries, micro_key_rows, micro_valid)
        peak = jnp.max(scores, axis=-1, keepdims=True)
        exponent = jnp.exp(scores - peak)
        row_total = jnp.sum(exponent, axis=-1, keepdims=True)
        probs_low = (exponent / row_total).astype(jnp.bfloat16)
        log_total = peak + jnp.log(row_total)
        attended = jnp.einsum(
            "bhqk,bkhd->bqhd", probs_low, value_rows, preferred_element_type=jnp.float32
        ).astype(jnp.bfloat16)
        merged = lax.all_to_all(
            attended.reshape(batch_size, length, 1, group_width),
            "seq",
            split_axis=1,
            concat_axis=2,
            tiled=True,
        ).reshape(row_count, width)
        middle = inputs + jnp.dot(merged, proj_full, preferred_element_type=jnp.float32)
        normed_two, norm_back_two = jax.vjp(
            layer_norm, middle, gain_two.astype(jnp.float32), offset_two.astype(jnp.float32)
        )
        hidden_two = normed_two.astype(jnp.bfloat16)
        logits = jnp.dot(hidden_two, router_full, preferred_element_type=jnp.float32)
        router_exp = jnp.exp(logits - jnp.max(logits, axis=-1, keepdims=True))
        router = router_exp / jnp.sum(router_exp, axis=-1, keepdims=True)
        id_block = expert_ids[first_image:last_image].reshape(row_count, 2)
        chosen = (id_block[:, 0:1] == expert_range) | (id_block[:, 1:2] == expert_range)
        combined = router * chosen.astype(jnp.float32)
        ranking = jnp.cumsum(chosen.astype(jnp.int32), axis=0) - 1
        target_slot = jnp.where(chosen, ranking, capacity)
        row_index = jnp.broadcast_to(
            jnp.arange(row_count, dtype=jnp.int32)[:, None], (row_count, E)
        )
        expert_index = jnp.broadcast_to(expert_range[None, :], (row_count, E))
        slot_rows = (
            jnp.zeros((E, capacity + 1), jnp.int32)
            .at[expert_index, target_slot]
            .set(row_index)[:, :capacity]
        )
        expert_in = hidden_two[slot_rows]
        slot_weight = combined[slot_rows, expert_range[:, None]]
        hidden_pre = jnp.einsum(
            "ecd,edf->ecf", expert_in, up_full, preferred_element_type=jnp.float32
        )
        activated_full, gelu_back = jax.vjp(gelu_exact, hidden_pre)
        activated = activated_full.astype(jnp.bfloat16)
        returned = jnp.einsum(
            "ecf,efd->ecd", activated, down_full, preferred_element_type=jnp.float32
        )
        mixture = (
            jnp.zeros((row_count, width), jnp.float32)
            .at[slot_rows]
            .add(returned * slot_weight[..., None])
        )
        layer = middle + mixture
        grad_out = cotangent[first_image:last_image].astype(jnp.float32).reshape(row_count, width)
        slot_grad = grad_out[slot_rows]
        return_low = (slot_grad * slot_weight[..., None]).astype(jnp.bfloat16)
        gate_slot = jnp.sum(slot_grad * returned, axis=-1)
        gate_grad = (
            jnp.zeros((row_count, E), jnp.float32)
            .at[slot_rows, expert_range[:, None]]
            .add(gate_slot)
        )
        logit_grad = (
            router * (gate_grad - jnp.sum(router * gate_grad, axis=-1, keepdims=True))
        ).astype(jnp.bfloat16)
        grad_router = jnp.dot(hidden_two.T, logit_grad, preferred_element_type=jnp.float32)
        grad_down = jnp.einsum(
            "ecf,ecd->efd", activated, return_low, preferred_element_type=jnp.float32
        )
        act_grad = jnp.einsum(
            "ecd,efd->ecf", return_low, down_full, preferred_element_type=jnp.float32
        )
        pre_grad = gelu_back(act_grad)[0].astype(jnp.bfloat16)
        grad_up = jnp.einsum(
            "ecd,ecf->edf", expert_in, pre_grad, preferred_element_type=jnp.float32
        )
        in_slot_grad = jnp.einsum(
            "ecf,edf->ecd", pre_grad, up_full, preferred_element_type=jnp.float32
        )
        hidden_two_grad = jnp.zeros((row_count, width), jnp.float32).at[slot_rows].add(in_slot_grad)
        hidden_two_grad = hidden_two_grad + jnp.dot(
            logit_grad, router_full.T, preferred_element_type=jnp.float32
        )
        middle_norm_grad, grad_gain_two, grad_offset_two = norm_back_two(hidden_two_grad)
        grad_middle = grad_out + middle_norm_grad
        middle_low = grad_middle.astype(jnp.bfloat16)
        grad_proj = jnp.dot(merged.T, middle_low, preferred_element_type=jnp.float32)
        attended_grad = jnp.dot(middle_low, proj_full.T, preferred_element_type=jnp.float32).astype(
            jnp.bfloat16
        )
        attended_grad = attended_grad.reshape(batch_size, quarter, n_seq, group_width)
        heads_grad = lax.all_to_all(
            attended_grad, "seq", split_axis=2, concat_axis=1, tiled=True
        ).reshape(batch_size, length, local_heads, head_dim)
        scores_again = masked_scores(micro_queries, micro_key_rows, micro_valid)
        probs = jnp.exp(scores_again - log_total)
        value_grad = jnp.einsum(
            "bhqk,bqhd->bkhd",
            probs.astype(jnp.bfloat16),
            heads_grad,
            preferred_element_type=jnp.float32,
        )
        prob_grad = jnp.einsum(
            "bqhd,bkhd->bhqk", heads_grad, value_rows, preferred_element_type=jnp.float32
        )
        delta_sum = jnp.sum(probs * prob_grad, axis=-1, keepdims=True)
        score_grad = (probs * (prob_grad - delta_sum)).astype(jnp.bfloat16)
        query_grad = (
            jnp.einsum(
                "bhqk,bkhd->bqhd", score_grad, micro_key_rows, preferred_element_type=jnp.float32
            )
            * scaling
        )
        key_grad = (
            jnp.einsum(
                "bhqk,bqhd->bkhd", score_grad, micro_queries, preferred_element_type=jnp.float32
            )
            * scaling
        )
        stacked = jnp.stack([query_grad, key_grad, value_grad], axis=2).astype(jnp.bfloat16)
        stacked = stacked.reshape(batch_size, length, 3, 1, group_width)
        packed_grad = lax.all_to_all(
            stacked, "seq", split_axis=1, concat_axis=3, tiled=True
        ).reshape(row_count, 3 * width)
        grad_qkv = jnp.dot(hidden_one.T, packed_grad, preferred_element_type=jnp.float32)
        hidden_one_grad = jnp.dot(packed_grad, qkv_full.T, preferred_element_type=jnp.float32)
        input_norm_grad, grad_gain_one, grad_offset_one = norm_back_one(hidden_one_grad)
        grad_input = grad_middle + input_norm_grad
        grads = (
            grad_gain_one,
            grad_offset_one,
            grad_qkv,
            grad_proj,
            grad_gain_two,
            grad_offset_two,
            grad_router,
            grad_up,
            grad_down,
        )
        layer_block, input_block, grads = (
            layer.astype(jnp.bfloat16).reshape(batch_size, quarter, width),
            grad_input.reshape(batch_size, quarter, width),
            grads,
        )
        layer_parts.append(layer_block)
        input_parts.append(input_block)
        settled = lax.psum(
            (
                lax.psum_scatter(grads[0], "wide", scatter_dimension=0, tiled=True),
                lax.psum_scatter(grads[1], "wide", scatter_dimension=0, tiled=True),
                lax.psum_scatter(grads[2], "wide", scatter_dimension=0, tiled=True),
                lax.psum_scatter(grads[3], "wide", scatter_dimension=0, tiled=True),
                lax.psum_scatter(grads[4], "wide", scatter_dimension=0, tiled=True),
                lax.psum_scatter(grads[5], "wide", scatter_dimension=0, tiled=True),
                lax.psum_scatter(grads[6], "wide", scatter_dimension=0, tiled=True),
                lax.psum_scatter(grads[7], "wide", scatter_dimension=1, tiled=True),
                lax.psum_scatter(grads[8], "wide", scatter_dimension=1, tiled=True),
            ),
            "seq",
        )
        totals = (
            settled
            if totals is None
            else tuple((left + right for left, right in zip(totals, settled)))
        )
    return (
        jnp.concatenate(layer_parts, axis=0),
        jnp.concatenate(input_parts, axis=0),
        totals[0],
        totals[1],
        totals[2],
        totals[3],
        totals[4],
        totals[5],
        totals[6],
        totals[7],
        totals[8],
    )


def solution(mesh):
    placed = (
        P("wide", "seq", None),
        P("wide", None),
        P("wide", "seq", None),
        P("wide"),
        P("wide"),
        P("wide", None),
        P("wide", None),
        P("wide"),
        P("wide"),
        P("wide", None),
        P(None, "wide", None),
        P(None, "wide", None),
        P("wide", "seq", None),
    )
    return jax.shard_map(
        shards,
        mesh=mesh,
        in_specs=placed,
        out_specs=(
            P("wide", "seq", None),
            P("wide", "seq", None),
            P("wide"),
            P("wide"),
            P("wide", None),
            P("wide", None),
            P("wide"),
            P("wide"),
            P("wide", None),
            P(None, "wide", None),
            P(None, "wide", None),
        ),
        check_vma=False,
    )
```

profile of v0, /device:TPU:0, one launch (start us, length us, event | category | flops | bytes accessed | tf_op | source)
XLA Modules:
  0.0 1479.3 jit_solution(14466146726880006982)
XLA Ops:
  45.0 23.2 %all-reduce.14 = (bf16[512]{0:T(512)(128)(2,1)S(1)}, bf16[512]{0:T(512)(128)(2,1)S(1)}, bf16[512]{0:T(512)(128)(2,1)S(1)}, bf16[512]{0:T(512)(128)(2,1)S(1)}) all-reduce(bf16[512]{0:T(512)(128)(2,1)S(1)} %dynamic-update-slice.1, bf16[512]{0:T(512)(128)(2,1)S(1)} %dynamic-update-slice, ...), channel_id=1, replica_groups=mesh['wide'=8,'seq'=4] {'wide'}, use_global_device_ids=true, to_apply=%add.4 | all-reduce | flops 2048 | bytes 8192
  70.9 16.4 %all-gather = bf16[8,64,4]{1,2,0:T(4,128)(2,1)S(1)} all-gather(bf16[1,64,4]{1,2,0:T(4,128)(2,1)S(1)} %bitcast.400), channel_id=1, replica_groups=mesh['wide'=8,'seq'=4] {'wide'}, dimensions={0}, use_global_device_ids=true | all-gather | bytes 4608 | tf_op jit(solution)/shard_map/all_gather | solution.py:73
  126.8 33.5 %all_gather.21 = bf16[512,512]{1,0:T(8,128)(2,1)S(1)} all-gather(bf16[64,512]{1,0:T(8,128)(2,1)S(1)} %copy-done.91), channel_id=1, replica_groups=mesh['wide'=8,'seq'=4] {'wide'}, dimensions={0}, use_global_device_ids=true | all-gather | bytes 589824 | tf_op jit(solution)/shard_map/all_gather | solution.py:70
  274.3 12.3 multiply_convert_fusion.5
  286.6 32.1 %all-gather.9.cloned.1.call-done = bf16[4,2048,512]{2,1,0:T(8,128)(2,1)} async-done(((bf16[4,256,512]{2,1,0:T(8,128)(2,1)}), bf16[4,2048,512]{2,1,0:T(8,128)(2,1)}) %all-gather.9.cloned.1.call-update) | async-done | bytes 8388624 | tf_op jit(solution)/shard_map/all_gather | solution.py:75
  325.7 30.5 %scatter_fusion.3 = f32[290,4]{0,1:T(4,128)S(1)} fusion(f32[290,4]{0,1:T(4,128)S(1)} %broadcast.528.clone, s32[580]{0:T(1024)S(1)} %reshape.845, f32[580]{0:T(1024)S(1)} %reshape.847), kind=kCustom, calls=%fused_computation.12 | custom fusion | flops 580 | bytes 11600 | tf_op jit(solution)/shard_map/scatter-add | solution.py:167
  365.2 9.8 add_convert_fusion.2
  392.3 12.2 multiply_convert_fusion.4
  411.4 30.5 %scatter_fusion.5 = f32[290,4]{0,1:T(4,128)S(1)} fusion(f32[290,4]{0,1:T(4,128)S(1)} %broadcast.528.clone.2, s32[580]{0:T(1024)S(1)} %reshape.859, f32[580]{0:T(1024)S(1)} %reshape.861), kind=kCustom, calls=%fused_computation.14 | custom fusion | flops 580 | bytes 11600 | tf_op jit(solution)/shard_map/scatter-add | solution.py:167
  443.4 8.4 gather_fusion.3
  451.9 9.8 add_convert_fusion.1
  478.9 12.2 multiply_convert_fusion.3
  497.9 30.5 %scatter_fusion.7 = f32[290,4]{0,1:T(4,128)S(1)} fusion(f32[290,4]{0,1:T(4,128)S(1)} %broadcast.528.clone.1, s32[580]{0:T(1024)S(1)} %reshape.873, f32[580]{0:T(1024)S(1)} %reshape.875), kind=kCustom, calls=%fused_computation.16 | custom fusion | flops 580 | bytes 11600 | tf_op jit(solution)/shard_map/scatter-add | solution.py:167
  529.8 8.6 gather_fusion.5
  538.5 9.8 add_convert_fusion
  575.6 9.3 scatter_fusion.8
  724.0 10.4 fusion.95
  742.7 20.4 %add_add_fusion = f32[4,2048,512]{2,1,0:T(8,128)} fusion(f32[4,2048,512]{2,1,0:T(8,128)} %fusion.93, f32[4,2048,512]{2,1,0:T(8,128)} %fusion.95, bf16[4,145,2048]{2,1,0:T(8,128)(2,1)} %copy-done.16, f32[4,145,512]{2,1,0:T(8,128)} %reshape.814, f32[4,145]{1,0:T(4,128)S(1)} %copy-done.90), kind=kOutput, calls=%fused_computation.21 | convolution fusion | flops 1225330688 | bytes 53897488 | tf_op jit(solution)/shard_map/ecf,ecd->efd/dot_general | solution.py:173
  764.9 9.4 fusion.182
  782.5 19.2 %add_add_fusion.1 = f32[4,512,2048]{2,1,0:T(8,128)} fusion(f32[4,512,2048]{2,1,0:T(8,128)} %fusion.181, f32[4,512,2048]{2,1,0:T(8,128)} %fusion.182, bf16[4,145,512]{2,1,0:T(8,128)(2,1)} %reshape.784, bf16[4,145,2048]{2,1,0:T(8,128)(2,1)S(1)} %copy-done.20), kind=kOutput, calls=%fused_computation.22 | convolution fusion | flops 1224736768 | bytes 53301248 | tf_op jit(solution)/shard_map/ecd,ecf->edf/dot_general | solution.py:180
  852.7 20.7 %all-reduce.11 = (f32[512]{0:T(512)S(1)}, f32[512]{0:T(512)S(1)}, f32[512]{0:T(512)S(1)}, f32[512]{0:T(512)S(1)}) all-reduce(f32[512]{0:T(512)S(1)} %add_add_fusion.17, f32[512]{0:T(512)S(1)} %add_add_fusion.16, f32[512]{0:T(512)S(1)} %add_add_fusion.15, f32[512]{0:T(512)S(1)} %add_add_fusion.14), channel_id=20, replica_groups=mesh['wide'=8,'seq'=4] {'wide'}, use_global_device_ids=true, to_apply=%region_64.65.clone | all-reduce | flops 2048 | bytes 16384
  873.8 208.4 %reduce-scatter.14.cloned.1.call-done = f32[4,256,512]{2,1,0:T(8,128)} async-done(((f32[4,2048,512]{2,1,0:T(8,128)}), f32[4,256,512]{2,1,0:T(8,128)}) %reduce-scatter.14.cloned.1.call-update) | async-done | bytes 2097168 | tf_op jit(solution)/shard_map/reduce_scatter | solution.py:263
  1082.2 285.6 %reduce-scatter.12.cloned.1.call-done = f32[4,64,2048]{2,1,0:T(8,128)} async-done(((f32[4,512,2048]{2,1,0:T(8,128)}), f32[4,64,2048]{2,1,0:T(8,128)}) %reduce-scatter.12.cloned.1.call-update) | async-done | bytes 2097168 | tf_op jit(solution)/shard_map/reduce_scatter | solution.py:262
  1383.1 81.3 %all-reduce.17.cloned.1.call-done = (f32[64,1536]{1,0:T(8,128)}, f32[64,512]{1,0:T(8,128)}, f32[4,64,2048]{2,1,0:T(8,128)}, f32[4,256,512]{2,1,0:T(8,128)}) async-done(((f32[64,1536]{1,0:T(8,128)}, f32[64,512]{1,0:T(8,128)}, f32[4,64,2048]{2,1,0:T(8,128)}, f32[4,256,512]{2,1,0:T(8,128)}), (f32[64,1536]{1,0:T(8,128)}, f32[64,512]{1,0:T(8,128)}, f32[4,64,2048]{2,1,0:T(8,128)}, ...) | async-done | bytes 4718608 | tf_op jit(solution)/shard_map/psum | solution.py:253
  (721 shorter events, 515.8 us)
Async XLA Ops:
  7.3 80.9 %all-gather.5.cloned.1.call-start = ((), (), s32[]{:S(2)}) async-start(), calls=%async_computation.17 | async-start | bytes 1769472 | tf_op jit(solution)/shard_map/all_gather | solution.py:69
  8.0 258.1 %all-gather.7.cloned.1.call-start = ((), (), s32[]{:S(2)}) async-start(), calls=%async_computation.18 | async-start | bytes 9437184 | tf_op jit(solution)/shard_map/all_gather | solution.py:74
  8.7 310.0 %all-gather.9.cloned.1.call-start = ((), (), s32[]{:S(2)}) async-start(), calls=%async_computation.19 | async-start | bytes 9437184 | tf_op jit(solution)/shard_map/all_gather | solution.py:75
  87.6 473.0 %copy-start.98 = (s32[580]{0:T(1024)}, s32[580]{0:T(1024)S(1)}, u32[]{:S(2)}) copy-start(s32[580]{0:T(1024)S(1)} %reshape.823) | copy-start | bytes 6964
  92.5 30.0 %all-to-all-start.2 = ((bf16[2,145,3,4,128]{4,0,2,1,3:T(2,128)(2,1)}), bf16[2,145,3,4,128]{4,0,2,1,3:T(2,128)(2,1)}, u32[]{:S(2)}, u32[]{:S(2)}) async-start(bf16[2,145,3,4,128]{4,0,2,1,3:T(2,128)(2,1)} %copy.110), calls=%async_computation.2 | async-start | bytes 1781760 | tf_op jit(solution)/shard_map/all_to_all | solution.py:99
  122.5 44.5 %all-to-all-start.4 = ((bf16[2,145,3,4,128]{4,0,2,1,3:T(2,128)(2,1)}), bf16[2,145,3,4,128]{4,0,2,1,3:T(2,128)(2,1)}, u32[]{:S(2)}, u32[]{:S(2)}) async-start(bf16[2,145,3,4,128]{4,0,2,1,3:T(2,128)(2,1)} %copy.122), calls=%async_computation.4 | async-start | bytes 1781760 | tf_op jit(solution)/shard_map/all_to_all | solution.py:99
  167.0 31.9 %all-to-all-start = ((bf16[2,145,3,4,128]{4,0,2,1,3:T(2,128)(2,1)}), bf16[2,145,3,4,128]{4,0,2,1,3:T(2,128)(2,1)}, u32[]{:S(2)}, u32[]{:S(2)}) async-start(bf16[2,145,3,4,128]{4,0,2,1,3:T(2,128)(2,1)} %copy.97), calls=%async_computation | async-start | bytes 1781760 | tf_op jit(solution)/shard_map/all_to_all | solution.py:99
  214.5 14.1 all-to-all-start.1
  228.6 9.8 all-to-all-start.5
  238.4 9.8 all-to-all-start.3
  241.9 603.2 %reduce-scatter.16.cloned.1.call-start = ((), (), s32[]{:S(2)}) async-start(), calls=%async_computation.24 | async-start | bytes 294912
  594.8 14.8 all-to-all-start.10
  598.9 274.8 %reduce-scatter.10.cloned.1.call-start = ((), (), s32[]{:S(2)}) async-start(), calls=%async_computation.21 | async-start | bytes 1179648 | tf_op jit(solution)/shard_map/reduce_scatter | solution.py:258
  609.6 16.9 %all-to-all-start.8 = ((bf16[2,145,4,128]{3,0,1,2:T(2,128)(2,1)}), bf16[2,145,4,128]{3,0,1,2:T(2,128)(2,1)S(1)}, u32[]{:S(2)}, u32[]{:S(2)}) async-start(bf16[2,145,4,128]{3,0,1,2:T(2,128)(2,1)} %copy.144), calls=%async_computation.8 | async-start | bytes 593920 | tf_op jit(solution)/shard_map/all_to_all | solution.py:198
  626.5 17.5 %all-to-all-start.6 = ((bf16[2,145,4,128]{3,0,1,2:T(2,128)(2,1)}), bf16[2,145,4,128]{3,0,1,2:T(2,128)(2,1)}, u32[]{:S(2)}, u32[]{:S(2)}) async-start(bf16[2,145,4,128]{3,0,1,2:T(2,128)(2,1)} %copy.134), calls=%async_computation.6 | async-start | bytes 593920 | tf_op jit(solution)/shard_map/all_to_all | solution.py:198
  660.1 16.3 %all-to-all-start.11 = ((bf16[2,580,3,1,128]{4,0,3,2,1:T(2,128)(2,1)}), bf16[2,580,3,1,128]{4,0,3,2,1:T(2,128)(2,1)S(1)}, u32[]{:S(2)}, u32[]{:S(2)}) async-start(bf16[2,580,3,1,128]{4,0,3,2,1:T(2,128)(2,1)} %pad_maximum_fusion.4), calls=%async_computation.11 | async-start | bytes 1781760 | tf_op jit(solution)/shard_map/all_to_all | solution.py:228
  676.4 19.9 %all-to-all-start.9 = ((bf16[2,580,3,1,128]{4,0,3,2,1:T(2,128)(2,1)}), bf16[2,580,3,1,128]{4,0,3,2,1:T(2,128)(2,1)S(1)}, u32[]{:S(2)}, u32[]{:S(2)}) async-start(bf16[2,580,3,1,128]{4,0,3,2,1:T(2,128)(2,1)} %pad_maximum_fusion.3), calls=%async_computation.9 | async-start | bytes 1781760 | tf_op jit(solution)/shard_map/all_to_all | solution.py:228
  696.3 17.1 %all-to-all-start.7 = ((bf16[2,580,3,1,128]{4,0,3,2,1:T(2,128)(2,1)}), bf16[2,580,3,1,128]{4,0,3,2,1:T(2,128)(2,1)}, u32[]{:S(2)}, u32[]{:S(2)}) async-start(bf16[2,580,3,1,128]{4,0,3,2,1:T(2,128)(2,1)} %pad_maximum_fusion.2), calls=%async_computation.7 | async-start | bytes 1781760 | tf_op jit(solution)/shard_map/all_to_all | solution.py:228
  700.5 173.2 %reduce-scatter.8.cloned.1.call-start = ((), (), s32[]{:S(2)}) async-start(), calls=%async_computation.20 | async-start | bytes 3538944 | tf_op jit(solution)/shard_map/reduce_scatter | solution.py:257
  723.8 358.4 %reduce-scatter.14.cloned.1.call-start = ((), (), s32[]{:S(2)}) async-start(), calls=%async_computation.23 | async-start | bytes 18874368 | tf_op jit(solution)/shard_map/reduce_scatter | solution.py:263
  763.2 604.7 %reduce-scatter.12.cloned.1.call-start = ((), (), s32[]{:S(2)}) async-start(), calls=%async_computation.22 | async-start | bytes 18874368 | tf_op jit(solution)/shard_map/reduce_scatter | solution.py:262
  801.8 662.7 %all-reduce.17.cloned.1.call-start = ((), (), s32[]{:S(2)}) async-start(), calls=%async_computation.25 | async-start | bytes 9437184 | tf_op jit(solution)/shard_map/psum | solution.py:253
  850.9 516.9 %copy-start.121 = (f32[290]{0:T(512)S(1)}, f32[290]{0:T(512)}, u32[]{:S(2)}) copy-start(f32[290]{0:T(512)} %copy-done.120) | copy-start | bytes 3484
  850.9 517.0 %copy-start.119 = (f32[290]{0:T(512)S(1)}, f32[290]{0:T(512)}, u32[]{:S(2)}) copy-start(f32[290]{0:T(512)} %copy-done.118) | copy-start | bytes 3484
  (156 other events, 3037.4 us)
Sparse Core Ops, SparseCore 0:
  10.3 47.1 all-gather.4
  59.6 133.6 all-gather.6
  195.6 123.0 all-gather.8
  560.8 59.3 reduce-scatter.15
  623.4 62.5 reduce-scatter.9
  723.9 71.7 reduce-scatter.7
  799.9 282.2 reduce-scatter.13
  1086.0 281.7 reduce-scatter.11
  1370.6 93.7 all-reduce.16
where the time goes:
time: 1490 us; the launch traced here: 1480 us
  waiting for transfers between devices  627 us (42%)
  matrix products  247 us (17%)
  other arithmetic  241 us (16%)
  local copies, waits for them, and re-layouts  195 us (13%)
  blocking collectives  102 us (7%)
  starting transfers between devices  48.6 us (3%)
  between operations  18.8 us (1%)
    reduce_scatter x1, waiting for transfers between devices, shards(): lax.psum_scatter(grads[7], 'wide', scatter_dimension=1, tiled=True)  286 us
    reduce_scatter x1, waiting for transfers between devices, shards(): lax.psum_scatter(grads[8], 'wide', scatter_dimension=1, tiled=True)  208 us
    scatter-add x3, other arithmetic, shards(): gate_grad = jnp.zeros((row_count, E), jnp.float32).at[slot_rows, expert_r...  91.6 us
    psum x1, waiting for transfers between devices, shards(): lax.psum((lax.psum_scatter(grads[0], 'wide', scatter_dimension=0, tiled=T...  81.3 us
    unnamed x365, local copies, waits for them, and re-layouts  59.2 us
    unnamed x2, blocking collectives  43.9 us
    dot_general x3, matrix products, shards(): jnp.einsum('ecf,ecd->efd', activated, return_low, preferred_element_type=...  39.1 us
    dot_general x3, matrix products, shards(): jnp.einsum('ecd,ecf->edf', expert_in, pre_grad, preferred_element_type=jn...  36.8 us
  transfers between devices with their start and end apart: 21, of which 8 were waited for; matrix products, arithmetic and copies ran while one was open for 29% of the time, Pallas kernels for 0%

commit v1 on v0

v1 whole, which is shorter than its diff:
```python
import functools
import math

import jax
import jax.numpy as jnp
from jax import lax
from jax.experimental import pallas as pl
from jax.experimental.pallas import tpu as pltpu
from jax.sharding import PartitionSpec as P

H = 8
E = 4
EPSILON = 1e-06
BIG = -1e30
MIB = 1024 * 1024
F32 = jnp.float32
BF16 = jnp.bfloat16


def dot(a, b, dims=((1,), (0,))):
    return lax.dot_general(a, b, (dims, ((), ())), preferred_element_type=F32)


def dot_nt(a, b):
    return dot(a, b, ((1,), (1,)))


def dot_tn(a, b):
    return dot(a, b, ((0,), (0,)))


def norm_parts(values):
    center = values - jnp.mean(values, axis=-1, keepdims=True)
    spread = jnp.mean(center * center, axis=-1, keepdims=True)
    rstd = lax.rsqrt(spread + EPSILON)
    return center * rstd, rstd


def norm_back(grad, xhat, rstd):
    return rstd * (
        grad
        - jnp.mean(grad, axis=-1, keepdims=True)
        - xhat * jnp.mean(grad * xhat, axis=-1, keepdims=True)
    )


def params(limit, **more):
    return pltpu.CompilerParams(vmem_limit_bytes=limit * MIB, **more)


def whole(shape):
    return pl.BlockSpec(shape, lambda *_: (0,) * len(shape))


def per_image(*shape):
    return pl.BlockSpec((1, *shape), lambda i: (i,) + (0,) * len(shape))


def attend_kernel(
    head_dim, own_ref, oth_ref, bias_ref, vec_ref, wq_ref,
    att_m_ref, att_o_ref, qkv_ref, hidden_ref, lse_ref,
):
    rows = own_ref.shape[1]
    gain, offset = vec_ref[0:1, :], vec_ref[1:2, :]
    for half, ref in enumerate((own_ref, oth_ref)):
        xhat, _ = norm_parts(ref[0].astype(F32))
        hidden_ref[0, half * rows : (half + 1) * rows, :] = (xhat * gain + offset).astype(BF16)
    width = wq_ref.shape[1] // 3
    packed = dot(hidden_ref[0], wq_ref[...]).astype(BF16)
    scaling = 1.0 / math.sqrt(head_dim)
    qkv_ref[0, :, :width] = (packed[:, :width].astype(F32) * scaling).astype(BF16)
    qkv_ref[0, :, width:] = packed[:, width:]
    bias = bias_ref[0]
    lane = lax.broadcasted_iota(jnp.int32, (1, 128), 1)
    sub = lax.broadcasted_iota(jnp.int32, (128, 1), 0)
    for pair in range(width // 128):
        cols = slice(pair * 128, pair * 128 + 128)
        q2 = qkv_ref[0, :, cols]
        k2 = qkv_ref[0, :, width + pair * 128 : width + pair * 128 + 128]
        v2 = qkv_ref[0, :, 2 * width + pair * 128 : 2 * width + pair * 128 + 128]
        v_t = v2.T
        both = []
        for part in range(2):
            mine = (lane >= head_dim * part) & (lane < head_dim * (part + 1))
            qm = jnp.where(mine, q2, jnp.zeros_like(q2))
            scores = dot_nt(k2, qm) + bias
            peak = jnp.max(scores, axis=0, keepdims=True)
            expo = jnp.exp(scores - peak)
            total = jnp.sum(expo, axis=0, keepdims=True)
            lse_ref[0, 2 * pair + part : 2 * pair + part + 1, :] = peak + jnp.log(total)
            both.append(dot(v_t, expo.astype(BF16)) * (1.0 / total))
        out = jnp.where(sub < head_dim, both[0], both[1]).astype(BF16).T
        att_m_ref[0, :, cols] = out[:rows]
        att_o_ref[0, :, cols] = out[rows:]


def attend(x_own, x_oth, bias, vecs, wq, head_dim):
    images, rows, width = x_own.shape
    group = wq.shape[1] // 3
    return pl.pallas_call(
        functools.partial(attend_kernel, head_dim),
        grid=(images,),
        in_specs=[
            per_image(rows, width),
            per_image(rows, width),
            per_image(2 * rows, 1),
            whole(vecs.shape),
            whole(wq.shape),
        ],
        out_specs=[
            per_image(rows, group),
            per_image(rows, group),
            per_image(2 * rows, 3 * group),
            per_image(2 * rows, width),
            per_image(8, 2 * rows),
        ],
        out_shape=[
            jax.ShapeDtypeStruct((images, rows, group), BF16),
            jax.ShapeDtypeStruct((images, rows, group), BF16),
            jax.ShapeDtypeStruct((images, 2 * rows, 3 * group), BF16),
            jax.ShapeDtypeStruct((images, 2 * rows, width), BF16),
            jax.ShapeDtypeStruct((images, 8, 2 * rows), F32),
        ],
        compiler_params=params(40),
        name="attend",
    )(x_own, x_oth, bias, vecs, wq)


def project_kernel(att_m_ref, att_r_ref, x_ref, pm_ref, pr_ref, vec_ref, middle_ref, hidden_ref):
    middle = (
        x_ref[0].astype(F32) + dot(att_m_ref[0], pm_ref[...]) + dot(att_r_ref[0], pr_ref[...])
    )
    middle_ref[0] = middle
    xhat, _ = norm_parts(middle)
    hidden_ref[0] = (xhat * vec_ref[2:3, :] + vec_ref[3:4, :]).astype(BF16)


def project(att_m, att_r, x_own, proj_m, proj_r, vecs):
    images, rows, width = x_own.shape
    group = att_m.shape[2]
    return pl.pallas_call(
        project_kernel,
        grid=(images,),
        in_specs=[
            per_image(rows, group),
            per_image(rows, group),
            per_image(rows, width),
            whole(proj_m.shape),
            whole(proj_r.shape),
            whole(vecs.shape),
        ],
        out_specs=[per_image(rows, width), per_image(rows, width)],
        out_shape=[
            jax.ShapeDtypeStruct(x_own.shape, F32),
            jax.ShapeDtypeStruct(x_own.shape, BF16),
        ],
        compiler_params=params(24),
        name="project",
    )(att_m, att_r, x_own, proj_m, proj_r, vecs)


BLOCKS = (
    ((0, 0), (0, 1)),
    ((2, 0), (2, 1)),
    ((1, 0), (1, 1)),
    ((3, 0), (3, 1)),
    ((0, 2), (1, 2)),
    ((2, 2), (3, 2)),
)


def expert_kernel(
    splits, pos_ref, h0, h1, h2, h3, c0, c1, c2, c3, up_ref, down_ref, wr_ref, sel_ref,
    ret_m, ret_o, dh_m, dh_o, xs_ref, g_ref, lg_ref, act_ref, gp_ref,
    cs_ref, ret_ref, dx_ref,
):
    step = pl.program_id(0)
    rows = h0.shape[1]
    hs, cs = (h0, h1, h2, h3), (c0, c1, c2, c3)
    slot = lax.broadcasted_iota(jnp.int32, (rows, rows), 0)
    picks = [
        (slot == pos_ref[0, k : k + 1, :]).astype(F32).astype(BF16) for k in range(2)
    ]
    for number, block in enumerate(BLOCKS):

        @pl.when(step == number)
        def _(block=block):
            (pa, ia), (pb, ib) = block
            xs_ref[...] = (dot(picks[0], hs[pa][ia]) + dot(picks[1], hs[pb][ib])).astype(BF16)
            cs_ref[...] = (dot(picks[0], cs[pa][ia]) + dot(picks[1], cs[pb][ib])).astype(BF16)

    xs = xs_ref[...]
    logits = dot(xs, wr_ref[...])
    lane = lax.broadcasted_iota(jnp.int32, (1, 128), 1)
    logits = jnp.where(lane < E, logits, BIG)
    grown = jnp.exp(logits - jnp.max(logits, axis=-1, keepdims=True))
    router = grown / jnp.sum(grown, axis=-1, keepdims=True)
    sel = sel_ref[...]
    weight = jnp.sum(router * sel, axis=-1, keepdims=True)
    g_ref[...] = (cs_ref[...].astype(F32) * weight).astype(BF16)
    ff = up_ref.shape[1]
    chunk = ff // splits
    for part in range(splits):
        cols = slice(part * chunk, (part + 1) * chunk)
        pre = dot(xs, up_ref[:, cols])
        back = dot_nt(g_ref[...], down_ref[cols, :])
        cdf = 0.5 + 0.5 * lax.erf(pre * math.sqrt(0.5))
        pdf = jnp.exp(-0.5 * pre * pre) * (1.0 / math.sqrt(2.0 * math.pi))
        act = (pre * cdf).astype(BF16)
        gp = (back * (cdf + pre * pdf)).astype(BF16)
        act_ref[:, cols] = act
        gp_ref[:, cols] = gp
        ret = dot(act, down_ref[cols, :])
        dx = dot_nt(gp, up_ref[:, cols])
        if part == 0:
            ret_ref[...] = ret
            dx_ref[...] = dx
        else:
            ret_ref[...] += ret
            dx_ref[...] += dx
    gate = jnp.sum(cs_ref[...].astype(F32) * ret_ref[...], axis=-1, keepdims=True)
    lg = (gate * weight * (sel - router)).astype(BF16)
    lg_ref[...] = lg
    dxb = (dx_ref[...] + dot_nt(lg, wr_ref[...])).astype(BF16)
    retb = (ret_ref[...] * weight).astype(BF16)
    rets, dhs = (ret_m, ret_o), (dh_m, dh_o)
    for number, block in enumerate(BLOCKS):

        @pl.when(step == number)
        def _(block=block):
            for pick, (piece, image) in zip(picks, block):
                rets[piece // 2][piece % 2, image] = dot_tn(pick, retb).astype(BF16)
                dhs[piece // 2][piece % 2, image] = dot_tn(pick, dxb).astype(BF16)


def run_expert(pos, hidden, cots, up, down, wr, sel):
    images, rows, width = hidden[0].shape
    ff = up.shape[1]
    count = len(BLOCKS)
    piece = whole((images, rows, width))
    pairs = whole((2, images, rows, width))
    pair_shape = jax.ShapeDtypeStruct((2, images, rows, width), BF16)

    def slots(cols, dtype=BF16):
        return (
            pl.BlockSpec((rows, cols), lambda i: (i, 0)),
            jax.ShapeDtypeStruct((count * rows, cols), dtype),
        )

    per_slot = [slots(width), slots(width), slots(128), slots(ff), slots(ff)]
    return pl.pallas_call(
        functools.partial(expert_kernel, 4),
        grid=(count,),
        in_specs=[
            pl.BlockSpec((1, 2, rows), lambda i: (i, 0, 0)),
            *[piece] * 8,
            whole(up.shape),
            whole(down.shape),
            whole(wr.shape),
            whole(sel.shape),
        ],
        out_specs=[pairs] * 4 + [spec for spec, _ in per_slot],
        out_shape=[pair_shape] * 4 + [shape for _, shape in per_slot],
        scratch_shapes=[
            pltpu.VMEM((rows, width), BF16),
            pltpu.VMEM((rows, width), F32),
            pltpu.VMEM((rows, width), F32),
        ],
        compiler_params=params(56),
        name="expert",
    )(pos, *hidden, *cots, up, down, wr, sel)


def middle_back_kernel(a_ref, ar_ref, xr_ref, mid_ref, cot_ref, vec_ref, gm_ref, low_ref, sums_ref):
    @pl.when(pl.program_id(0) == 0)
    def _():
        sums_ref[...] = jnp.zeros_like(sums_ref)

    grad = a_ref[0].astype(F32) + ar_ref[0].astype(F32) + xr_ref[0].astype(F32)
    xhat, rstd = norm_parts(mid_ref[0])
    sums_ref[0:1, :] += jnp.sum(grad * xhat, axis=0, keepdims=True)
    sums_ref[1:2, :] += jnp.sum(grad, axis=0, keepdims=True)
    out = cot_ref[0].astype(F32) + norm_back(grad * vec_ref[2:3, :], xhat, rstd)
    gm_ref[0] = out
    low_ref[0] = out.astype(BF16)


def middle_back(a, ar, xr, middle, cot, vecs):
    images, rows, width = middle.shape
    one = per_image(rows, width)
    return pl.pallas_call(
        middle_back_kernel,
        grid=(images,),
        in_specs=[one] * 5 + [whole(vecs.shape)],
        out_specs=[one, one, whole((8, width))],
        out_shape=[
            jax.ShapeDtypeStruct(middle.shape, F32),
            jax.ShapeDtypeStruct(middle.shape, BF16),
            jax.ShapeDtypeStruct((8, width), F32),
        ],
        compiler_params=params(24),
        name="middle_back",
    )(a, ar, xr, middle, cot, vecs)


def attend_back_kernel(
    head_dim, lm_ref, lo_ref, pm_ref, qkv_ref, lse_ref, am_ref, ao_ref, bias_ref, h1_ref, wq_ref,
    dm_ref, do_ref, gq_ref, gp_ref, grad_ref, att_ref, low_ref,
):
    rows = lm_ref.shape[1]
    low_ref[:rows, :] = lm_ref[0]
    low_ref[rows:, :] = lo_ref[0]
    att_ref[:rows, :] = am_ref[0]
    att_ref[rows:, :] = ao_ref[0]
    out_grad = dot_nt(low_ref[...], pm_ref[...]).astype(BF16)
    width = pm_ref.shape[0]
    bias = bias_ref[0]
    lane = lax.broadcasted_iota(jnp.int32, (1, 128), 1)
    sub = lax.broadcasted_iota(jnp.int32, (128, 1), 0)
    scaling = 1.0 / math.sqrt(head_dim)
    for pair in range(width // 128):
        cols = slice(pair * 128, pair * 128 + 128)
        k_cols = slice(width + pair * 128, width + pair * 128 + 128)
        v_cols = slice(2 * width + pair * 128, 2 * width + pair * 128 + 128)
        q2, k2, v2 = qkv_ref[0, :, cols], qkv_ref[0, :, k_cols], qkv_ref[0, :, v_cols]
        o2 = out_grad[:, cols]
        k_t = k2.T
        dv = dk = None
        both = []
        for part in range(2):
            mine = (lane >= head_dim * part) & (lane < head_dim * (part + 1))
            qm = jnp.where(mine, q2, jnp.zeros_like(q2))
            om = jnp.where(mine, o2, jnp.zeros_like(o2))
            head = 2 * pair + part
            probs = jnp.exp(dot_nt(k2, qm) + bias - lse_ref[0, head : head + 1, :])
            prob_grad = dot_nt(v2, om)
            delta = jnp.sum(probs * prob_grad, axis=0, keepdims=True)
            score_grad = (probs * (prob_grad - delta)).astype(BF16)
            dv_part = dot(probs.astype(BF16), om)
            dk_part = dot(score_grad, qm)
            dv = dv_part if dv is None else dv + dv_part
            dk = dk_part if dk is None else dk + dk_part
            both.append(dot(k_t, score_grad))
        dq = (jnp.where(sub < head_dim, both[0], both[1]) * scaling).astype(BF16).T
        grad_ref[:, cols] = dq
        grad_ref[:, k_cols] = dk.astype(BF16)
        grad_ref[:, v_cols] = dv.astype(BF16)
    hidden_grad = dot_nt(grad_ref[...], wq_ref[...]).astype(BF16)
    dm_ref[0] = hidden_grad[:rows]
    do_ref[0] = hidden_grad[rows:]

    @pl.when(pl.program_id(0) == 0)
    def _():
        gq_ref[...] = jnp.zeros_like(gq_ref)
        gp_ref[...] = jnp.zeros_like(gp_ref)

    gq_ref[...] += dot_tn(h1_ref[0], grad_ref[...])
    gp_ref[...] += dot_tn(att_ref[...], low_ref[...])


def attend_back(low_m, low_o, proj_m, qkv, lse, att_m, att_o, bias, hidden_one, wq, head_dim):
    images, rows, width = low_m.shape
    group = att_m.shape[2]
    return pl.pallas_call(
        functools.partial(attend_back_kernel, head_dim),
        grid=(images,),
        in_specs=[
            per_image(rows, width),
            per_image(rows, width),
            whole(proj_m.shape),
            per_image(2 * rows, 3 * group),
            per_image(8, 2 * rows),
            per_image(rows, group),
            per_image(rows, group),
            per_image(2 * rows, 1),
            per_image(2 * rows, width),
            whole(wq.shape),
        ],
        out_specs=[
            per_image(rows, width),
            per_image(rows, width),
            whole((width, 3 * group)),
            whole((group, width)),
        ],
        out_shape=[
            jax.ShapeDtypeStruct((images, rows, width), BF16),
            jax.ShapeDtypeStruct((images, rows, width), BF16),
            jax.ShapeDtypeStruct((width, 3 * group), F32),
            jax.ShapeDtypeStruct((group, width), F32),
        ],
        scratch_shapes=[
            pltpu.VMEM((2 * rows, 3 * group), BF16),
            pltpu.VMEM((2 * rows, group), BF16),
            pltpu.VMEM((2 * rows, width), BF16),
        ],
        compiler_params=params(48),
        name="attend_back",
    )(low_m, low_o, proj_m, qkv, lse, att_m, att_o, bias, hidden_one, wq)


def input_back_kernel(a_ref, ar_ref, x_ref, gm_ref, vec_ref, out_ref, sums_ref):
    @pl.when(pl.program_id(0) == 0)
    def _():
        sums_ref[...] = jnp.zeros_like(sums_ref)

    grad = a_ref[0].astype(F32) + ar_ref[0].astype(F32)
    xhat, rstd = norm_parts(x_ref[0].astype(F32))
    sums_ref[0:1, :] += jnp.sum(grad * xhat, axis=0, keepdims=True)
    sums_ref[1:2, :] += jnp.sum(grad, axis=0, keepdims=True)
    out_ref[0] = gm_ref[0] + norm_back(grad * vec_ref[0:1, :], xhat, rstd)


def input_back(a, ar, x_own, grad_middle, vecs):
    images, rows, width = x_own.shape
    one = per_image(rows, width)
    return pl.pallas_call(
        input_back_kernel,
        grid=(images,),
        in_specs=[one] * 4 + [whole(vecs.shape)],
        out_specs=[one, whole((8, width))],
        out_shape=[
            jax.ShapeDtypeStruct(x_own.shape, F32),
            jax.ShapeDtypeStruct((8, width), F32),
        ],
        compiler_params=params(24),
        name="input_back",
    )(a, ar, x_own, grad_middle, vecs)


def shards(
    tokens,
    key_mask,
    expert_ids,
    ln1_gain,
    ln1_bias,
    qkv_weight,
    proj_weight,
    ln2_gain,
    ln2_bias,
    router_weight,
    up_weight,
    down_weight,
    cotangent,
):
    n_seq = lax.axis_size("seq")
    images, quarter, width = tokens.shape
    head_dim = width // H
    group = width // 2
    rows = -(-2 * quarter // 16) * 16
    place = lax.axis_index("seq")
    chip, core = place // 2, place % 2
    flip_x = [(i, i ^ 2) for i in range(n_seq)]
    flip_core = [(i, i ^ 1) for i in range(n_seq)]

    def over_x(a):
        return lax.ppermute(a, "seq", flip_x)

    def over_core(a):
        return lax.ppermute(a, "seq", flip_core)

    def images_of(a, of_chip):
        pair = lax.dynamic_slice_in_dim(a, of_chip * (images - 2), 2, 0)
        single = lax.dynamic_slice_in_dim(a, images // 2 - 1 + of_chip, 1, 0)
        return jnp.concatenate([pair, single], axis=0)

    def joined(first, second):
        both = jnp.concatenate([first, second], axis=1)
        return jnp.pad(both, ((0, 0), (0, rows - 2 * quarter)) + ((0, 0),) * (both.ndim - 2))

    down_rows = down_weight.shape[1]
    wq_shard = lax.dynamic_slice_in_dim(
        qkv_weight.reshape(-1, 3, 2, group), core, 1, axis=2
    ).reshape(-1, 3 * group)
    vec_shard = jnp.stack([ln1_gain, ln1_bias, ln2_gain, ln2_bias], axis=1)
    pack = jnp.concatenate(
        [
            wq_shard,
            proj_weight,
            vec_shard,
            router_weight,
            jnp.zeros((vec_shard.shape[0], 128 - 4 - E), BF16),
        ],
        axis=1,
    )
    pack = lax.all_gather(pack, "wide", axis=0, tiled=True)
    wq = pack[:, : 3 * group]
    proj = pack[:, 3 * group : 3 * group + width]
    small = pack[:, 3 * group + width :]
    vecs = jnp.pad(small[:, :4].astype(F32).T, ((0, 4), (0, 0)))
    wr = jnp.pad(small[:, 4 : 4 + E], ((0, 0), (0, 128 - E)))
    proj_m = lax.dynamic_slice_in_dim(proj, core * group, group, 0)
    proj_r = lax.dynamic_slice_in_dim(proj, (1 - core) * group, group, 0)
    up = lax.all_gather(
        lax.dynamic_index_in_dim(up_weight, place, 0, False), "wide", axis=0, tiled=True
    )
    down = lax.all_gather(
        lax.dynamic_index_in_dim(down_weight, place, 0, False), "wide", axis=0, tiled=True
    )

    x_own = joined(images_of(tokens, chip), over_x(images_of(tokens, 1 - chip)))
    x_oth = over_core(x_own)
    cot_got = over_x(cotangent)
    cot_a = joined(images_of(cotangent, chip), images_of(cot_got, chip))
    cot_b = joined(images_of(cot_got, 1 - chip), images_of(cotangent, 1 - chip))
    cots = (cot_a, cot_b, over_core(cot_a), over_core(cot_b))

    def cells(quarters, of_chip, of_core):
        first = lax.dynamic_index_in_dim(quarters, 2 * of_chip + of_core, 1, False)
        second = lax.dynamic_index_in_dim(quarters, 2 * (1 - of_chip) + of_core, 1, False)
        return joined(images_of(first, of_chip), images_of(second, of_chip))

    mask = key_mask.reshape(images, n_seq, quarter)
    valid = jnp.concatenate([cells(mask, chip, core), cells(mask, chip, 1 - core)], axis=1)
    bias = jnp.where(valid > 0, 0.0, BIG).astype(F32)[..., None]
    ids = lax.all_gather(expert_ids, "seq", axis=1)
    chosen = jnp.any(ids == place, axis=-1).astype(jnp.int32)
    flags = [
        cells(chosen, a, b)
        for a, b in ((chip, core), (1 - chip, core), (chip, 1 - core), (1 - chip, 1 - core))
    ]
    flags = jnp.stack([jnp.concatenate([flags[p][i] for p, i in block]) for block in BLOCKS])
    before = (
        lax.broadcasted_iota(jnp.int32, (2 * rows, 2 * rows), 0)
        < lax.broadcasted_iota(jnp.int32, (2 * rows, 2 * rows), 1)
    ).astype(BF16)
    rank = dot(flags.astype(BF16), before).astype(jnp.int32)
    pos = jnp.where(flags > 0, rank, -1).reshape(len(BLOCKS), 2, rows)
    sel = (jnp.arange(128, dtype=jnp.int32) == place).astype(F32)[None, :]

    att_m, att_o, qkv, hidden_one, lse = attend(x_own, x_oth, bias, vecs, wq, head_dim)
    att_r = over_core(att_o)
    middle, hidden_two = project(att_m, att_r, x_own, proj_m, proj_r, vecs)

    hidden_b = over_x(hidden_two)
    hidden = (hidden_two, hidden_b, over_core(hidden_two), over_core(hidden_b))
    ret_m, ret_o, dh_m, dh_o, xs, g_slots, lg, act, gp = run_expert(
        pos, hidden, cots, up, down, wr, sel
    )
    dh_r = over_core(dh_o)
    dh_x = over_x(dh_m[1] + dh_r[1])
    ret_r = over_core(ret_o)
    ret_x = over_x(ret_m[1] + ret_r[1])
    grad_up = dot_tn(xs, gp).astype(BF16)
    grad_down = dot_tn(act, g_slots).astype(BF16)
    grad_router = dot_tn(xs, lg)
    layer = (
        middle + ret_m[0].astype(F32) + ret_r[0].astype(F32) + ret_x.astype(F32)
    ).astype(BF16)

    grad_middle, low_m, sums_two = middle_back(dh_m[0], dh_r[0], dh_x, middle, cot_a, vecs)
    low_o = over_core(low_m)
    dh1_m, dh1_o, grad_qkv, grad_proj = attend_back(
        low_m, low_o, proj_m, qkv, lse, att_m, att_o, bias, hidden_one, wq, head_dim
    )
    dh1_r = over_core(dh1_o)
    grad_input, sums_one = input_back(dh1_m, dh1_r, x_own, grad_middle, vecs)

    def settle(a):
        mine, other = a[:, :quarter], a[:, quarter : 2 * quarter]
        got = over_x(other.astype(BF16)).astype(a.dtype)
        pair, rest = slice(0, 2), slice(2, 3)
        return jnp.where(
            chip == 0,
            jnp.concatenate([mine[pair], mine[rest], got[rest], got[pair]], axis=0),
            jnp.concatenate([got[pair], got[rest], mine[rest], mine[pair]], axis=0),
        )

    layer_out = settle(layer)
    input_grad = settle(grad_input)

    def over_wide(a, dim=0):
        return lax.psum_scatter(a, "wide", scatter_dimension=dim, tiled=True)

    grad_up = over_wide(grad_up)
    grad_down = over_wide(grad_down)

    def all_experts(a):
        pairs = jnp.stack([a, over_core(a)])
        four = jnp.concatenate([pairs, over_x(pairs)], axis=0)
        return jnp.stack(
            [lax.dynamic_index_in_dim(four, place ^ e, 0, False) for e in range(E)]
        ).astype(F32)

    grad_up = all_experts(grad_up)
    grad_down = all_experts(grad_down)
    proj_wide = lax.dynamic_update_slice_in_dim(
        jnp.zeros((width, width), F32), grad_proj, core * group, 0
    )
    rest = jnp.concatenate(
        [
            grad_qkv,
            proj_wide,
            sums_one[:2].T,
            sums_two[:2].T,
            grad_router[:, :E],
            jnp.zeros((width, 128 - 4 - E), F32),
        ],
        axis=1,
    ).astype(BF16)
    rest = over_wide(rest).astype(F32)
    rest = rest + over_x(rest.astype(BF16)).astype(F32)
    other = over_core(rest.astype(BF16)).astype(F32)
    group_three = 3 * group
    own_q = rest[:, :group_three].reshape(-1, 3, group)
    oth_q = other[:, :group_three].reshape(-1, 3, group)
    grad_qkv = jnp.where(
        core == 0,
        jnp.stack([own_q, oth_q], axis=2),
        jnp.stack([oth_q, own_q], axis=2),
    ).reshape(-1, 3 * width)
    tail = rest[:, group_three:] + other[:, group_three:]
    grad_proj = tail[:, :width]
    small_grad = tail[:, width:]
    return (
        layer_out,
        input_grad,
        small_grad[:, 0],
        small_grad[:, 1],
        grad_qkv,
        grad_proj,
        small_grad[:, 2],
        small_grad[:, 3],
        small_grad[:, 4 : 4 + E],
        grad_up,
        grad_down,
    )


def solution(mesh):
    placed = (
        P("wide", "seq", None),
        P("wide", None),
        P("wide", "seq", None),
        P("wide"),
        P("wide"),
        P("wide", None),
        P("wide", None),
        P("wide"),
        P("wide"),
        P("wide", None),
        P(None, "wide", None),
        P(None, "wide", None),
        P("wide", "seq", None),
    )
    return jax.shard_map(
        shards,
        mesh=mesh,
        in_specs=placed,
        out_specs=(
            P("wide", "seq", None),
            P("wide", "seq", None),
            P("wide"),
            P("wide"),
            P("wide", None),
            P("wide", None),
            P("wide"),
            P("wide"),
            P("wide", None),
            P(None, "wide", None),
            P(None, "wide", None),
        ),
        check_vma=False,
    )
```

time: 1490 us -> 444 us (0.30)
  waiting for transfers between devices: 627 us -> 226 us
  matrix products: 247 us -> 22.1 us
  other arithmetic: 241 us -> 22.1 us
  local copies, waits for them, and re-layouts: 195 us -> 42.8 us
  blocking collectives: 102 us -> 7.79 us
  Pallas kernels: 0 us -> 84.4 us
  starting transfers between devices: 48.6 us -> 16.4 us
    reduce_scatter x4 -> x3, waiting for transfers between devices: 494 us -> 96.8 us  [over_wide(): return lax.psum_scatter(a, 'wide', scatter_dimension=dim, tiled=True)]
    dot_general x63 -> x4, matrix products: 247 us -> 22.1 us  [dot(): return lax.dot_general(a, b, (dims, ((), ())), preferred_element_type=F32)]
    scatter-add x9 -> x0, other arithmetic: 137 us -> none  [the longest x3 91.6 us: shards(): gate_grad = jnp.zeros((row_count, E), jnp.float32).at[slot_rows, expert_r...]
    ppermute x0 -> x23, waiting for transfers between devices: none -> 84.5 us  [the longest x10 81.5 us: over_x(): return lax.ppermute(a, 'seq', flip_x)]
    pallas_call x0 -> x6, Pallas kernels: none -> 84.4 us  [the longest x1 41.8 us: run_expert(): pl.pallas_call(functools.partial(expert_kernel, 4), grid=(count,), in_spe...]
    psum x1 -> x0, waiting for transfers between devices: 81.3 us -> none  [shards(): lax.psum((lax.psum_scatter(grads[0], 'wide', scatter_dimension=0, tiled=T...]
    gather x18 -> x0, local copies, waits for them, and re-layouts: 49.1 us -> none  [the longest x6 25.7 us: shards(): slot_weight = combined[slot_rows, expert_range[:, None]]]
    unnamed x365 -> x111, local copies, waits for them, and re-layouts: 59.2 us -> 11.3 us
  transfers between devices with their start and end apart: 21 -> 29, of which waited for: 8 -> 12; matrix products, arithmetic and copies ran while one was open for 29% -> 13% of each run, Pallas kernels for 0% -> 10%
where the time goes in v1:
time: 444 us; the launch traced here: 437 us
  waiting for transfers between devices  226 us (51%)
  Pallas kernels  84.4 us (19%)
  local copies, waits for them, and re-layouts  42.8 us (10%)
  other arithmetic  22.1 us (5%)
  matrix products  22.1 us (5%)
  starting transfers between devices  16.4 us (4%)
  between operations  15.7 us (4%)
  blocking collectives  7.79 us (2%)
    reduce_scatter x3, waiting for transfers between devices, over_wide(): return lax.psum_scatter(a, 'wide', scatter_dimension=dim, tiled=True)  96.8 us
    ppermute x10, waiting for transfers between devices, over_x(): return lax.ppermute(a, 'seq', flip_x)  81.5 us
    pallas_call x1, Pallas kernels, run_expert(): pl.pallas_call(functools.partial(expert_kernel, 4), grid=(count,), in_spe...  41.8 us
    all_gather x1, waiting for transfers between devices, shards(): lax.all_gather(lax.dynamic_index_in_dim(down_weight, place, 0, False), 'w...  37.8 us
    pallas_call x1, Pallas kernels, attend_back(): pl.pallas_call(functools.partial(attend_back_kernel, head_dim), grid=(ima...  23.3 us
    dot_general x4, matrix products, dot(): return lax.dot_general(a, b, (dims, ((), ())), preferred_element_type=F32)  22.1 us
    ppermute x10, starting transfers between devices, over_x(): return lax.ppermute(a, 'seq', flip_x)  14.9 us
    pallas_call x1, Pallas kernels, attend(): pl.pallas_call(functools.partial(attend_kernel, head_dim), grid=(images,)...  12.3 us
  transfers between devices with their start and end apart: 29, of which 12 were waited for; matrix products, arithmetic and copies ran while one was open for 13% of the time, Pallas kernels for 10%

profile of v1, /device:TPU:0, one launch (start us, length us, event | category | flops | bytes accessed | tf_op | source)
XLA Modules:
  0.0 437.2 jit_solution(13111397599358411267)
XLA Ops:
  15.4 3.0 collective-permute-start.6
  18.4 20.7 %collective-permute-done.6 = bf16[6,145,512]{2,1,0:T(8,128)(2,1)S(1)} collective-permute-done((bf16[6,145,512]{2,1,0:T(8,128)(2,1)S(1)}, bf16[6,145,512]{2,1,0:T(8,128)(2,1)S(1)}, u32[]{:S(2)}, u32[]{:S(2)}) %collective-permute-start.6) | collective-permute-done | bytes 890912 | tf_op jit(solution)/shard_map/ppermute | solution.py:456
  44.8 8.2 %collective-permute-done = bf16[3,145,512]{2,1,0:T(8,128)(2,1)S(1)} collective-permute-done((bf16[3,145,512]{2,1,0:T(8,128)(2,1)S(1)}, bf16[3,145,512]{2,1,0:T(8,128)(2,1)S(1)}, u32[]{:S(2)}, u32[]{:S(2)}) %collective-permute-start) | collective-permute-done | bytes 445472 | tf_op jit(solution)/shard_map/ppermute | solution.py:456
  53.9 6.6 %all-gather.7.cloned.1.call-done = bf16[512,1408]{1,0:T(8,128)(2,1)} async-done(((bf16[64,1408]{1,0:T(8,128)(2,1)}), bf16[512,1408]{1,0:T(8,128)(2,1)}) %all-gather.7.cloned.1.call-update) | async-done | bytes 1441808 | tf_op jit(solution)/shard_map/all_gather | solution.py:485
  63.6 12.3 %attend.1 = (bf16[3,304,256]{2,1,0:T(8,128)(2,1)S(1)}, bf16[3,304,256]{2,1,0:T(8,128)(2,1)}, bf16[3,608,768]{2,1,0:T(8,128)(2,1)S(1)}, bf16[3,608,512]{2,1,0:T(8,128)(2,1)S(1)}, f32[3,8,608]{2,1,0:T(8,128)S(1)}) custom-call(bf16[3,304,512]{2,1,0:T(8,128)(2,1)S(1)} %fusion.17.own_ref.x_ref, bf16[3,304,512]{2,1,0:T(8,128)(2,1)S(1)} %collective-permute-done.1.oth_ref, ...), custom_call_target="tpu_custom_call" | custom-call | tf_op jit(solution)/shard_map/attend/pallas_call | solution.py:100
  78.9 7.8 %all-gather = s32[6,580,2]{0,2,1:T(2,128)S(1)} all-gather(s32[6,145,2]{0,2,1:T(2,128)S(1)} %copy.149), channel_id=2, replica_groups=mesh['wide'=8,'seq'=4] {'seq'}, dimensions={1}, use_global_device_ids=true | all-gather | bytes 34800 | tf_op jit(solution)/shard_map/all_gather | solution.py:515
  94.9 18.8 %collective-permute-done.3.h1 = bf16[3,304,512]{2,1,0:T(8,128)(2,1)} collective-permute-done((bf16[3,304,512]{2,1,0:T(8,128)(2,1)S(1)}, bf16[3,304,512]{2,1,0:T(8,128)(2,1)}, u32[]{:S(2)}, u32[]{:S(2)}) %collective-permute-start.3) | collective-permute-done | bytes 933920 | tf_op jit(solution)/shard_map/ppermute | solution.py:456
  123.1 37.8 %all-gather.11.cloned.1.call-done = bf16[1,2048,512]{2,1,0:T(8,128)(2,1)} async-done(((bf16[1,256,512]{2,1,0:T(8,128)(2,1)}), bf16[1,2048,512]{2,1,0:T(8,128)(2,1)}) %all-gather.11.cloned.1.call-update) | async-done | bytes 2097168 | tf_op jit(solution)/shard_map/all_gather | solution.py:496
  160.9 41.8 %expert.1 = (bf16[2,3,304,512]{3,2,1,0:T(8,128)(2,1)}, bf16[2,3,304,512]{3,2,1,0:T(8,128)(2,1)}, bf16[2,3,304,512]{3,2,1,0:T(8,128)(2,1)}, bf16[2,3,304,512]{3,2...) custom-call(s32[6,2,304]{2,1,0:T(2,128)} %reshape.114.pos_ref, ...), custom_call_target="tpu_custom_call" | custom-call | tf_op jit(solution)/shard_map/expert/pallas_call | solution.py:251
  202.7 9.6 %convolution_convert_fusion.1 = bf16[512,2048]{1,0:T(8,128)(2,1)} fusion(bf16[1824,512]{1,0:T(8,128)(2,1)} %get-tuple-element.56, bf16[1824,2048]{1,0:T(8,128)(2,1)} %get-tuple-element.58), kind=kOutput, calls=%fused_computation.1 | convolution fusion | flops 3826253824 | bytes 11436032 | tf_op jit(solution)/shard_map/dot_general | solution.py:21
  212.5 9.5 %convolution_convert_fusion = bf16[2048,512]{1,0:T(8,128)(2,1)} fusion(bf16[1824,2048]{1,0:T(8,128)(2,1)} %get-tuple-element.59, bf16[1824,512]{1,0:T(8,128)(2,1)} %get-tuple-element.60), kind=kOutput, calls=%fused_computation | convolution fusion | flops 3826253824 | bytes 11436032 | tf_op jit(solution)/shard_map/dot_general | solution.py:21
  223.3 2.4 fusion.24
  227.5 21.4 %collective-permute-done.13.xr_ref = bf16[3,304,512]{2,1,0:T(8,128)(2,1)S(1)} collective-permute-done((bf16[3,304,512]{2,1,0:T(8,128)(2,1)S(1)}, bf16[3,304,512]{2,1,0:T(8,128)(2,1)S(1)}, u32[]{:S(2)}, u32[]{:S(2)}) %collective-permute-start.13) | collective-permute-done | bytes 933920 | tf_op jit(solution)/shard_map/ppermute | solution.py:456
  248.9 2.0 middle_back.1
  252.2 2.5 collective-permute-done.14.lo_ref
  255.6 23.3 %attend_back.1 = (bf16[3,304,512]{2,1,0:T(8,128)(2,1)S(1)}, bf16[3,304,512]{2,1,0:T(8,128)(2,1)}, f32[512,768]{1,0:T(8,128)}, f32[256,512]{1,0:T(8,128)S(1)}) custom-call(bf16[3,304,512]{2,1,0:T(8,128)(2,1)S(1)} %get-tuple-element.44.lm_ref, bf16[3,304,512]{2,1,0:T(8,128)(2,1)} %copy-done.31, bf16[256,512]{1,0:T(8,128)(2,1)S(1)} %get-tuple-element.193.pm_ref, ...), custom_call_target="tpu_custom_call" | custom-call | tf_op jit(solution)/shard_map/attend_back/pallas_call | solution.py:364
  283.8 2.5 convert.31
  287.2 3.1 input_back.1
  291.8 3.9 concatenate.185
  295.8 9.4 %collective-permute-done.10 = bf16[3,304,512]{2,1,0:T(8,128)(2,1)} collective-permute-done((bf16[3,304,512]{2,1,0:T(8,128)(2,1)}, bf16[3,304,512]{2,1,0:T(8,128)(2,1)}, u32[]{:S(2)}, u32[]{:S(2)}) %collective-permute-start.10) | collective-permute-done | bytes 933920 | tf_op jit(solution)/shard_map/ppermute | solution.py:456
  305.3 2.3 fusion.12
  311.3 38.0 %reduce-scatter.8.cloned.1.call-done = bf16[256,512]{1,0:T(8,128)(2,1)} async-done(((bf16[2048,512]{1,0:T(8,128)(2,1)}), bf16[256,512]{1,0:T(8,128)(2,1)}) %reduce-scatter.8.cloned.1.call-update) | async-done | bytes 262160 | tf_op jit(solution)/shard_map/reduce_scatter | solution.py:572
  357.8 58.8 %reduce-scatter.4.cloned.1.call-done = bf16[64,1408]{1,0:T(8,128)(2,1)} async-done(((bf16[512,1408]{1,0:T(8,128)(2,1)}), bf16[64,1408]{1,0:T(8,128)(2,1)}) %reduce-scatter.4.cloned.1.call-update) | async-done | bytes 180240 | tf_op jit(solution)/shard_map/reduce_scatter | solution.py:572
  419.3 3.0 collective-permute-done.17
  (272 shorter events, 72.7 us)
Async XLA Ops:
  7.2 53.3 %all-gather.7.cloned.1.call-start = ((), (), s32[]{:S(2)}) async-start(), calls=%async_computation.3 | async-start | bytes 1622016 | tf_op jit(solution)/shard_map/all_gather | solution.py:485
  14.6 108.5 %all-gather.9.cloned.1.call-start = ((), (), s32[]{:S(2)}) async-start(), calls=%async_computation.7 | async-start | bytes 2359296 | tf_op jit(solution)/shard_map/all_gather | solution.py:493
  15.4 145.5 %all-gather.11.cloned.1.call-start = ((), (), s32[]{:S(2)}) async-start(), calls=%async_computation.8 | async-start | bytes 2359296 | tf_op jit(solution)/shard_map/all_gather | solution.py:496
  15.4 23.7 %collective-permute-start.6 = (bf16[6,145,512]{2,1,0:T(8,128)(2,1)S(1)}, bf16[6,145,512]{2,1,0:T(8,128)(2,1)S(1)}, u32[]{:S(2)}, u32[]{:S(2)}) collective-permute-start(bf16[6,145,512]{2,1,0:T(8,128)(2,1)S(1)} %copy-done.33), channel_id=1, source_target_pairs={{0,2},{1,3},{2,0},{3,1},{4,6},{5,7},{6,4},{7,5},{8,10},{9,11},{10,... | collective-permute-start | bytes 2672648 | tf_op jit(solution)/shard_map/ppermute | solution.py:456
  40.9 12.1 %collective-permute-start = (bf16[3,145,512]{2,1,0:T(8,128)(2,1)S(1)}, bf16[3,145,512]{2,1,0:T(8,128)(2,1)S(1)}, u32[]{:S(2)}, u32[]{:S(2)}) collective-permute-start(bf16[3,145,512]{2,1,0:T(8,128)(2,1)S(1)} %pad_maximum_fusion.4), channel_id=1, source_target_pairs={{0,2},{1,3},{2,0},{3,1},{4,6},{5,7},{6,4},{7,5},{8,10},{9,11},{10,... | collective-permute-start | bytes 1336328 | tf_op jit(solution)/shard_map/ppermute | solution.py:456
  44.4 251.3 %reduce-scatter.6.cloned.1.call-start = ((), (), s32[]{:S(2)}) async-start(), calls=%async_computation.5 | async-start | bytes 2359296 | tf_op jit(solution)/shard_map/reduce_scatter | solution.py:572
  53.1 10.5 %collective-permute-start.1 = (bf16[3,304,512]{2,1,0:T(8,128)(2,1)S(1)}, bf16[3,304,512]{2,1,0:T(8,128)(2,1)S(1)}, u32[]{:S(2)}, u32[]{:S(2)}) collective-permute-start(bf16[3,304,512]{2,1,0:T(8,128)(2,1)S(1)} %fusion.17.own_ref.x_ref), channel_id=1, source_target_pairs={{0,1},{1,0},{2,3},{3,2},{4,5},{5,4},{6,7},{7,6},{8,9},{9,8},{10,11... | collective-permute-start | bytes 2801672 | tf_op jit(solution)/shard_map/ppermute | solution.py:459
  78.7 10.0 %collective-permute-start.2 = (bf16[3,304,256]{2,1,0:T(8,128)(2,1)}, bf16[3,304,256]{2,1,0:T(8,128)(2,1)S(1)}, u32[]{:S(2)}, u32[]{:S(2)}) collective-permute-start(bf16[3,304,256]{2,1,0:T(8,128)(2,1)} %get-tuple-element.37.ao_ref), channel_id=1, source_target_pairs={{0,1},{1,0},{2,3},{3,2},{4,5},{5,4},{6,7},{7,6},{8,9},{9,8},{10,11... | collective-permute-start | bytes 1400840 | tf_op jit(solution)/shard_map/ppermute | solution.py:459
  90.5 23.1 %collective-permute-start.3 = (bf16[3,304,512]{2,1,0:T(8,128)(2,1)S(1)}, bf16[3,304,512]{2,1,0:T(8,128)(2,1)}, u32[]{:S(2)}, u32[]{:S(2)}) collective-permute-start(bf16[3,304,512]{2,1,0:T(8,128)(2,1)S(1)} %get-tuple-element.39.h0), channel_id=1, source_target_pairs={{0,2},{1,3},{2,0},{3,1},{4,6},{5,7},{6,4},{7,5},{8,10},{9,11},{10,... | collective-permute-start | bytes 2801672 | tf_op jit(solution)/shard_map/ppermute | solution.py:456
  92.6 30.5 %collective-permute-start.7 = (bf16[3,304,512]{2,1,0:T(8,128)(2,1)S(1)}, bf16[3,304,512]{2,1,0:T(8,128)(2,1)}, u32[]{:S(2)}, u32[]{:S(2)}) collective-permute-start(bf16[3,304,512]{2,1,0:T(8,128)(2,1)S(1)} %fusion.19.c0.cot_ref), channel_id=1, source_target_pairs={{0,1},{1,0},{2,3},{3,2},{4,5},{5,4},{6,7},{7,6},{8,9},{9,8},{10,11... | collective-permute-start | bytes 2801672 | tf_op jit(solution)/shard_map/ppermute | solution.py:459
  94.4 28.7 %collective-permute-start.8 = (bf16[3,304,512]{2,1,0:T(8,128)(2,1)}, bf16[3,304,512]{2,1,0:T(8,128)(2,1)}, u32[]{:S(2)}, u32[]{:S(2)}) collective-permute-start(bf16[3,304,512]{2,1,0:T(8,128)(2,1)} %fusion.22.c1), channel_id=1, source_target_pairs={{0,1},{1,0},{2,3},{3,2},{4,5},{5,4},{6,7},{7,6},{8,9},{9,8},{10,11... | collective-permute-start | bytes 2801672 | tf_op jit(solution)/shard_map/ppermute | solution.py:459
  94.4 66.4 %collective-permute-start.4 = (bf16[3,304,512]{2,1,0:T(8,128)(2,1)S(1)}, bf16[3,304,512]{2,1,0:T(8,128)(2,1)}, u32[]{:S(2)}, u32[]{:S(2)}) collective-permute-start(bf16[3,304,512]{2,1,0:T(8,128)(2,1)S(1)} %get-tuple-element.39.h0), channel_id=1, source_target_pairs={{0,1},{1,0},{2,3},{3,2},{4,5},{5,4},{6,7},{7,6},{8,9},{9,8},{10,11... | collective-permute-start | bytes 2801672 | tf_op jit(solution)/shard_map/ppermute | solution.py:459
  113.6 47.2 %collective-permute-start.5 = (bf16[3,304,512]{2,1,0:T(8,128)(2,1)}, bf16[3,304,512]{2,1,0:T(8,128)(2,1)}, u32[]{:S(2)}, u32[]{:S(2)}) collective-permute-start(bf16[3,304,512]{2,1,0:T(8,128)(2,1)} %collective-permute-done.3.h1), channel_id=1, source_target_pairs={{0,1},{1,0},{2,3},{3,2},{4,5},{5,4},{6,7},{7,6},{8,9},{9,8},{10,11... | collective-permute-start | bytes 2801672 | tf_op jit(solution)/shard_map/ppermute | solution.py:459
  212.3 137.0 %reduce-scatter.8.cloned.1.call-start = ((), (), s32[]{:S(2)}) async-start(), calls=%async_computation.6 | async-start | bytes 2359296 | tf_op jit(solution)/shard_map/reduce_scatter | solution.py:572
  212.4 9.7 %collective-permute-start.12 = (bf16[2,3,304,512]{3,2,1,0:T(8,128)(2,1)}, bf16[2,3,304,512]{3,2,1,0:T(8,128)(2,1)S(1)}, u32[]{:S(2)}, u32[]{:S(2)}) collective-permute-start(bf16[2,3,304,512]{3,2,1,0:T(8,128)(2,1)} %get-tuple-element.43), channel_id=1, source_target_pairs={{0,1},{1,0},{2,3},{3,2},{4,5},{5,4},{6,7},{7,6},{8,9},{9,8},{10,11... | collective-permute-start | bytes 5603336 | tf_op jit(solution)/shard_map/ppermute | solution.py:459
  222.0 194.6 %reduce-scatter.4.cloned.1.call-start = ((), (), s32[]{:S(2)}) async-start(), calls=%async_computation.4 | async-start | bytes 1622016 | tf_op jit(solution)/shard_map/reduce_scatter | solution.py:572
  225.7 23.2 %collective-permute-start.13 = (bf16[3,304,512]{2,1,0:T(8,128)(2,1)S(1)}, bf16[3,304,512]{2,1,0:T(8,128)(2,1)S(1)}, u32[]{:S(2)}, u32[]{:S(2)}) collective-permute-start(bf16[3,304,512]{2,1,0:T(8,128)(2,1)S(1)} %get-tuple-element.165), channel_id=1, source_target_pairs={{0,2},{1,3},{2,0},{3,1},{4,6},{5,7},{6,4},{7,5},{8,10},{9,11},{10,... | collective-permute-start | bytes 2801672 | tf_op jit(solution)/shard_map/ppermute | solution.py:456
  227.3 53.3 %collective-permute-start.9 = (bf16[2,3,304,512]{3,2,1,0:T(8,128)(2,1)S(1)}, bf16[2,3,304,512]{3,2,1,0:T(8,128)(2,1)S(1)}, u32[]{:S(2)}, u32[]{:S(2)}) collective-permute-start(bf16[2,3,304,512]{3,2,1,0:T(8,128)(2,1)S(1)} %copy-done.45), channel_id=1, source_target_pairs={{0,1},{1,0},{2,3},{3,2},{4,5},{5,4},{6,7},{7,6},{8,9},{9,8},{10,11... | collective-permute-start | bytes 5603336 | tf_op jit(solution)/shard_map/ppermute | solution.py:459
  282.1 23.2 %collective-permute-start.10 = (bf16[3,304,512]{2,1,0:T(8,128)(2,1)}, bf16[3,304,512]{2,1,0:T(8,128)(2,1)}, u32[]{:S(2)}, u32[]{:S(2)}) collective-permute-start(bf16[3,304,512]{2,1,0:T(8,128)(2,1)} %fusion.25), channel_id=1, source_target_pairs={{0,2},{1,3},{2,0},{3,1},{4,6},{5,7},{6,4},{7,5},{8,10},{9,11},{10,... | collective-permute-start | bytes 2801672 | tf_op jit(solution)/shard_map/ppermute | solution.py:456
  295.7 14.2 %collective-permute-start.19 = (bf16[64,2048]{1,0:T(8,128)(2,1)}, bf16[64,2048]{1,0:T(8,128)(2,1)S(1)}, u32[]{:S(2)}, u32[]{:S(2)}) collective-permute-start(bf16[64,2048]{1,0:T(8,128)(2,1)} %reduce-scatter.6.cloned.1.call-done), channel_id=1, source_target_pairs={{0,1},{1,0},{2,3},{3,2},{4,5},{5,4},{6,7},{7,6},{8,9},{9,8},{10,11... | collective-permute-start | bytes 786440 | tf_op jit(solution)/shard_map/ppermute | solution.py:459
  308.4 41.0 %collective-permute-start.11 = (bf16[3,145,512]{2,1,0:T(8,128)(2,1)}, bf16[3,145,512]{2,1,0:T(8,128)(2,1)S(1)}, u32[]{:S(2)}, u32[]{:S(2)}) collective-permute-start(bf16[3,145,512]{2,1,0:T(8,128)(2,1)} %get-tuple-element.179), channel_id=1, source_target_pairs={{0,2},{1,3},{2,0},{3,1},{4,6},{5,7},{6,4},{7,5},{8,10},{9,11},{10,... | collective-permute-start | bytes 1336328 | tf_op jit(solution)/shard_map/ppermute | solution.py:456
  310.8 44.3 %collective-permute-start.20 = (bf16[2,64,2048]{2,1,0:T(8,128)(2,1)}, bf16[2,64,2048]{2,1,0:T(8,128)(2,1)}, u32[]{:S(2)}, u32[]{:S(2)}) collective-permute-start(bf16[2,64,2048]{2,1,0:T(8,128)(2,1)} %pad_maximum_fusion.2), channel_id=1, source_target_pairs={{0,2},{1,3},{2,0},{3,1},{4,6},{5,7},{6,4},{7,5},{8,10},{9,11},{10,... | collective-permute-start | bytes 1572872 | tf_op jit(solution)/shard_map/ppermute | solution.py:456
  351.9 66.1 %collective-permute-start.22 = (bf16[2,256,512]{2,1,0:T(8,128)(2,1)}, bf16[2,256,512]{2,1,0:T(8,128)(2,1)}, u32[]{:S(2)}, u32[]{:S(2)}) collective-permute-start(bf16[2,256,512]{2,1,0:T(8,128)(2,1)} %pad_maximum_fusion.3), channel_id=1, source_target_pairs={{0,2},{1,3},{2,0},{3,1},{4,6},{5,7},{6,4},{7,5},{8,10},{9,11},{10,... | collective-permute-start | bytes 1572872 | tf_op jit(solution)/shard_map/ppermute | solution.py:456
  354.5 69.5 %collective-permute-start.16 = (bf16[3,145,512]{2,1,0:T(8,128)(2,1)}, bf16[3,145,512]{2,1,0:T(8,128)(2,1)S(1)}, u32[]{:S(2)}, u32[]{:S(2)}) collective-permute-start(bf16[3,145,512]{2,1,0:T(8,128)(2,1)} %slice.317), channel_id=1, source_target_pairs={{0,2},{1,3},{2,0},{3,1},{4,6},{5,7},{6,4},{7,5},{8,10},{9,11},{10,... | collective-permute-start | bytes 1336328 | tf_op jit(solution)/shard_map/ppermute | solution.py:456
  (53 other events, 484.4 us)
Sparse Core Ops, SparseCore 0:
  14.7 45.7 all-gather.6
  63.2 47.6 all-gather.8
  113.0 47.7 all-gather.10
  212.4 66.2 reduce-scatter.5
  282.7 66.5 reduce-scatter.7
  352.6 63.9 reduce-scatter.3

commit v2 on v1

v2 whole, which is shorter than its diff:
```python
import functools
import math

import jax
import jax.numpy as jnp
from jax import lax
from jax.experimental import pallas as pl
from jax.experimental.pallas import tpu as pltpu
from jax.sharding import PartitionSpec as P

H = 8
E = 4
EPSILON = 1e-06
BIG = -1e30
MIB = 1024 * 1024
F32 = jnp.float32
BF16 = jnp.bfloat16


def dot(a, b, dims=((1,), (0,))):
    return lax.dot_general(a, b, (dims, ((), ())), preferred_element_type=F32)


def dot_nt(a, b):
    return dot(a, b, ((1,), (1,)))


def dot_tn(a, b):
    return dot(a, b, ((0,), (0,)))


def norm_parts(values):
    center = values - jnp.mean(values, axis=-1, keepdims=True)
    spread = jnp.mean(center * center, axis=-1, keepdims=True)
    rstd = lax.rsqrt(spread + EPSILON)
    return center * rstd, rstd


def norm_back(grad, xhat, rstd):
    return rstd * (
        grad
        - jnp.mean(grad, axis=-1, keepdims=True)
        - xhat * jnp.mean(grad * xhat, axis=-1, keepdims=True)
    )


TINY = pl.CostEstimate(flops=1000, bytes_accessed=1000, transcendentals=0)


def params(limit, **more):
    return pltpu.CompilerParams(vmem_limit_bytes=limit * MIB, **more)


def placed(*arrays):
    return [
        pltpu.with_memory_space_constraint(a, pltpu.HBM) if a.size > 1 << 15 else a for a in arrays
    ]


def in_hbm(shape, dtype):
    return pltpu.HBM(shape, dtype)


def whole(shape):
    return pl.BlockSpec(shape, lambda *_: (0,) * len(shape))


def per_image(*shape):
    return pl.BlockSpec((1, *shape), lambda i: (i,) + (0,) * len(shape))


SCALARS = pl.BlockSpec(memory_space=pltpu.SMEM)


def attend_kernel(
    images, head_dim, at_ref, own_ref, oth_ref, bias_ref, parts_ref,
    att_m_ref, mail_ref, qkv_ref, hidden_ref, lse_ref, wq_ref, small_ref, vec_ref,
):
    rows = own_ref.shape[1]
    features = wq_ref.shape[0]

    @pl.when(pl.program_id(0) == 0)
    def _():
        part = features // 8
        vec = jnp.zeros((8, features), F32)
        row = lax.broadcasted_iota(jnp.int32, (part, features), 0)
        col = lax.broadcasted_iota(jnp.int32, (part, features), 1)
        for index in range(8):
            base = index * part
            wq_ref[base : base + part, :] = parts_ref[index, :part, : wq_ref.shape[1]]
            there = slice(images * rows + base, images * rows + base + part)
            mail_ref[there, :] = parts_ref[index, :part, wq_ref.shape[1] :]
            spread = (col == row + base).astype(F32).astype(BF16)
            vec = vec + dot(parts_ref[index, part:, :part], spread)[:8]
        vec_ref[...] = vec
        tall = jnp.concatenate([vec, vec[4:], jnp.zeros((116, features), F32)], axis=0)
        small_ref[...] = tall.T.astype(BF16)

    gain, offset = vec_ref[0:1, :], vec_ref[1:2, :]
    for half, ref in enumerate((own_ref, oth_ref)):
        xhat, _ = norm_parts(ref[0].astype(F32))
        hidden_ref[0, half * rows : (half + 1) * rows, :] = (xhat * gain + offset).astype(BF16)
    width = wq_ref.shape[1] // 3
    packed = dot(hidden_ref[0], wq_ref[...]).astype(BF16)
    scaling = 1.0 / math.sqrt(head_dim)
    qkv_ref[0, :, :width] = (packed[:, :width].astype(F32) * scaling).astype(BF16)
    qkv_ref[0, :, width:] = packed[:, width:]
    bias = bias_ref[0]
    lane = lax.broadcasted_iota(jnp.int32, (1, 128), 1)
    sub = lax.broadcasted_iota(jnp.int32, (128, 1), 0)
    for pair in range(width // 128):
        cols = slice(pair * 128, pair * 128 + 128)
        q2 = qkv_ref[0, :, cols]
        k2 = qkv_ref[0, :, width + pair * 128 : width + pair * 128 + 128]
        v2 = qkv_ref[0, :, 2 * width + pair * 128 : 2 * width + pair * 128 + 128]
        v_t = v2.T
        both = []
        for part in range(2):
            mine = (lane >= head_dim * part) & (lane < head_dim * (part + 1))
            qm = jnp.where(mine, q2, jnp.zeros_like(q2))
            scores = dot_nt(k2, qm) + bias
            peak = jnp.max(scores, axis=0, keepdims=True)
            expo = jnp.exp(scores - peak)
            total = jnp.sum(expo, axis=0, keepdims=True)
            lse_ref[0, 2 * pair + part : 2 * pair + part + 1, :] = peak + jnp.log(total)
            both.append(dot(v_t, (expo * (1.0 / total)).astype(BF16)))
        out = jnp.where(sub < head_dim, both[0], both[1]).astype(BF16).T
        att_m_ref[0, :, cols] = out[:rows]
        mail_ref[pl.ds(pl.multiple_of(pl.program_id(0) * rows, 16), rows), cols] = out[rows:]


def attend(at, x_own, x_oth, bias, parts, head_dim):
    images, rows, width = x_own.shape
    group = width // 2
    return pl.pallas_call(
        functools.partial(attend_kernel, images, head_dim),
        grid=(images,),
        in_specs=[
            SCALARS,
            per_image(rows, width),
            per_image(rows, width),
            per_image(2 * rows, 1),
            whole(parts.shape),
        ],
        out_specs=[
            per_image(rows, group),
            whole((images * rows + width, group)),
            per_image(2 * rows, 3 * group),
            per_image(2 * rows, width),
            per_image(8, 2 * rows),
            whole((width, 3 * group)),
            whole((width, 128)),
            whole((8, width)),
        ],
        out_shape=[
            jax.ShapeDtypeStruct((images, rows, group), BF16),
            jax.ShapeDtypeStruct((images * rows + width, group), BF16),
            in_hbm((images, 2 * rows, 3 * group), BF16),
            in_hbm((images, 2 * rows, width), BF16),
            in_hbm((images, 8, 2 * rows), F32),
            in_hbm((width, 3 * group), BF16),
            in_hbm((width, 128), BF16),
            jax.ShapeDtypeStruct((8, width), F32),
        ],
        compiler_params=params(40),
        cost_estimate=TINY,
        name="attend",
    )(*placed(at, x_own, x_oth, bias, parts))


def project_kernel(
    at_ref, att_m_ref, sent_ref, got_ref, x_ref, vec_ref, middle_ref, hidden_ref, proj_ref
):
    rows, group = att_m_ref.shape[1:]
    core, first = at_ref[1], pl.num_programs(0) * rows
    mine = pl.ds(pl.multiple_of(core * group + first, 16), group)
    other = pl.ds(pl.multiple_of((1 - core) * group + first, 16), group)

    def in_order(a, b):
        return jnp.concatenate([jnp.where(core == 0, a, b), jnp.where(core == 0, b, a)], axis=1)

    @pl.when(pl.program_id(0) == 0)
    def _():
        proj_ref[...] = in_order(sent_ref[mine, :], got_ref[mine, :])

    att_r = got_ref[pl.ds(pl.multiple_of(pl.program_id(0) * rows, 16), rows), :]
    halves = [
        dot(att_m_ref[0], ref[mine, :]) + dot(att_r, ref[other, :]) for ref in (sent_ref, got_ref)
    ]
    middle = x_ref[0].astype(F32) + in_order(*halves)
    middle_ref[0] = middle
    xhat, _ = norm_parts(middle)
    hidden_ref[0] = (xhat * vec_ref[2:3, :] + vec_ref[3:4, :]).astype(BF16)


def project(at, att_m, sent, got, x_own, vecs):
    images, rows, width = x_own.shape
    group = att_m.shape[2]
    return pl.pallas_call(
        project_kernel,
        grid=(images,),
        in_specs=[
            SCALARS,
            per_image(rows, group),
            whole(sent.shape),
            whole(got.shape),
            per_image(rows, width),
            whole(vecs.shape),
        ],
        out_specs=[per_image(rows, width), per_image(rows, width), whole((group, width))],
        out_shape=[
            in_hbm(x_own.shape, F32),
            jax.ShapeDtypeStruct(x_own.shape, BF16),
            in_hbm((group, width), BF16),
        ],
        compiler_params=params(24),
        cost_estimate=TINY,
        name="project",
    )(*placed(at, att_m, sent, got, x_own, vecs))


BLOCKS = (
    ((1, 0), (1, 1)),
    ((3, 0), (3, 1)),
    ((1, 2), (0, 2)),
    ((3, 2), (2, 2)),
    ((0, 0), (0, 1)),
    ((2, 0), (2, 1)),
)
EARLY = 4


def load_weights(parts_ref, up_ref, down_ref, sem):
    part = up_ref.shape[0] // 8
    width, units = down_ref.shape[1], up_ref.shape[1] // 8
    copies = []
    for index in range(8):
        base = slice(index * part, index * part + part)
        for block in range(up_ref.shape[1] // width):
            copies.append(
                pltpu.make_async_copy(
                    parts_ref.at[index, block * part : (block + 1) * part, :],
                    up_ref.at[base, block * width : (block + 1) * width],
                    sem.at[0],
                )
            )
        base = slice(index * units, (index + 1) * units)
        first = up_ref.shape[1] // width * part
        copies.append(
            pltpu.make_async_copy(
                parts_ref.at[index, first : first + units, :], down_ref.at[base, :], sem.at[1]
            )
        )
    return copies


def hidden_units(splits, xs, g_ref, up_ref, down_ref, act_ref, gp_ref):
    ff = up_ref.shape[1]
    chunk = ff // splits
    ret = dx = None
    for part in range(splits):
        cols = slice(part * chunk, (part + 1) * chunk)
        pre = dot(xs, up_ref[:, cols])
        back = dot_nt(g_ref[...], down_ref[cols, :])
        cdf = 0.5 + 0.5 * lax.erf(pre * math.sqrt(0.5))
        pdf = jnp.exp(-0.5 * pre * pre) * (1.0 / math.sqrt(2.0 * math.pi))
        act = (pre * cdf).astype(BF16)
        gp = (back * (cdf + pre * pdf)).astype(BF16)
        act_ref[:, cols] = act
        gp_ref[:, cols] = gp
        ret_part = dot(act, down_ref[cols, :])
        dx_part = dot_nt(gp, up_ref[:, cols])
        ret = ret_part if ret is None else ret + ret_part
        dx = dx_part if dx is None else dx + dx_part
    return ret, dx


def routing(xs, wr_ref, mine):
    logits = dot(xs, wr_ref[...])
    lane = lax.broadcasted_iota(jnp.int32, (1, 128), 1)
    logits = jnp.where((lane >= 4) & (lane < 4 + 2 * E), logits, BIG)
    grown = jnp.exp(logits - jnp.max(logits, axis=-1, keepdims=True))
    once = lane < 4 + E
    router = grown / jnp.sum(jnp.where(once, grown, 0.0), axis=-1, keepdims=True)
    sel = jnp.where((lane == 4 + mine) | (lane == 4 + E + mine), 1.0, 0.0)
    return router, sel, jnp.sum(jnp.where(once, router * sel, 0.0), axis=-1, keepdims=True)


def two_parts(values):
    high = values.astype(BF16)
    return high, (values - high.astype(F32)).astype(BF16)


def expert_first_kernel(
    splits, filled, at_ref, h0, h1, h2, h3, cm, co, wr_ref, parts_ref,
    pos_ref, xs_ref, cs_ref, g_ref, act_ref, gp_ref, ret_ref, dx_ref,
    up_ref, down_ref, sem, piece_ref, piece_sem,
):
    step = pl.program_id(0)
    rows = h0.shape[1]
    hs, cs = (h0, h1, h2, h3), (cm.at[0], cm.at[1], co.at[0], co.at[1])
    mine = at_ref[2]

    def pieces_of(number):
        copies = []
        for k, (piece, image) in enumerate(BLOCKS[number]):
            for j, kind in enumerate((hs, cs)):
                spot = number * 4 + 2 * k + j
                copies.append(
                    pltpu.make_async_copy(
                        kind[piece].at[image], piece_ref.at[spot], piece_sem.at[number]
                    )
                )
        return copies

    def copies():
        return load_weights(parts_ref, up_ref, down_ref, sem)

    @pl.when(step == 0)
    def _():
        for number in range(len(BLOCKS)):
            for copy in pieces_of(number):
                copy.start()
            if number == 0:
                for copy in copies():
                    copy.start()

    token = lax.broadcasted_iota(jnp.int32, (1, rows), 1)
    slot = lax.broadcasted_iota(jnp.int32, (rows, rows), 0)
    before = (slot < lax.broadcasted_iota(jnp.int32, (rows, rows), 1)).astype(F32).astype(BF16)
    for number, block in enumerate(BLOCKS):

        @pl.when(step == number)
        def _(number=number, block=block):
            for copy in pieces_of(number):
                copy.wait()
            base, xs, got = 0.0, None, None
            for k in range(2):
                spot = number * 4 + 2 * k
                code = piece_ref[spot + 1, filled // 16 * 16 : filled // 16 * 16 + 16, :rows]
                code = code.astype(F32)[filled % 16 : filled % 16 + 1, :]
                first = jnp.floor(code * (1.0 / E))
                second = code - E * first
                own = mine.astype(F32)
                named = ((first == own) | (second == own)) & (token < filled)
                flag = jnp.where(named, 1.0, 0.0)
                rank = dot(jnp.broadcast_to(flag, (16, rows)).astype(BF16), before)[0:1, :] + base
                rank = jnp.where(named, rank, -1.0)
                base = base + jnp.sum(flag, axis=-1, keepdims=True)
                pos_ref[k : k + 1, :] = rank
                pick = (slot.astype(F32) == rank).astype(F32).astype(BF16)
                a, b = dot(pick, piece_ref[spot]), dot(pick, piece_ref[spot + 1])
                xs, got = (a, b) if xs is None else (xs + a, got + b)
            xs_ref[...] = xs.astype(BF16)
            cs_ref[...] = got.astype(BF16)

    xs = xs_ref[...]
    _, _, weight = routing(xs, wr_ref, mine)
    g_ref[...] = (cs_ref[...].astype(F32) * weight).astype(BF16)

    @pl.when(step == 0)
    def _():
        for copy in copies():
            copy.wait()

    ret, dx = hidden_units(splits, xs, g_ref, up_ref, down_ref, act_ref, gp_ref)
    ret_ref[...] = ret.astype(BF16)
    dx_ref[...] = dx.astype(BF16)


def slot_block(rows, cols, first=0):
    return pl.BlockSpec((rows, cols), lambda i: (i + first, 0))


def expert_first(at, hidden, cots_m, cots_o, wr, parts, filled):
    images, rows, width = hidden[0].shape
    ff = (parts.shape[1] - 2 * width // 8) * 8
    count = len(BLOCKS)
    outs = [
        (8, rows, F32),
        (rows, width, BF16),
        (rows, width, BF16),
        (rows, width, BF16),
        (rows, ff, BF16),
        (rows, ff, BF16),
        (rows, width, BF16),
        (rows, width, BF16),
    ]
    return pl.pallas_call(
        functools.partial(expert_first_kernel, 2, filled),
        grid=(count,),
        in_specs=[
            SCALARS,
            *[pl.BlockSpec(memory_space=pl.ANY)] * 6,
            whole(wr.shape),
            pl.BlockSpec(memory_space=pl.ANY),
        ],
        out_specs=[slot_block(a, b) for a, b, _ in outs],
        out_shape=[in_hbm((count * a, b), kind) for a, b, kind in outs],
        scratch_shapes=[
            pltpu.VMEM((width, ff), BF16),
            pltpu.VMEM((ff, width), BF16),
            pltpu.SemaphoreType.DMA((2,)),
            pltpu.VMEM((4 * count, rows, width), BF16),
            pltpu.SemaphoreType.DMA((count,)),
        ],
        compiler_params=params(30),
        cost_estimate=TINY,
        name="expert_first",
    )(*placed(at, *hidden, cots_m, cots_o, wr, parts))


def expert_second_kernel(
    splits, step_count, at_ref, pos_ref, xs_ref, cs_ref, g_ref, ret0_ref, dx0_ref, wr_ref,
    parts_ref, *refs,
):
    step = pl.program_id(0)
    rows = xs_ref.shape[0]
    *refs, up_ref, down_ref, sem = refs
    early = step_count == EARLY
    if early:
        act_ref, gp_ref, lg_ref, dh_m, dh_o, ret_m, ret_o, extra_m, extra_o = refs
        firsts = [((dh_m, ret_m), 0), ((dh_o, ret_o), 0)]
        targets = [[(dh, 0, back, 0), (dh, 1, back, 1)] for (dh, back), _ in firsts]
        targets += [
            [(dh, 2, back, 2), (extra, 0, extra, 1)]
            for ((dh, back), _), extra in zip(firsts, (extra_m, extra_o))
        ]
    else:
        extra_m, extra_o, act_ref, gp_ref, lg_ref, dh_m, dh_o, ret_m, ret_o = refs
        targets = [[(a, 0, b, 0), (a, 1, b, 1)] for a, b in ((dh_m, ret_m), (dh_o, ret_o))]

        @pl.when(step == 0)
        def _():
            for extra, dh, back in ((extra_m, dh_m, ret_m), (extra_o, dh_o, ret_o)):
                dh[2] = extra[0]
                back[2] = extra[1]


    @pl.when(step == 0)
    def _():
        copies = load_weights(parts_ref, up_ref, down_ref, sem)
        for copy in copies:
            copy.start()
        for copy in copies:
            copy.wait()

    ret, dx = hidden_units(splits, xs_ref[...], g_ref, up_ref, down_ref, act_ref, gp_ref)
    ret = ret + ret0_ref[...].astype(F32)
    router, sel, weight = routing(xs_ref[...], wr_ref, at_ref[2])
    gate = jnp.sum(cs_ref[...].astype(F32) * ret, axis=-1, keepdims=True)
    high, low = two_parts(gate * weight * (sel - router))
    lg = jnp.where(lax.broadcasted_iota(jnp.int32, (1, 128), 1) < 4 + E, high, low)
    lg_ref[...] = lg
    dxb = (dx + dx0_ref[...].astype(F32) + dot_nt(lg, wr_ref[...])).astype(BF16)
    retb = (ret * weight).astype(BF16)
    slot = lax.broadcasted_iota(jnp.int32, (rows, rows), 0).astype(F32)
    picks = [(slot == pos_ref[k : k + 1, :]).astype(F32).astype(BF16) for k in range(2)]
    for number, target in enumerate(targets):

        @pl.when(step == number)
        def _(target=target):
            for pick, (dh, i, back, j) in zip(picks, target):
                dh[i] = dot_tn(pick, dxb).astype(BF16)
                back[j] = dot_tn(pick, retb).astype(BF16)


def expert_second(at, first, wr, parts, start, count, extras=()):
    pos, xs, cs, g, _, _, ret, dx = first
    rows, width = xs.shape[0] // len(BLOCKS), xs.shape[1]
    ff = (parts.shape[1] - 2 * width // 8) * 8
    sizes = (3, 3, 3, 3) if extras else (3, 3, 3, 3, 2, 2)
    return pl.pallas_call(
        functools.partial(expert_second_kernel, 2, count),
        grid=(count,),
        in_specs=[
            SCALARS,
            slot_block(8, rows, start),
            slot_block(rows, width, start),
            slot_block(rows, width, start),
            slot_block(rows, width, start),
            slot_block(rows, width, start),
            slot_block(rows, width, start),
            whole(wr.shape),
            pl.BlockSpec(memory_space=pl.ANY),
            *[whole(e.shape) for e in extras],
        ],
        out_specs=[slot_block(rows, ff), slot_block(rows, ff), slot_block(rows, 128)]
        + [whole((n, rows, width)) for n in sizes],
        out_shape=[
            in_hbm((count * rows, ff), BF16),
            in_hbm((count * rows, ff), BF16),
            in_hbm((count * rows, 128), BF16),
        ]
        + [jax.ShapeDtypeStruct((n, rows, width), BF16) for n in sizes],
        scratch_shapes=[
            pltpu.VMEM((width, ff), BF16),
            pltpu.VMEM((ff, width), BF16),
            pltpu.SemaphoreType.DMA((2,)),
        ],
        compiler_params=params(30),
        cost_estimate=TINY,
        name="expert_second",
    )(*placed(at, pos, xs, cs, g, ret, dx, wr, parts, *extras))


def weight_grad_kernel(ends, *refs):
    count = len(ends)
    _, xs_ref, g_ref = refs[:3]
    lgs, gps, acts = refs[3 : 3 + count], refs[3 + count : 3 + 2 * count], refs[3 + 2 * count : 3 + 3 * count]
    out_ref, router_ref, xs_t, g_t, turned = refs[3 + 3 * count :]
    step = pl.program_id(0)
    width = xs_t.shape[0]
    part, cols = width // 8, gps[0].shape[1]
    spans = list(zip((0, *ends[:-1]), ends))

    @pl.when(step == 0)
    def _():
        xs_t[...] = xs_ref[...].T
        g_t[...] = g_ref[...].T
        total = None
        for (low, high), lg in zip(spans, lgs):
            one = dot(xs_t[:, low:high], lg[...])
            total = one if total is None else total + one
        router_ref[...] = total

    up = down = None
    for (low, high), gp, act in zip(spans, gps, acts):
        one, two = dot(xs_t[:, low:high], gp[...]), dot(g_t[:, low:high], act[...])
        up, down = (one, two) if up is None else (up + one, down + two)
    turned[:width, :] = up.astype(BF16)
    block = step * cols // width
    lanes = pl.ds(pl.multiple_of(step * cols % width, cols), cols)
    into = pl.ds(pl.multiple_of(block * part, part), part)
    for index in range(8):
        out_ref[index, into, lanes] = turned[index * part : (index + 1) * part, :]
    half = cols // 2
    first = out_ref.shape[1] - half
    tall = down.T.astype(BF16)
    out_ref[2 * step, first:, :] = tall[:half]
    out_ref[2 * step + 1, first:, :] = tall[half:]


def weight_grad(at, xs, g, lgs, gps, acts):
    slots, width = xs.shape
    ff = gps[0].shape[1]
    cols = ff // 4
    out = (8, ff // width * (width // 8) + ff // 8, width)
    ends = []
    for gp in gps:
        ends.append(gp.shape[0] + (ends[-1] if ends else 0))
    return pl.pallas_call(
        functools.partial(weight_grad_kernel, tuple(ends)),
        grid=(4,),
        in_specs=[SCALARS, whole(xs.shape), whole(g.shape)]
        + [whole(a.shape) for a in lgs]
        + [pl.BlockSpec((a.shape[0], cols), lambda i: (0, i)) for a in (*gps, *acts)],
        out_specs=[whole(out), whole((width, 128))],
        out_shape=[jax.ShapeDtypeStruct(out, BF16), in_hbm((width, 128), F32)],
        scratch_shapes=[
            pltpu.VMEM((width, slots), BF16),
            pltpu.VMEM((width, slots), BF16),
            pltpu.VMEM((width, cols), BF16),
        ],
        compiler_params=params(30),
        cost_estimate=TINY,
        name="weight_grad",
    )(*placed(at, xs, g, *lgs, *gps, *acts))


def settle_kernel(at_ref, zero_ref, one_ref, up_ref, down_ref):
    part, units = up_ref.shape[1], zero_ref.shape[1] - 2 * up_ref.shape[1]
    for half, ref in enumerate((zero_ref, one_ref)):
        for index in range(8):
            rows = slice(index // 4 * part, index // 4 * part + part)
            to = (2 * index + half) * units
            from_ = index % 4 * units
            up_ref[0, :, to : to + units] = ref[0, rows, from_ : from_ + units].astype(F32)
        down_ref[0, half * units : (half + 1) * units, :] = ref[0, 2 * part :, :].astype(F32)


def settle_experts(at, zero, one):
    _, rows, width = zero.shape
    part = width // 8
    units = rows - 2 * part
    piece = pl.BlockSpec((1, rows, width), lambda i, at: (i ^ at[2], 0, 0))
    return pl.pallas_call(
        settle_kernel,
        grid_spec=pltpu.PrefetchScalarGridSpec(
            num_scalar_prefetch=1,
            grid=(E,),
            in_specs=[piece, piece],
            out_specs=[
                pl.BlockSpec((1, part, 16 * units), lambda i, at: (i, 0, 0)),
                pl.BlockSpec((1, 2 * units, width), lambda i, at: (i, 0, 0)),
            ],
        ),
        out_shape=[
            jax.ShapeDtypeStruct((E, part, 16 * units), F32),
            jax.ShapeDtypeStruct((E, 2 * units, width), F32),
        ],
        compiler_params=params(24),
        cost_estimate=TINY,
        name="settle_experts",
    )(*placed(at, zero, one))


def middle_back_kernel(
    filled, at_ref, a_ref, ar_ref, xr_ref, mid_ref, cot_ref, vec_ref, am_ref,
    got_ref, r0_ref, r1_ref,
    gm_ref, low_ref, send_ref, keep_ref, sums_ref, proj_ref,
):
    rows, width = mid_ref.shape[1:]
    group = am_ref.shape[2]

    @pl.when(pl.program_id(0) == 0)
    def _():
        sums_ref[...] = jnp.zeros_like(sums_ref)
        proj_ref[...] = jnp.zeros_like(proj_ref)

    grad = a_ref[0].astype(F32) + ar_ref[0].astype(F32) + xr_ref[0].astype(F32)
    xhat, rstd = norm_parts(mid_ref[0])
    sums_ref[2:3, :] += jnp.sum(grad * xhat, axis=0, keepdims=True)
    sums_ref[3:4, :] += jnp.sum(grad, axis=0, keepdims=True)
    out = cot_ref[0, 0].astype(F32) + norm_back(grad * vec_ref[2:3, :], xhat, rstd)
    row = lax.broadcasted_iota(jnp.int32, (rows, 1), 0)
    out = jnp.where(row < filled, out, 0.0)
    gm_ref[0] = out
    low = out.astype(BF16)
    low_ref[0] = low
    proj_ref[:group, :] += dot_tn(am_ref[0], low)
    att_r = got_ref[pl.ds(pl.multiple_of(pl.program_id(0) * rows, 16), rows), :]
    proj_ref[group:, :] += dot_tn(att_r, low)

    @pl.when(pl.program_id(0) == pl.num_programs(0) - 1)
    def _():
        part = width // 8
        router = (r0_ref[...] + r1_ref[...]).T
        router = jnp.concatenate([jnp.zeros((4, width), F32), router[4:8] + router[8:12]], axis=0)
        lines = jnp.concatenate(two_parts(sums_ref[...] + router), axis=0)
        row = lax.broadcasted_iota(jnp.int32, (width, 128), 0)
        col = lax.broadcasted_iota(jnp.int32, (width, 128), 1)
        for ref, side in ((send_ref, 1 - at_ref[3]), (keep_ref, at_ref[3])):
            for z in range(4):
                base = (2 * z + side) * part
                from_ = pl.multiple_of(base ^ (at_ref[1] * group), part)
                ref[z, :part, :] = proj_ref[pl.ds(from_, part), :].astype(BF16)
                pick = ((row == col + base) & (col < part)).astype(F32).astype(BF16)
                ref[z, part:, :128] = dot(lines, pick).astype(BF16)
                ref[z, part:, 128:] = jnp.zeros((16, width - 128), BF16)


def middle_back(at, mine, near, from_x, middle, cots, vecs, att_m, got, routers, filled):
    images, rows, width = middle.shape
    one = per_image(rows, width)
    cot = pl.BlockSpec((1, 1, rows, width), lambda i: (0, i, 0, 0))
    group = att_m.shape[2]
    piece = (4, width // 8 + 16, width)
    return pl.pallas_call(
        functools.partial(middle_back_kernel, filled),
        grid=(images,),
        in_specs=[SCALARS]
        + [one] * 4
        + [cot, whole(vecs.shape), per_image(rows, group), whole(got.shape)]
        + [whole(routers[0].shape)] * 2,
        out_specs=[one, one, whole(piece), whole(piece)],
        out_shape=[
            in_hbm(middle.shape, F32),
            jax.ShapeDtypeStruct(middle.shape, BF16),
            in_hbm(piece, BF16),
            in_hbm(piece, BF16),
        ],
        scratch_shapes=[
            pltpu.VMEM((8, width), F32),
            pltpu.VMEM((width, width), F32),
        ],
        compiler_params=params(32),
        cost_estimate=TINY,
        name="middle_back",
    )(*placed(at, mine, near, from_x, middle, cots, vecs, att_m, got, *routers))


def layer_kernel(mid_ref, a_ref, ar_ref, xr_ref, mine_ref, send_ref):
    total = mid_ref[0] + a_ref[0].astype(F32) + ar_ref[0].astype(F32) + xr_ref[0].astype(F32)
    count = mine_ref.shape[1]
    mine_ref[0] = total[:count].astype(BF16)
    send_ref[0] = total[count : 2 * count].astype(BF16)


def layer_sum(middle, mine, near, from_x, quarter):
    images, rows, width = middle.shape
    one, part = per_image(rows, width), per_image(quarter, width)
    return pl.pallas_call(
        layer_kernel,
        grid=(images,),
        in_specs=[one] * 4,
        out_specs=[part, part],
        out_shape=[jax.ShapeDtypeStruct((images, quarter, width), BF16)] * 2,
        compiler_params=params(24),
        cost_estimate=TINY,
        name="layer_sum",
    )(*placed(middle, mine, near, from_x))


def attend_back_kernel(
    head_dim, at_ref, lm_ref, lo_ref, pm_ref, qkv_ref, lse_ref, bias_ref, h1_ref, wq_ref,
    dm_ref, do_ref, gq_ref, grad_ref, low_ref,
):
    rows = lm_ref.shape[1]
    low_ref[:rows, :] = lm_ref[0]
    low_ref[rows:, :] = lo_ref[0]
    out_grad = dot_nt(low_ref[...], pm_ref[...]).astype(BF16)
    width = pm_ref.shape[0]
    bias = bias_ref[0]
    lane = lax.broadcasted_iota(jnp.int32, (1, 128), 1)
    sub = lax.broadcasted_iota(jnp.int32, (128, 1), 0)
    scaling = 1.0 / math.sqrt(head_dim)
    for pair in range(width // 128):
        cols = slice(pair * 128, pair * 128 + 128)
        k_cols = slice(width + pair * 128, width + pair * 128 + 128)
        v_cols = slice(2 * width + pair * 128, 2 * width + pair * 128 + 128)
        q2, k2, v2 = qkv_ref[0, :, cols], qkv_ref[0, :, k_cols], qkv_ref[0, :, v_cols]
        o2 = out_grad[:, cols]
        k_t = k2.T
        dv = dk = None
        both = []
        for part in range(2):
            mine = (lane >= head_dim * part) & (lane < head_dim * (part + 1))
            qm = jnp.where(mine, q2, jnp.zeros_like(q2))
            om = jnp.where(mine, o2, jnp.zeros_like(o2))
            head = 2 * pair + part
            probs = jnp.exp(dot_nt(k2, qm) + bias - lse_ref[0, head : head + 1, :])
            prob_grad = dot_nt(v2, om)
            delta = jnp.sum(probs * prob_grad, axis=0, keepdims=True)
            score_grad = (probs * (prob_grad - delta)).astype(BF16)
            dv_part = dot(probs.astype(BF16), om)
            dk_part = dot(score_grad, qm)
            dv = dv_part if dv is None else dv + dv_part
            dk = dk_part if dk is None else dk + dk_part
            both.append(dot(k_t, score_grad))
        dq = (jnp.where(sub < head_dim, both[0], both[1]) * scaling).astype(BF16).T
        grad_ref[:, cols] = dq
        grad_ref[:, k_cols] = dk.astype(BF16)
        grad_ref[:, v_cols] = dv.astype(BF16)
    hidden_grad = dot_nt(grad_ref[...], wq_ref[...]).astype(BF16)
    dm_ref[0] = hidden_grad[:rows]
    do_ref[0] = hidden_grad[rows:]
    grad_qkv = dot_tn(h1_ref[0], grad_ref[...])

    @pl.when(pl.program_id(0) == 0)
    def _():
        gq_ref[...] = grad_qkv

    @pl.when(pl.program_id(0) > 0)
    def _():
        gq_ref[...] += grad_qkv


def attend_back(at, low_m, low_o, proj_m, qkv, lse, bias, hidden_one, wq, head_dim):
    images, rows, width = low_m.shape
    group = proj_m.shape[0]
    return pl.pallas_call(
        functools.partial(attend_back_kernel, head_dim),
        grid=(images,),
        in_specs=[
            SCALARS,
            per_image(rows, width),
            per_image(rows, width),
            whole(proj_m.shape),
            per_image(2 * rows, 3 * group),
            per_image(8, 2 * rows),
            per_image(2 * rows, 1),
            per_image(2 * rows, width),
            whole(wq.shape),
        ],
        out_specs=[
            per_image(rows, width),
            per_image(rows, width),
            whole((width, 3 * group)),
        ],
        out_shape=[
            in_hbm((images, rows, width), BF16),
            jax.ShapeDtypeStruct((images, rows, width), BF16),
            in_hbm((width, 3 * group), F32),
        ],
        scratch_shapes=[
            pltpu.VMEM((2 * rows, 3 * group), BF16),
            pltpu.VMEM((2 * rows, width), BF16),
        ],
        compiler_params=params(48),
        cost_estimate=TINY,
        name="attend_back",
    )(*placed(at, low_m, low_o, proj_m, qkv, lse, bias, hidden_one, wq))


def input_back_kernel(
    at_ref, x_ref, gm_ref, vec_ref, a_ref, ar_ref, gq_ref, r_send_ref, r_keep_ref,
    out_ref, go_ref, send_ref, keep_ref, sums_ref,
):
    step, images = pl.program_id(0), pl.num_programs(0)
    grad = a_ref[0].astype(F32) + ar_ref[0].astype(F32)
    xhat, rstd = norm_parts(x_ref[0].astype(F32))
    out = gm_ref[0] + norm_back(grad * vec_ref[0:1, :], xhat, rstd)
    count = out_ref.shape[1]
    out_ref[0] = out[:count]
    go_ref[0] = out[count : 2 * count].astype(BF16)

    @pl.when(step == 0)
    def _():
        sums_ref[...] = jnp.zeros_like(sums_ref)

    sums_ref[0:1, :] += jnp.sum(grad * xhat, axis=0, keepdims=True)
    sums_ref[1:2, :] += jnp.sum(grad, axis=0, keepdims=True)

    @pl.when(step == images - 1)
    def _():
        total = gq_ref[...]
        width = grad.shape[1]
        part = width // 8
        lines = jnp.concatenate(two_parts(sums_ref[...]), axis=0)
        row = lax.broadcasted_iota(jnp.int32, (width, 128), 0)
        col = lax.broadcasted_iota(jnp.int32, (width, 128), 1)
        for index in range(8):
            base = index * part
            own = total[base : base + part].astype(BF16)
            half = jnp.concatenate([own[: part // 2, width:], own[part // 2 :, width:]], axis=1)
            pick_line = ((row == col + base) & (col < part)).astype(F32).astype(BF16)
            line = dot(lines, pick_line).astype(BF16)
            tail = jnp.concatenate([line, jnp.zeros((16, width - 128), BF16)], axis=1)
            block = jnp.concatenate([own[:, :width], half], axis=0)
            last = part + block.shape[0]

            def put(ref, block=block, tail=tail, z=index // 2, last=last):
                ref[z, part:last] = block
                ref[z, last + 16 :] = tail

            @pl.when(at_ref[3] == index % 2)
            def _(put=put):
                put(keep_ref)

            @pl.when(at_ref[3] != index % 2)
            def _(put=put):
                put(send_ref)

        last = send_ref.shape[1] - 32
        for ref, from_ in ((send_ref, r_send_ref), (keep_ref, r_keep_ref)):
            ref[:, :part] = from_[:, :part]
            ref[:, last : last + 16] = from_[:, part:]


def input_back(at, x_own, grad_middle, vecs, mine, near, grads, r_parts, quarter):
    images, rows, width = x_own.shape
    one, part = per_image(rows, width), per_image(quarter, width)
    first = r_parts[0].shape[1]
    more = (4, first + width // 8 + (grads.shape[1] - width) * (width // 8) // width + 16, width)
    return pl.pallas_call(
        input_back_kernel,
        grid=(images,),
        in_specs=[SCALARS, one, one, whole(vecs.shape), one, one, whole(grads.shape)]
        + [whole(r.shape) for r in r_parts],
        out_specs=[part, part, whole(more), whole(more)],
        out_shape=[
            jax.ShapeDtypeStruct((images, quarter, width), F32),
            jax.ShapeDtypeStruct((images, quarter, width), BF16),
            jax.ShapeDtypeStruct(more, BF16),
            jax.ShapeDtypeStruct(more, BF16),
        ],
        scratch_shapes=[pltpu.VMEM((8, width), F32)],
        compiler_params=params(32),
        cost_estimate=TINY,
        name="input_back",
    )(*placed(at, x_own, grad_middle, vecs, mine, near, grads, *r_parts))


def shards(
    tokens,
    key_mask,
    expert_ids,
    ln1_gain,
    ln1_bias,
    qkv_weight,
    proj_weight,
    ln2_gain,
    ln2_bias,
    router_weight,
    up_weight,
    down_weight,
    cotangent,
):
    n_seq, n_wide = lax.axis_size("seq"), lax.axis_size("wide")
    images, quarter, width = tokens.shape
    head_dim = width // H
    group = width // 2
    filled = 2 * quarter
    rows = -(-(filled + 1) // 16) * 16
    place = lax.axis_index("seq")
    chip, core = place // 2, place % 2
    direct = n_wide == 8
    spot = lax.axis_index("wide") if direct else 0
    at = jnp.stack([jnp.int32(spot), core, place, jnp.int32(spot) % 2])
    part = width // 8

    def over_seq(a, turn):
        return lax.ppermute(a, "seq", [(i, i ^ turn) for i in range(n_seq)])

    def over_x(a):
        return over_seq(a, 2)

    def over_core(a):
        return over_seq(a, 1)

    def over_wide(a, turn):
        return lax.ppermute(a, "wide", [(i, i ^ turn) for i in range(n_wide)])

    def after(value, *first):
        return lax.optimization_barrier((value, *first))[0]

    def images_of(a, of_chip):
        pair = lax.dynamic_slice_in_dim(a, of_chip * (images - 2), 2, 0)
        single = lax.dynamic_slice_in_dim(a, images // 2 - 1 + of_chip, 1, 0)
        return jnp.concatenate([pair, single], axis=0)

    def joined(first, second):
        both = jnp.concatenate([first, second], axis=1)
        return jnp.pad(both, ((0, 0), (0, rows - filled)) + ((0, 0),) * (both.ndim - 2))

    def cells(quarters, of_chip, of_core):
        first = lax.dynamic_index_in_dim(quarters, 2 * of_chip + of_core, 1, False)
        second = lax.dynamic_index_in_dim(quarters, 2 * (1 - of_chip) + of_core, 1, False)
        return joined(images_of(first, of_chip), images_of(second, of_chip))

    mask = key_mask.reshape(images, n_seq, quarter)
    valid = jnp.concatenate([cells(mask, chip, core), cells(mask, chip, 1 - core)], axis=1)
    bias = jnp.where(valid > 0, 0.0, BIG).astype(F32)[..., None]

    def heads_of(a):
        return jnp.concatenate(
            [lax.dynamic_slice_in_dim(a, (2 * i + core) * group, group, 1) for i in range(3)],
            axis=1,
        )

    wq = heads_of(qkv_weight)
    proj = lax.dynamic_slice_in_dim(proj_weight, core * group, group, 1)
    lines = jnp.stack([ln1_gain, ln1_bias, ln2_gain, ln2_bias])
    lines = jnp.concatenate([lines, router_weight.T], axis=0)
    up = lax.dynamic_index_in_dim(up_weight, place, 0, False)
    down = lax.dynamic_index_in_dim(down_weight, place, 0, False)
    units = down.shape[0] // 2

    def first_parts(wq, proj, lines):
        both = jnp.concatenate([wq, proj], axis=1)
        fill = ((0, 16 - lines.shape[0]), (0, both.shape[1] - lines.shape[1]))
        return jnp.concatenate([both, jnp.pad(lines, fill)], axis=0)

    def half_of(up, down, half):
        cols = up.reshape(up.shape[0], n_wide, 2, units)[:, :, half].reshape(up.shape[0], -1)
        down = down.reshape(-1, 2, units, width)[:, half].reshape(-1, width)
        blocks = [cols[:, i : i + width] for i in range(0, cols.shape[1], width)]
        return jnp.concatenate([*blocks, down], axis=0)

    one_all = first_parts(wq, proj, lines)
    one_all = jnp.broadcast_to(one_all[None], (8, *one_all.shape))
    codes = (expert_ids[..., 0] * E + expert_ids[..., 1]).astype(BF16)
    codes = jnp.pad(codes, ((0, 0), (0, width - quarter)))[:, None, :]
    cot = jnp.concatenate([cotangent, codes], axis=1)
    x_got = over_x(images_of(after(tokens, one_all), 1 - chip))
    x_own = joined(images_of(tokens, chip), x_got)
    x_oth = over_core(after(x_own, bias, cot))
    cot_got = over_x(after(cot, x_got))

    def cot_of(first, second):
        code = jnp.concatenate(
            [first[:, quarter:, :quarter], second[:, quarter:, :quarter]], axis=2
        )
        code = jnp.pad(code, ((0, 0), (0, rows - filled - 1), (0, width - filled)))
        return jnp.concatenate([first[:, :quarter], second[:, :quarter], code], axis=1)

    z_groups = [[y + 2 * z for z in range(4)] for y in range(2)]

    def all_of(a, axis=0):
        return lax.all_gather(a, "wide", axis=axis, tiled=True)

    if direct:
        ones = lax.all_to_all(one_all, "wide", 0, 0, tiled=True)
        twos, threes = (
            lax.all_gather(after(half_of(up, down, half), ones, x_oth), "wide") for half in range(2)
        )
    else:

        def eight(a, axis=0):
            return jnp.split(a, 8, axis=axis)

        ones = jnp.stack([first_parts(*a) for a in zip(eight(all_of(wq)), eight(all_of(proj)), eight(all_of(lines, 1), 1))])
        ups, downs = eight(all_of(up)), eight(all_of(down))
        twos, threes = (
            jnp.stack([half_of(a, b, half) for a, b in zip(ups, downs)]) for half in range(2)
        )

    att_m, mail, qkv, hidden_one, lse, wq, small, vecs = attend(
        at, x_own, x_oth, bias, ones, head_dim
    )
    mail_got = over_core(mail)
    middle, hidden_two, proj_m = project(at, att_m, mail, mail_got, x_own, vecs)
    cot_got = after(cot_got, hidden_two)
    cots_m = jnp.stack(
        [
            cot_of(images_of(cot, chip), images_of(cot_got, chip)),
            cot_of(images_of(cot_got, 1 - chip), images_of(cot, 1 - chip)),
        ]
    )
    cots_o = over_core(cots_m)
    hidden_b = over_x(hidden_two)
    hidden = (hidden_two, hidden_b, over_core(hidden_two), over_core(hidden_b))
    first = expert_first(at, hidden, cots_m, cots_o, small, twos, filled)
    _, xs, _, g_slots, act0, gp0, _, _ = first
    no_lg = jnp.zeros((xs.shape[0], 128), BF16)
    parts0, router0 = weight_grad(at, xs, g_slots, [no_lg], [gp0], [act0])
    act1, gp1, lg1, dh_m, dh_o, ret_m, ret_o, *extras = expert_second(
        after(at, parts0), first, small, threes, 0, EARLY
    )
    dh_r = over_core(dh_o)
    dh_b = dh_m + dh_r
    dh_x = over_x(dh_b)
    ret_r = over_core(ret_o)
    def over_y(send, keep, *first):
        if not direct:
            return jnp.stack([keep, send], axis=1)
        got = over_wide(send, 1)
        return after(keep, *first) + after(got, *first)

    def over_z(both):
        return lax.all_to_all(both, "wide", 0, 0, axis_index_groups=z_groups, tiled=True)

    def expert_sum(both):
        both = both.reshape(8, -1, width)
        cut = 2 * part
        cols = jnp.moveaxis(both[:, :cut].reshape(8, 2, part, width), 1, 2).reshape(width, -1)
        rows = both[:, cut:].reshape(-1, width)
        return tuple(
            lax.psum_scatter(a, "wide", scatter_dimension=0, tiled=True) for a in (cols, rows)
        )

    def near_pair(a):
        return jnp.stack([a, over_core(a)])

    def near_experts(pairs):
        return jnp.concatenate([pairs, over_x(pairs)], axis=0)

    act2, gp2, lg2, late_m, late_o, late_ret_m, late_ret_o = expert_second(
        after(at, dh_b), first, small, threes, EARLY, len(BLOCKS) - EARLY, extras
    )
    late_r = over_core(late_o)
    late_ret_r = over_core(late_ret_o)
    if direct:
        sum0 = lax.all_to_all(parts0, "wide", 0, 0, tiled=True)
    ret_b = after(ret_m, act2) + ret_r
    parts1, router1 = weight_grad(
        after(at, ret_b), xs, g_slots, [lg1, lg2], [gp1, gp2], [act1, act2]
    )
    ret_x = over_x(after(ret_b, dh_x))

    grad_middle, low_m, *r_parts = middle_back(
        at,
        late_m,
        late_r,
        dh_x,
        middle,
        cots_m,
        vecs,
        att_m,
        mail_got,
        (router0, router1),
        filled,
    )
    low_o = over_core(low_m)
    hold = after(at, ret_x)
    if direct:
        sum1 = lax.all_to_all(after(parts1, dh_x, ret_b), "wide", 0, 0, tiled=True)
        sum0 = jnp.sum(after(sum0, low_m).astype(F32), axis=0).astype(BF16)
        pair0 = near_pair(sum0)
        near0 = near_experts(pair0)
        hold = after(hold, pair0)
    layer_mine, layer_send = layer_sum(middle, late_ret_m, late_ret_r, ret_x, quarter)
    layer_got = over_x(layer_send)
    dh1_m, dh1_o, grad_qkv = attend_back(
        after(hold, layer_send), low_m, low_o, proj_m, qkv, lse, bias, hidden_one, wq, head_dim
    )
    dh1_o = after(dh1_o, layer_got)
    if direct:
        dh1_o = after(dh1_o, near0)
    dh1_r = over_core(dh1_o)
    input_mine, input_send, q_send, q_keep = input_back(
        at, x_own, grad_middle, vecs, dh1_m, dh1_r, grad_qkv, r_parts, quarter
    )
    input_got = over_x(input_send)
    if direct:
        sum1 = jnp.sum(after(sum1, q_send).astype(F32), axis=0).astype(BF16)
        pair1 = near_pair(sum1)
        near1 = near_experts(pair1)
        got = after(over_wide(q_send, 1), pair1)
        last = q_send.shape[1] - 32
        q_both = jnp.concatenate(
            [q_keep[:, :last] + got[:, :last], q_keep[:, last:], got[:, last:]], axis=1
        )
    else:
        q_both = over_y(q_send, q_keep)
        sum0 = expert_sum(parts0)
        sum1 = expert_sum(parts1)

    def settle(mine, got):
        got = got.astype(mine.dtype)
        pair, rest = slice(0, 2), slice(2, 3)
        return jnp.where(
            chip == 0,
            jnp.concatenate([mine[pair], mine[rest], got[rest], got[pair]], axis=0),
            jnp.concatenate([got[pair], got[rest], mine[rest], mine[pair]], axis=0),
        )

    input_grad = settle(input_mine, after(input_got, q_both))
    if not direct:

        def in_order(a):
            four = near_experts(near_pair(a))
            return jnp.stack(
                [lax.dynamic_index_in_dim(four, place ^ e, 0, False) for e in range(E)]
            ).astype(F32)

        up0, up1, down0, down1 = (in_order(s[i]) for i in range(2) for s in (sum0, sum1))
        halves = [a.reshape(E, -1, n_wide, units) for a in (up0, up1)]
        grad_up = jnp.stack(halves, axis=3).reshape(E, -1, up.shape[1])
        grad_down = jnp.concatenate([down0, down1], axis=1)

    def over_seq_group(rows, lines):
        count = rows.shape[0]

        def sent(over, rows, lines):
            got = over(jnp.concatenate([rows.astype(BF16), *two_parts(lines)])).astype(F32)
            low = got[count : count + lines.shape[0]] + got[count + lines.shape[0] :]
            return got[:count], lines + low

        got, lines = sent(over_x, rows, lines)
        rows = rows + got
        other, lines = sent(over_core, rows, lines)
        return rows, other, lines

    owned = proj_weight.shape[0]
    if direct:
        rest = jnp.sum(over_z(q_both).astype(F32), axis=0)
        rows, lines = rest[:last], rest[last:].reshape(2, 2, 2, 8, width)
        lines = jnp.sum(lines, axis=(0, 2)).reshape(16, width)
    else:
        both = q_both.reshape(8, -1, width).astype(F32)
        last = both.shape[1] - 32
        rows = [both[:, :part], both[:, part : 2 * part]]
        halves = both[:, 2 * part : last].reshape(8, -1, 2, group)
        rows.append(jnp.moveaxis(halves, 2, 1).reshape(8, part, group))
        lines = jnp.sum(both[:, last:, :part].reshape(8, 2, 2, 8, part), axis=2)
        rows.append(jnp.moveaxis(lines.reshape(8, 16, part), 1, 2))
        rows = jnp.concatenate(rows, axis=2).reshape(width, -1)
        rows = lax.psum_scatter(rows, "wide", scatter_dimension=0, tiled=True)
        lines = jnp.pad(rows[:, -16:].T, ((0, 0), (0, width - owned)))
        more = rows[:, 2 * width : -16]
        more = jnp.concatenate([more[: owned // 2], more[owned // 2 :]], axis=1)
        rows = jnp.concatenate([rows[:, :width], rows[:, width : 2 * width], more])
    total, other, lines = over_seq_group(rows, lines)
    if direct:
        grad_up, grad_down = settle_experts(after(at, total), near0, near1)
    layer_out = settle(layer_mine, after(layer_got, total))
    grad_proj = total[:owned] + other[:owned]

    def thirds(a):
        more = a[2 * owned :]
        more = jnp.concatenate([more[:, :group], more[:, group:]])
        return [a[owned : 2 * owned, :group], a[owned : 2 * owned, group:], more]

    lines = lines[:, :owned]
    pairs = zip(thirds(total), thirds(other))
    ordered = [(jnp.where(core == 0, a, b), jnp.where(core == 0, b, a)) for a, b in pairs]
    grad_qkv = jnp.concatenate([a for pair in ordered for a in pair], axis=1)
    return (
        layer_out,
        input_grad,
        lines[8],
        lines[9],
        grad_qkv,
        grad_proj,
        lines[2],
        lines[3],
        lines[4 : 4 + E].T,
        grad_up,
        grad_down,
    )


def solution(mesh):
    placed = (
        P("wide", "seq", None),
        P("wide", None),
        P("wide", "seq", None),
        P("wide"),
        P("wide"),
        P("wide", None),
        P("wide", None),
        P("wide"),
        P("wide"),
        P("wide", None),
        P(None, "wide", None),
        P(None, "wide", None),
        P("wide", "seq", None),
    )
    return jax.shard_map(
        shards,
        mesh=mesh,
        in_specs=placed,
        out_specs=(
            P("wide", "seq", None),
            P("wide", "seq", None),
            P("wide"),
            P("wide"),
            P("wide", None),
            P("wide", None),
            P("wide"),
            P("wide"),
            P("wide", None),
            P(None, "wide", None),
            P(None, "wide", None),
        ),
        check_vma=False,
    )
```

time: 444 us -> 351 us (0.79); the launches traced: 437 us -> 349 us
  waiting for transfers between devices: 226 us -> 96.1 us
  Pallas kernels: 84.4 us -> 137 us
  starting transfers between devices: 16.4 us -> 45.2 us
  matrix products: 22.1 us -> 0 us
  local copies, waits for them, and re-layouts: 42.8 us -> 28.9 us
  blocking collectives: 7.79 us -> 0 us
    reduce_scatter x3 -> x0, waiting for transfers between devices: 96.8 us -> none  [over_wide(): return lax.psum_scatter(a, 'wide', scatter_dimension=dim, tiled=True)]
    pallas_call x5 -> x11, Pallas kernels: 61 us -> 114 us  [the longest x2 26.9 us: expert_second(): pl.pallas_call(functools.partial(expert_second_kernel, 2, count), grid=(c...]
    all_gather x3 -> x2, waiting for transfers between devices: 44.4 us -> 4.35 us  [shards(): lax.all_gather(after(half_of(up, down, half), ones, x_oth), 'wide')]
    all_to_all x0 -> x4, starting transfers between devices: none -> 31 us  [the longest x1 14.3 us: shards(): sum1 = lax.all_to_all(after(parts1, dh_x, ret_b), 'wide', 0, 0, tiled=True)]
    dot_general x4 -> x0, matrix products: 22.1 us -> none  [dot(): return lax.dot_general(a, b, (dims, ((), ())), preferred_element_type=F32)]
    all_to_all x0 -> x4, waiting for transfers between devices: none -> 21.4 us  [the longest x1 14.3 us: shards(): ones = lax.all_to_all(one_all, 'wide', 0, 0, tiled=True)]
    ppermute x23 -> x25, waiting for transfers between devices: 84.5 us -> 70.3 us  [the longest x24 56.8 us: over_seq(): return lax.ppermute(a, 'seq', [(i, i ^ turn) for i in range(n_seq)])]
    all_gather x1 -> x0, blocking collectives: 7.79 us -> none  [shards(): ids = lax.all_gather(expert_ids, 'seq', axis=1)]
  transfers between devices with their start and end apart: 29 -> 31, of which waited for: 12 -> 15; matrix products, arithmetic and copies ran while one was open for 13% -> 11% of each run, Pallas kernels for 10% -> 39%
where the time goes in v2:
time: 351 us; the launch traced here: 349 us
  Pallas kernels  137 us (39%)
  waiting for transfers between devices  96.1 us (27%)
  starting transfers between devices  45.2 us (13%)
  local copies, waits for them, and re-layouts  28.9 us (8%)
  other arithmetic  26.2 us (7%)
  between operations  15.4 us (4%)
    ppermute x24, waiting for transfers between devices, over_seq(): return lax.ppermute(a, 'seq', [(i, i ^ turn) for i in range(n_seq)])  56.8 us
    pallas_call x2, Pallas kernels, expert_second(): pl.pallas_call(functools.partial(expert_second_kernel, 2, count), grid=(c...  26.9 us
    pallas_call x1, Pallas kernels, attend_back(): pl.pallas_call(functools.partial(attend_back_kernel, head_dim), grid=(ima...  23.7 us
    pallas_call x1, Pallas kernels, expert_first(): pl.pallas_call(functools.partial(expert_first_kernel, 2, filled), grid=(c...  23 us
    pallas_call x2, Pallas kernels, weight_grad(): pl.pallas_call(functools.partial(weight_grad_kernel, tuple(ends)), grid=(...  22.4 us
    pallas_call x1, Pallas kernels, attend(): pl.pallas_call(functools.partial(attend_kernel, images, head_dim), grid=(...  15.5 us
    all_to_all x1, starting transfers between devices, shards(): sum1 = lax.all_to_all(after(parts1, dh_x, ret_b), 'wide', 0, 0, tiled=True)  14.3 us
    all_to_all x1, waiting for transfers between devices, shards(): ones = lax.all_to_all(one_all, 'wide', 0, 0, tiled=True)  14.3 us
  transfers between devices with their start and end apart: 31, of which 15 were waited for; matrix products, arithmetic and copies ran while one was open for 11% of the time, Pallas kernels for 39%

profile of v2, /device:TPU:0, one launch (start us, length us, event | category | flops | bytes accessed | tf_op | source)
XLA Modules:
  0.0 349.2 jit_solution(9082081035875215218)
XLA Ops:
  10.2 7.4 %all-to-all-start = ((bf16[8,80,1024]{2,1,0:T(8,128)(2,1)}), bf16[8,80,1024]{2,1,0:T(8,128)(2,1)}, u32[]{:S(2)}, u32[]{:S(2)}) async-start(bf16[8,80,1024]{2,1,0:T(8,128)(2,1)} %broadcast_in_dim.21), calls=%async_computation | async-start | bytes 2621440 | tf_op jit(solution)/shard_map/all_to_all | solution.py:984
  24.5 6.5 %collective-permute-done = bf16[3,145,512]{2,1,0:T(8,128)(2,1)} collective-permute-done((bf16[3,145,512]{2,1,0:T(8,128)(2,1)}, bf16[3,145,512]{2,1,0:T(8,128)(2,1)}, u32[]{:S(2)}, u32[]{:S(2)}) %collective-permute-start) | collective-permute-done | bytes 445472 | tf_op jit(solution)/shard_map/ppermute | solution.py:904
  34.7 14.3 %all-to-all-done.parts_ref = bf16[8,80,1024]{2,1,0:T(8,128)(2,1)} async-done(((bf16[8,80,1024]{2,1,0:T(8,128)(2,1)}), bf16[8,80,1024]{2,1,0:T(8,128)(2,1)}, u32[]{:S(2)}, u32[]{:S(2)}) %all-to-all-start) | async-done | bytes 1310752 | tf_op jit(solution)/shard_map/all_to_all | solution.py:984
  51.0 15.5 %attend.1 = (bf16[3,304,256]{2,1,0:T(8,128)(2,1)S(1)}, bf16[1424,256]{1,0:T(8,128)(2,1)S(1)}, bf16[3,608,768]{2,1,0:T(8,128)(2,1)}, bf16[3,608,512]{2,1,0:T(8,12...) custom-call(s32[4]{0:T(128)S(1)} %pad_add_fusion.at_ref.refs_0_, ...), custom_call_target="tpu_custom_call" | custom-call | flops 1000 | bytes 1000 | tf_op jit(solution)/shard_map/attend/pallas_call | solution.py:135
  69.7 4.4 %project.1 = (f32[3,304,512]{2,1,0:T(8,128)}, bf16[3,304,512]{2,1,0:T(8,128)(2,1)S(1)}, bf16[256,512]{1,0:T(8,128)(2,1)}) custom-call(s32[4]{0:T(128)S(1)} %pad_add_fusion.at_ref.refs_0_, bf16[3,304,256]{2,1,0:T(8,128)(2,1)} %copy-done.2, bf16[1424,256]{1,0:T(8,128)(2,1)} %copy-done.7, bf16[1424,256]{1,0:T(8,128)(2,1)} %copy-done.18, ...), custom_call_target="tpu_custom_call" | custom-call | flops 1000 | bytes 1000 | tf_op jit(solution)/shard_map/project/pallas_call | solution.py:199
  79.1 22.3 %collective-permute-done.3.h1 = bf16[3,304,512]{2,1,0:T(8,128)(2,1)S(1)} collective-permute-done((bf16[3,304,512]{2,1,0:T(8,128)(2,1)S(1)}, bf16[3,304,512]{2,1,0:T(8,128)(2,1)S(1)}, u32[]{:S(2)}, u32[]{:S(2)}) %collective-permute-start.3) | collective-permute-done | bytes 933920 | tf_op jit(solution)/shard_map/ppermute | solution.py:904
  104.1 23.0 %expert_first.1 = (f32[48,304]{1,0:T(8,128)}, bf16[1824,512]{1,0:T(8,128)(2,1)}, bf16[1824,512]{1,0:T(8,128)(2,1)}, bf16[1824,512]{1,0:T(8,128)(2,1)}, bf16[1824...) custom-call(s32[4]{0:T(128)S(1)} %pad_add_fusion.at_ref.refs_0_, ...), custom_call_target="tpu_custom_call" | custom-call | flops 1000 | bytes 1000 | tf_op jit(solution)/shard_map/expert_first/pallas_call | solution.py:389
  127.9 11.2 %weight_grad.2 = (bf16[8,256,512]{2,1,0:T(8,128)(2,1)}, f32[512,128]{1,0:T(8,128)}) custom-call(s32[4]{0:T(128)S(1)} %pad_add_fusion.at_ref.refs_0_, bf16[1824,512]{1,0:T(8,128)(2,1)} %get-tuple-element.99.refs_1_.xs_ref, bf16[1824,512]{1,0:T(8,128)(2,1)} %get-tuple-element.100.refs_2_.g_ref, bf16[1824,128]{1,0:T(8,128)(2,1)} %broadcast_in_dim.25.refs_3_, ...), custom_call_target="tpu_custom_call" | custom-call | flops 1000 | bytes 1000 | tf_op jit(solution)/shard_map/weight_grad/pallas_call | solution.py:552
  139.2 4.5 %all-to-all-start.1 = ((bf16[8,256,512]{2,1,0:T(8,128)(2,1)}), bf16[8,256,512]{2,1,0:T(8,128)(2,1)}, u32[]{:S(2)}, u32[]{:S(2)}) async-start(bf16[8,256,512]{2,1,0:T(8,128)(2,1)} %get-tuple-element.103), calls=%async_computation.1 | async-start | bytes 4194304 | tf_op jit(solution)/shard_map/all_to_all | solution.py:1055
  143.7 4.4 %all-gather.7.cloned.1.call-done = bf16[2048,512]{1,0:T(8,128)(2,1)} async-done(((bf16[256,512]{1,0:T(8,128)(2,1)}), bf16[2048,512]{1,0:T(8,128)(2,1)}) %all-gather.7.cloned.1.call-update) | async-done | bytes 2097168 | tf_op jit(solution)/shard_map/all_gather | solution.py:986
  148.0 16.3 %expert_second.2 = (bf16[1216,1024]{1,0:T(8,128)(2,1)}, bf16[1216,1024]{1,0:T(8,128)(2,1)}, bf16[1216,128]{1,0:T(8,128)(2,1)}, bf16[3,304,512]{2,1,0:T(8,128)(2,...) custom-call(s32[4]{0:T(128)S(1)} %pad_add_fusion.at_ref.refs_0_, ...), custom_call_target="tpu_custom_call" | custom-call | flops 1000 | bytes 1000 | tf_op jit(solution)/shard_map/expert_second/pallas_call | solution.py:473
  168.9 10.6 %expert_second.3 = (bf16[608,1024]{1,0:T(8,128)(2,1)}, bf16[608,1024]{1,0:T(8,128)(2,1)}, bf16[608,128]{1,0:T(8,128)(2,1)}, bf16[3,304,512]{2,1,0:T(8,128)(2,1)S...) custom-call(s32[4]{0:T(128)S(1)} %pad_add_fusion.at_ref.refs_0_, ...), custom_call_target="tpu_custom_call" | custom-call | flops 1000 | bytes 1000 | tf_op jit(solution)/shard_map/expert_second/pallas_call | solution.py:473
  182.6 11.2 %weight_grad.3 = (bf16[8,256,512]{2,1,0:T(8,128)(2,1)}, f32[512,128]{1,0:T(8,128)}) custom-call(s32[4]{0:T(128)S(1)} %pad_add_fusion.at_ref.refs_0_, bf16[1824,512]{1,0:T(8,128)(2,1)} %get-tuple-element.99.refs_1_.xs_ref, bf16[1824,512]{1,0:T(8,128)(2,1)} %get-tuple-element.100.refs_2_.g_ref, bf16[1216,128]{1,0:T(8,128)(2,1)} %get-tuple-element.128.refs_3_, ...), custom_call_target="tpu_custom_call" | custom-call | flops 1000 | bytes 1000 | tf_op jit(solution)/shard_map/weight_grad/pallas_call | solution.py:552
  193.9 14.3 %all-to-all-start.2 = ((bf16[8,256,512]{2,1,0:T(8,128)(2,1)}), bf16[8,256,512]{2,1,0:T(8,128)(2,1)}, u32[]{:S(2)}, u32[]{:S(2)}) async-start(bf16[8,256,512]{2,1,0:T(8,128)(2,1)} %get-tuple-element.155), calls=%async_computation.2 | async-start | bytes 4194304 | tf_op jit(solution)/shard_map/all_to_all | solution.py:1078
  212.3 7.3 %middle_back.1 = (f32[3,304,512]{2,1,0:T(8,128)}, bf16[3,304,512]{2,1,0:T(8,128)(2,1)S(1)}, bf16[4,80,512]{2,1,0:T(8,128)(2,1)}, bf16[4,80,512]{2,1,0:T(8,128)(2,1)}) custom-call(s32[4]{0:T(128)S(1)} %pad_add_fusion.at_ref.refs_0_, bf16[3,304,512]{2,1,0:T(8,128)(2,1)} %copy-done.4, bf16[3,304,512]{2,1,0:T(8,128)(2,1)} %copy-done.40, ...), custom_call_target="tpu_custom_call" | custom-call | flops 1000 | bytes 1000 | tf_op jit(solution)/shard_map/middle_back/pallas_call | solution.py:659
  223.7 9.0 %collective-permute-done.12.xr_ref = bf16[3,304,512]{2,1,0:T(8,128)(2,1)} collective-permute-done((bf16[3,304,512]{2,1,0:T(8,128)(2,1)}, bf16[3,304,512]{2,1,0:T(8,128)(2,1)}, u32[]{:S(2)}, u32[]{:S(2)}) %collective-permute-start.12) | collective-permute-done | bytes 933920 | tf_op jit(solution)/shard_map/ppermute | solution.py:904
  232.7 3.2 layer_sum.1
  236.0 23.7 %attend_back.1 = (bf16[3,304,512]{2,1,0:T(8,128)(2,1)}, bf16[3,304,512]{2,1,0:T(8,128)(2,1)S(1)}, f32[512,768]{1,0:T(8,128)}) custom-call(s32[4]{0:T(128)S(1)} %pad_add_fusion.at_ref.refs_0_, bf16[3,304,512]{2,1,0:T(8,128)(2,1)} %copy-done.5, bf16[3,304,512]{2,1,0:T(8,128)(2,1)} %collective-permute-done.16.lo_ref, ...), custom_call_target="tpu_custom_call" | custom-call | flops 1000 | bytes 1000 | tf_op jit(solution)/shard_map/attend_back/pallas_call | solution.py:762
  264.2 6.1 %input_back.1 = (f32[3,145,512]{2,1,0:T(8,128)S(1)}, bf16[3,145,512]{2,1,0:T(8,128)(2,1)S(1)}, bf16[4,192,512]{2,1,0:T(8,128)(2,1)S(1)}, bf16[4,192,512]{2,1,0:T(8,128)(2,1)S(1)}) custom-call(s32[4]{0:T(128)S(1)} %pad_add_fusion.at_ref.refs_0_, bf16[3,304,512]{2,1,0:T(8,128)(2,1)} %copy-done.15, f32[3,304,512]{2,1,0:T(8,128)} %get-tuple-element.134.gm_ref, ...), custom_call_target="tpu_custom_call" | custom-call | flops 1000 | bytes 1000 | tf_op jit(solution)/shard_map/input_back/pallas_call | solution.py:856
  277.6 13.5 %collective-permute-done.19 = bf16[4,192,512]{2,1,0:T(8,128)(2,1)} collective-permute-done((bf16[4,192,512]{2,1,0:T(8,128)(2,1)S(1)}, bf16[4,192,512]{2,1,0:T(8,128)(2,1)}, u32[]{:S(2)}, u32[]{:S(2)}) %collective-permute-start.19) | collective-permute-done | bytes 786464 | tf_op jit(solution)/shard_map/ppermute | solution.py:913
  294.2 4.8 %all-to-all-start.3 = ((bf16[4,224,512]{2,1,0:T(8,128)(2,1)}), bf16[4,224,512]{2,1,0:T(8,128)(2,1)}, u32[]{:S(2)}, u32[]{:S(2)}) async-start(bf16[4,224,512]{2,1,0:T(8,128)(2,1)} %pad_maximum_fusion.4), calls=%async_computation.3 | async-start | bytes 1835008 | tf_op jit(solution)/shard_map/all_to_all | solution.py:1032
  304.1 8.6 %collective-permute-done.22 = bf16[3,145,512]{2,1,0:T(8,128)(2,1)S(1)} collective-permute-done((bf16[3,145,512]{2,1,0:T(8,128)(2,1)S(1)}, bf16[3,145,512]{2,1,0:T(8,128)(2,1)S(1)}, u32[]{:S(2)}, u32[]{:S(2)}) %collective-permute-start.22) | collective-permute-done | bytes 445472 | tf_op jit(solution)/shard_map/ppermute | solution.py:904
  314.4 7.1 %all-to-all-done.3 = bf16[4,224,512]{2,1,0:T(8,128)(2,1)} async-done(((bf16[4,224,512]{2,1,0:T(8,128)(2,1)}), bf16[4,224,512]{2,1,0:T(8,128)(2,1)}, u32[]{:S(2)}, u32[]{:S(2)}) %all-to-all-start.3) | async-done | bytes 917536 | tf_op jit(solution)/shard_map/all_to_all | solution.py:1032
  333.5 4.7 %settle_experts.1 = (f32[4,64,2048]{2,1,0:T(8,128)}, f32[4,256,512]{2,1,0:T(8,128)}) custom-call(s32[4]{0:T(128)S(1)} %pad_add_fusion.at_ref.refs_0_, bf16[4,256,512]{2,1,0:T(8,128)(2,1)} %pad_maximum_fusion.2.zero_ref, bf16[4,256,512]{2,1,0:T(8,128)(2,1)} %pad_maximum_fusion.3.one_ref), custom_call_target="tpu_custom_call" | custom-call | flops 1000 | bytes 1000 | tf_op jit(solution)/shard_map/settle_experts/pallas_call | solution.py:587
  (256 shorter events, 79.9 us)
Async XLA Ops:
  10.2 38.9 %all-to-all-start = ((bf16[8,80,1024]{2,1,0:T(8,128)(2,1)}), bf16[8,80,1024]{2,1,0:T(8,128)(2,1)}, u32[]{:S(2)}, u32[]{:S(2)}) async-start(bf16[8,80,1024]{2,1,0:T(8,128)(2,1)} %broadcast_in_dim.21), calls=%async_computation | async-start | bytes 2621440 | tf_op jit(solution)/shard_map/all_to_all | solution.py:984
  17.6 86.5 %all-gather.5.cloned.1.call-start = ((), (), s32[]{:S(2)}) async-start(), calls=%async_computation.4 | async-start | bytes 2359296 | tf_op jit(solution)/shard_map/all_gather | solution.py:986
  18.5 12.5 %collective-permute-start = (bf16[3,145,512]{2,1,0:T(8,128)(2,1)}, bf16[3,145,512]{2,1,0:T(8,128)(2,1)}, u32[]{:S(2)}, u32[]{:S(2)}) collective-permute-start(bf16[3,145,512]{2,1,0:T(8,128)(2,1)} %pad_maximum_fusion.7), channel_id=1, source_target_pairs={{0,2},{1,3},{2,0},{3,1},{4,6},{5,7},{6,4},{7,5},{8,10},{9,11},{10,... | collective-permute-start | bytes 1336328 | tf_op jit(solution)/shard_map/ppermute | solution.py:904
  49.1 98.9 %all-gather.7.cloned.1.call-start = ((), (), s32[]{:S(2)}) async-start(), calls=%async_computation.5 | async-start | bytes 2359296 | tf_op jit(solution)/shard_map/all_gather | solution.py:986
  49.3 24.8 %collective-permute-start.6 = (bf16[6,146,512]{2,1,0:T(8,128)(2,1)}, bf16[6,146,512]{2,1,0:T(8,128)(2,1)}, u32[]{:S(2)}, u32[]{:S(2)}) collective-permute-start(bf16[6,146,512]{2,1,0:T(8,128)(2,1)} %pad_maximum_fusion), channel_id=1, source_target_pairs={{0,2},{1,3},{2,0},{3,1},{4,6},{5,7},{6,4},{7,5},{8,10},{9,11},{10,... | collective-permute-start | bytes 2691080 | tf_op jit(solution)/shard_map/ppermute | solution.py:904
  78.2 23.2 %collective-permute-start.7 = (bf16[2,3,304,512]{3,2,1,0:T(8,128)(2,1)S(1)}, bf16[2,3,304,512]{3,2,1,0:T(8,128)(2,1)S(1)}, u32[]{:S(2)}, u32[]{:S(2)}) collective-permute-start(bf16[2,3,304,512]{3,2,1,0:T(8,128)(2,1)S(1)} %pad_maximum_fusion.1.cm.cot_ref), channel_id=1, source_target_pairs={{0,1},{1,0},{2,3},{3,2},{4,5},{5,4},{6,7},{7,6},{8,9},{9,8},{10,11... | collective-permute-start | bytes 5603336 | tf_op jit(solution)/shard_map/ppermute | solution.py:904
  78.5 22.9 %collective-permute-start.3 = (bf16[3,304,512]{2,1,0:T(8,128)(2,1)S(1)}, bf16[3,304,512]{2,1,0:T(8,128)(2,1)S(1)}, u32[]{:S(2)}, u32[]{:S(2)}) collective-permute-start(bf16[3,304,512]{2,1,0:T(8,128)(2,1)S(1)} %get-tuple-element.94.h0), channel_id=1, source_target_pairs={{0,2},{1,3},{2,0},{3,1},{4,6},{5,7},{6,4},{7,5},{8,10},{9,11},{10,... | collective-permute-start | bytes 2801672 | tf_op jit(solution)/shard_map/ppermute | solution.py:904
  79.1 22.3 %collective-permute-start.4 = (bf16[3,304,512]{2,1,0:T(8,128)(2,1)S(1)}, bf16[3,304,512]{2,1,0:T(8,128)(2,1)S(1)}, u32[]{:S(2)}, u32[]{:S(2)}) collective-permute-start(bf16[3,304,512]{2,1,0:T(8,128)(2,1)S(1)} %get-tuple-element.94.h0), channel_id=1, source_target_pairs={{0,1},{1,0},{2,3},{3,2},{4,5},{5,4},{6,7},{7,6},{8,9},{9,8},{10,11... | collective-permute-start | bytes 2801672 | tf_op jit(solution)/shard_map/ppermute | solution.py:904
  139.2 54.7 %all-to-all-start.1 = ((bf16[8,256,512]{2,1,0:T(8,128)(2,1)}), bf16[8,256,512]{2,1,0:T(8,128)(2,1)}, u32[]{:S(2)}, u32[]{:S(2)}) async-start(bf16[8,256,512]{2,1,0:T(8,128)(2,1)} %get-tuple-element.103), calls=%async_computation.1 | async-start | bytes 4194304 | tf_op jit(solution)/shard_map/all_to_all | solution.py:1055
  164.4 16.9 %collective-permute-start.10 = (bf16[3,304,512]{2,1,0:T(8,128)(2,1)S(1)}, bf16[3,304,512]{2,1,0:T(8,128)(2,1)S(1)}, u32[]{:S(2)}, u32[]{:S(2)}) collective-permute-start(bf16[3,304,512]{2,1,0:T(8,128)(2,1)S(1)} %get-tuple-element.120), channel_id=1, source_target_pairs={{0,1},{1,0},{2,3},{3,2},{4,5},{5,4},{6,7},{7,6},{8,9},{9,8},{10,11... | collective-permute-start | bytes 2801672 | tf_op jit(solution)/shard_map/ppermute | solution.py:904
  167.2 26.7 %collective-permute-start.11 = (bf16[3,304,512]{2,1,0:T(8,128)(2,1)S(1)}, bf16[3,304,512]{2,1,0:T(8,128)(2,1)}, u32[]{:S(2)}, u32[]{:S(2)}) collective-permute-start(bf16[3,304,512]{2,1,0:T(8,128)(2,1)S(1)} %add.196), channel_id=1, source_target_pairs={{0,2},{1,3},{2,0},{3,1},{4,6},{5,7},{6,4},{7,5},{8,10},{9,11},{10,... | collective-permute-start | bytes 2801672 | tf_op jit(solution)/shard_map/ppermute | solution.py:904
  193.9 79.3 %all-to-all-start.2 = ((bf16[8,256,512]{2,1,0:T(8,128)(2,1)}), bf16[8,256,512]{2,1,0:T(8,128)(2,1)}, u32[]{:S(2)}, u32[]{:S(2)}) async-start(bf16[8,256,512]{2,1,0:T(8,128)(2,1)} %get-tuple-element.155), calls=%async_computation.2 | async-start | bytes 4194304 | tf_op jit(solution)/shard_map/all_to_all | solution.py:1078
  208.2 3.1 collective-permute-start.14
  208.3 15.4 %collective-permute-start.9 = (bf16[3,304,512]{2,1,0:T(8,128)(2,1)S(1)}, bf16[3,304,512]{2,1,0:T(8,128)(2,1)}, u32[]{:S(2)}, u32[]{:S(2)}) collective-permute-start(bf16[3,304,512]{2,1,0:T(8,128)(2,1)S(1)} %get-tuple-element.116), channel_id=1, source_target_pairs={{0,1},{1,0},{2,3},{3,2},{4,5},{5,4},{6,7},{7,6},{8,9},{9,8},{10,11... | collective-permute-start | bytes 2801672 | tf_op jit(solution)/shard_map/ppermute | solution.py:904
  208.8 23.9 %collective-permute-start.12 = (bf16[3,304,512]{2,1,0:T(8,128)(2,1)}, bf16[3,304,512]{2,1,0:T(8,128)(2,1)}, u32[]{:S(2)}, u32[]{:S(2)}) collective-permute-start(bf16[3,304,512]{2,1,0:T(8,128)(2,1)} %add.197), channel_id=1, source_target_pairs={{0,2},{1,3},{2,0},{3,1},{4,6},{5,7},{6,4},{7,5},{8,10},{9,11},{10,... | collective-permute-start | bytes 2801672 | tf_op jit(solution)/shard_map/ppermute | solution.py:904
  219.6 16.3 %collective-permute-start.16 = (bf16[3,304,512]{2,1,0:T(8,128)(2,1)S(1)}, bf16[3,304,512]{2,1,0:T(8,128)(2,1)}, u32[]{:S(2)}, u32[]{:S(2)}) collective-permute-start(bf16[3,304,512]{2,1,0:T(8,128)(2,1)S(1)} %get-tuple-element.136.lm_ref), channel_id=1, source_target_pairs={{0,1},{1,0},{2,3},{3,2},{4,5},{5,4},{6,7},{7,6},{8,9},{9,8},{10,11... | collective-permute-start | bytes 2801672 | tf_op jit(solution)/shard_map/ppermute | solution.py:904
  223.6 36.1 %collective-permute-start.17 = (bf16[2,256,512]{2,1,0:T(8,128)(2,1)S(1)}, bf16[2,256,512]{2,1,0:T(8,128)(2,1)S(1)}, u32[]{:S(2)}, u32[]{:S(2)}) collective-permute-start(bf16[2,256,512]{2,1,0:T(8,128)(2,1)S(1)} %pad_maximum_fusion.5), channel_id=1, source_target_pairs={{0,2},{1,3},{2,0},{3,1},{4,6},{5,7},{6,4},{7,5},{8,10},{9,11},{10,... | collective-permute-start | bytes 1572872 | tf_op jit(solution)/shard_map/ppermute | solution.py:904
  235.9 23.8 %collective-permute-start.13 = (bf16[3,145,512]{2,1,0:T(8,128)(2,1)S(1)}, bf16[3,145,512]{2,1,0:T(8,128)(2,1)S(1)}, u32[]{:S(2)}, u32[]{:S(2)}) collective-permute-start(bf16[3,145,512]{2,1,0:T(8,128)(2,1)S(1)} %get-tuple-element.123), channel_id=1, source_target_pairs={{0,2},{1,3},{2,0},{3,1},{4,6},{5,7},{6,4},{7,5},{8,10},{9,11},{10,... | collective-permute-start | bytes 1336328 | tf_op jit(solution)/shard_map/ppermute | solution.py:904
  271.1 20.0 %collective-permute-start.19 = (bf16[4,192,512]{2,1,0:T(8,128)(2,1)S(1)}, bf16[4,192,512]{2,1,0:T(8,128)(2,1)}, u32[]{:S(2)}, u32[]{:S(2)}) collective-permute-start(bf16[4,192,512]{2,1,0:T(8,128)(2,1)S(1)} %get-tuple-element.153), channel_id=1, source_target_pairs={{0,4},{4,0},{8,12},{12,8},{16,20},{20,16},{24,28},{28,24},{1,5},{5... | collective-permute-start | bytes 2359304 | tf_op jit(solution)/shard_map/ppermute | solution.py:913
  294.2 27.3 %all-to-all-start.3 = ((bf16[4,224,512]{2,1,0:T(8,128)(2,1)}), bf16[4,224,512]{2,1,0:T(8,128)(2,1)}, u32[]{:S(2)}, u32[]{:S(2)}) async-start(bf16[4,224,512]{2,1,0:T(8,128)(2,1)} %pad_maximum_fusion.4), calls=%async_computation.3 | async-start | bytes 1835008 | tf_op jit(solution)/shard_map/all_to_all | solution.py:1032
  299.0 13.6 %collective-permute-start.22 = (bf16[3,145,512]{2,1,0:T(8,128)(2,1)S(1)}, bf16[3,145,512]{2,1,0:T(8,128)(2,1)S(1)}, u32[]{:S(2)}, u32[]{:S(2)}) collective-permute-start(bf16[3,145,512]{2,1,0:T(8,128)(2,1)S(1)} %copy-done.13), channel_id=1, source_target_pairs={{0,2},{1,3},{2,0},{3,1},{4,6},{5,7},{6,4},{7,5},{8,10},{9,11},{10,... | collective-permute-start | bytes 1336328 | tf_op jit(solution)/shard_map/ppermute | solution.py:904
  304.0 27.1 %collective-permute-start.24 = (bf16[2,256,512]{2,1,0:T(8,128)(2,1)}, bf16[2,256,512]{2,1,0:T(8,128)(2,1)}, u32[]{:S(2)}, u32[]{:S(2)}) collective-permute-start(bf16[2,256,512]{2,1,0:T(8,128)(2,1)} %pad_maximum_fusion.6), channel_id=1, source_target_pairs={{0,2},{1,3},{2,0},{3,1},{4,6},{5,7},{6,4},{7,5},{8,10},{9,11},{10,... | collective-permute-start | bytes 1572872 | tf_op jit(solution)/shard_map/ppermute | solution.py:904
  326.1 7.1 %collective-permute-start.21 = (bf16[192,512]{1,0:T(8,128)(2,1)S(1)}, bf16[192,512]{1,0:T(8,128)(2,1)S(1)}, u32[]{:S(2)}, u32[]{:S(2)}) collective-permute-start(bf16[192,512]{1,0:T(8,128)(2,1)S(1)} %pad_maximum_fusion.10), channel_id=1, source_target_pairs={{0,2},{1,3},{2,0},{3,1},{4,6},{5,7},{6,4},{7,5},{8,10},{9,11},{10,... | collective-permute-start | bytes 589832 | tf_op jit(solution)/shard_map/ppermute | solution.py:904
  333.4 6.0 %collective-permute-start.23 = (bf16[192,512]{1,0:T(8,128)(2,1)S(1)}, bf16[192,512]{1,0:T(8,128)(2,1)S(1)}, u32[]{:S(2)}, u32[]{:S(2)}) collective-permute-start(bf16[192,512]{1,0:T(8,128)(2,1)S(1)} %pad_maximum_fusion.11), channel_id=1, source_target_pairs={{0,1},{1,0},{2,3},{3,2},{4,5},{5,4},{6,7},{7,6},{8,9},{9,8},{10,11... | collective-permute-start | bytes 589832 | tf_op jit(solution)/shard_map/ppermute | solution.py:904
  (60 other events, 363.3 us)
Sparse Core Ops, SparseCore 0:
  49.2 48.4 all-gather.4
  99.9 48.1 all-gather.6

commit v3 on v2

--- a/solution.py
+++ b/solution.py
@@ -73,7 +73,7 @@
 
 
 def attend_kernel(
-    images, head_dim, at_ref, own_ref, oth_ref, bias_ref, parts_ref,
+    images, head_dim, at_ref, own_ref, oth_ref, bias_ref, here_ref, there_ref,
     att_m_ref, mail_ref, qkv_ref, hidden_ref, lse_ref, wq_ref, small_ref, vec_ref,
 ):
     rows = own_ref.shape[1]
@@ -86,14 +86,15 @@
         row = lax.broadcasted_iota(jnp.int32, (part, features), 0)
         col = lax.broadcasted_iota(jnp.int32, (part, features), 1)
         for index in range(8):
-            base = index * part
-            wq_ref[base : base + part, :] = parts_ref[index, :part, : wq_ref.shape[1]]
-            there = slice(images * rows + base, images * rows + base + part)
-            mail_ref[there, :] = parts_ref[index, :part, wq_ref.shape[1] :]
+            side = at_ref[3] if index % 2 == 0 else 1 - at_ref[3]
+            ref = (here_ref, there_ref)[index % 2].at[index // 2]
+            base = pl.multiple_of((index // 2 * 2 + side) * part, part)
+            wq_ref[pl.ds(base, part), :] = ref[:part, : wq_ref.shape[1]]
+            mail_ref[pl.ds(images * rows + base, part), :] = ref[:part, wq_ref.shape[1] :]
             spread = (col == row + base).astype(F32).astype(BF16)
-            vec = vec + dot(parts_ref[index, part:, :part], spread)[:8]
+            vec = vec + dot(ref[part:, :part], spread)[:8]
         vec_ref[...] = vec
-        tall = jnp.concatenate([vec, vec[4:], jnp.zeros((116, features), F32)], axis=0)
+        tall = jnp.concatenate([vec, jnp.zeros((120, features), F32)], axis=0)
         small_ref[...] = tall.T.astype(BF16)
 
     gain, offset = vec_ref[0:1, :], vec_ref[1:2, :]
@@ -129,7 +130,7 @@
         mail_ref[pl.ds(pl.multiple_of(pl.program_id(0) * rows, 16), rows), cols] = out[rows:]
 
 
-def attend(at, x_own, x_oth, bias, parts, head_dim):
+def attend(at, x_own, x_oth, bias, here, there, head_dim):
     images, rows, width = x_own.shape
     group = width // 2
     return pl.pallas_call(
@@ -140,7 +141,8 @@
             per_image(rows, width),
             per_image(rows, width),
             per_image(2 * rows, 1),
-            whole(parts.shape),
+            whole(here.shape),
+            whole(there.shape),
         ],
         out_specs=[
             per_image(rows, group),
@@ -165,7 +167,7 @@
         compiler_params=params(40),
         cost_estimate=TINY,
         name="attend",
-    )(*placed(at, x_own, x_oth, bias, parts))
+    )(*placed(at, x_own, x_oth, bias, here, there))
 
 
 def project_kernel(
@@ -217,6 +219,45 @@
         cost_estimate=TINY,
         name="project",
     )(*placed(at, att_m, sent, got, x_own, vecs))
+
+
+def join_kernel(at_ref, cot_ref, got_ref, out_ref):
+    ours = pl.program_id(0) < pl.num_programs(0) // 2
+    first = jnp.where(ours, cot_ref[0], got_ref[0])
+    second = jnp.where(ours, got_ref[0], cot_ref[0])
+    count = first.shape[0] - 1
+    rows, width = out_ref.shape[1:]
+    codes = jnp.concatenate(
+        [first[count:, :count], second[count:, :count], jnp.zeros((1, width - 2 * count), BF16)],
+        axis=1,
+    )
+    fill = jnp.zeros((rows - 2 * count - 1, width), BF16)
+    out_ref[0] = jnp.concatenate([first[:count], second[:count], codes, fill], axis=0)
+
+
+def join_cots(at, cot, got, rows):
+    images, _, width = cot.shape
+    half = images // 2
+
+    def image(i, at):
+        chip = (at[2] // 2 + i // half) % 2
+        k = i % half
+        return (jnp.where(k < half - 1, chip * (images - 2) + k, half - 1 + chip), 0, 0)
+
+    one = pl.BlockSpec((1, *cot.shape[1:]), image)
+    return pl.pallas_call(
+        join_kernel,
+        grid_spec=pltpu.PrefetchScalarGridSpec(
+            num_scalar_prefetch=1,
+            grid=(images,),
+            in_specs=[one, one],
+            out_specs=pl.BlockSpec((1, rows, width), lambda i, at: (i, 0, 0)),
+        ),
+        out_shape=in_hbm((images, rows, width), BF16),
+        compiler_params=params(24),
+        cost_estimate=TINY,
+        name="join_cots",
+    )(*placed(at, cot, got))
 
 
 BLOCKS = (
@@ -275,15 +316,18 @@
     return ret, dx
 
 
-def routing(xs, wr_ref, mine):
-    logits = dot(xs, wr_ref[...])
+def routing(hidden, wr_ref):
+    logits = dot(hidden, wr_ref[...])
     lane = lax.broadcasted_iota(jnp.int32, (1, 128), 1)
-    logits = jnp.where((lane >= 4) & (lane < 4 + 2 * E), logits, BIG)
+    logits = jnp.where((lane >= 4) & (lane < 4 + E), logits, BIG)
     grown = jnp.exp(logits - jnp.max(logits, axis=-1, keepdims=True))
-    once = lane < 4 + E
-    router = grown / jnp.sum(jnp.where(once, grown, 0.0), axis=-1, keepdims=True)
-    sel = jnp.where((lane == 4 + mine) | (lane == 4 + E + mine), 1.0, 0.0)
-    return router, sel, jnp.sum(jnp.where(once, router * sel, 0.0), axis=-1, keepdims=True)
+    return grown / jnp.sum(grown, axis=-1, keepdims=True)
+
+
+def weight_of(hidden, wr_ref, mine):
+    lane = lax.broadcasted_iota(jnp.int32, (1, 128), 1)
+    router = jnp.where(lane == 4 + mine, routing(hidden, wr_ref), 0.0)
+    return jnp.sum(router, axis=-1, keepdims=True)
 
 
 def two_parts(values):
@@ -292,18 +336,25 @@
 
 
 def expert_first_kernel(
-    splits, filled, at_ref, h0, h1, h2, h3, cm, co, wr_ref, parts_ref,
-    pos_ref, xs_ref, cs_ref, g_ref, act_ref, gp_ref, ret_ref, dx_ref,
-    up_ref, down_ref, sem, piece_ref, piece_sem,
+    splits, filled, blocks, kinds, at_ref, wr_ref, parts_ref, *refs
 ):
     step = pl.program_id(0)
-    rows = h0.shape[1]
-    hs, cs = (h0, h1, h2, h3), (cm.at[0], cm.at[1], co.at[0], co.at[1])
+    hs = dict(zip(kinds, refs))
+    cots = refs[len(kinds) : len(kinds) + 2]
+    cs = {k: cots[k // 2].at[pl.ds(k % 2 * (cots[0].shape[0] // 2), cots[0].shape[0] // 2)] for k in kinds}
+    refs = refs[len(kinds) + 2 :]
+    *refs, up_ref, down_ref, sem, piece_ref, piece_sem, act_ref, gp_ref, gu_ref, gd_ref = refs
+    late = len(blocks) == EARLY
+    if late:
+        gu_in, gd_in, pos_ref, xs_ref, cs_ref, g_ref, ret_ref, dx_ref, out_ref = refs
+    else:
+        pos_ref, xs_ref, cs_ref, g_ref, ret_ref, dx_ref, gu_out, gd_out = refs
+    rows = xs_ref.shape[0]
     mine = at_ref[2]
 
     def pieces_of(number):
         copies = []
-        for k, (piece, image) in enumerate(BLOCKS[number]):
+        for k, (piece, image) in enumerate(blocks[number]):
             for j, kind in enumerate((hs, cs)):
                 spot = number * 4 + 2 * k + j
                 copies.append(
@@ -313,22 +364,31 @@
                 )
         return copies
 
+    def sum_copies():
+        return [
+            pltpu.make_async_copy(gu_in, gu_ref, sem.at[2]),
+            pltpu.make_async_copy(gd_in, gd_ref, sem.at[3]),
+        ]
+
     def copies():
         return load_weights(parts_ref, up_ref, down_ref, sem)
 
     @pl.when(step == 0)
     def _():
-        for number in range(len(BLOCKS)):
+        for number in range(len(blocks)):
             for copy in pieces_of(number):
                 copy.start()
             if number == 0:
                 for copy in copies():
                     copy.start()
+        if late:
+            for copy in sum_copies():
+                copy.start()
 
     token = lax.broadcasted_iota(jnp.int32, (1, rows), 1)
     slot = lax.broadcasted_iota(jnp.int32, (rows, rows), 0)
     before = (slot < lax.broadcasted_iota(jnp.int32, (rows, rows), 1)).astype(F32).astype(BF16)
-    for number, block in enumerate(BLOCKS):
+    for number, block in enumerate(blocks):
 
         @pl.when(step == number)
         def _(number=number, block=block):
@@ -355,7 +415,7 @@
             cs_ref[...] = got.astype(BF16)
 
     xs = xs_ref[...]
-    _, _, weight = routing(xs, wr_ref, mine)
+    weight = weight_of(xs, wr_ref, mine)
     g_ref[...] = (cs_ref[...].astype(F32) * weight).astype(BF16)
 
     @pl.when(step == 0)
@@ -366,52 +426,90 @@
     ret, dx = hidden_units(splits, xs, g_ref, up_ref, down_ref, act_ref, gp_ref)
     ret_ref[...] = ret.astype(BF16)
     dx_ref[...] = dx.astype(BF16)
+    gu, gd = dot_tn(xs, gp_ref[...]), dot_tn(g_ref[...], act_ref[...])
+
+    @pl.when(step == 0)
+    def _():
+        if late:
+            for copy in sum_copies():
+                copy.wait()
+            gu_ref[...] += gu
+            gd_ref[...] += gd
+        else:
+            gu_ref[...] = gu
+            gd_ref[...] = gd
+
+    @pl.when(step > 0)
+    def _():
+        gu_ref[...] += gu
+        gd_ref[...] += gd
+
+    if not late:
+
+        @pl.when(step == len(blocks) - 1)
+        def _():
+            gu_out[...] = gu_ref[...]
+            gd_out[...] = gd_ref[...]
+
+        return
+
+    @pl.when(step == len(blocks) - 1)
+    def _():
+        width, ff = gu_ref.shape
+        part, units = width // 8, ff // 8
+        for index in range(8):
+            own = gu_ref[index * part : (index + 1) * part, :].astype(BF16)
+            for block in range(ff // width):
+                into = slice(block * part, (block + 1) * part)
+                out_ref[index, into, :] = own[:, block * width : (block + 1) * width]
+            down = gd_ref[:, index * units : (index + 1) * units].T.astype(BF16)
+            out_ref[index, ff // width * part :, :] = down
 
 
 def slot_block(rows, cols, first=0):
     return pl.BlockSpec((rows, cols), lambda i: (i + first, 0))
 
 
-def expert_first(at, hidden, cots_m, cots_o, wr, parts, filled):
-    images, rows, width = hidden[0].shape
+def expert_first(at, hidden, cots, wr, parts, filled, start, count, sums=()):
+    _, rows, width = hidden[0].shape
     ff = (parts.shape[1] - 2 * width // 8) * 8
-    count = len(BLOCKS)
-    outs = [
-        (8, rows, F32),
-        (rows, width, BF16),
-        (rows, width, BF16),
-        (rows, width, BF16),
-        (rows, ff, BF16),
-        (rows, ff, BF16),
-        (rows, width, BF16),
-        (rows, width, BF16),
-    ]
+    blocks = BLOCKS[start : start + count]
+    kinds = tuple(sorted({piece for block in blocks for piece, _ in block}))
+    outs = [(8, rows, F32), *[(rows, width, BF16)] * 5]
+    anywhere = pl.BlockSpec(memory_space=pl.ANY)
+    if sums:
+        more_specs, more = [whole(parts.shape)], [in_hbm(parts.shape, BF16)]
+    else:
+        more_specs, more = [whole((width, ff))] * 2, [in_hbm((width, ff), F32)] * 2
     return pl.pallas_call(
-        functools.partial(expert_first_kernel, 2, filled),
+        functools.partial(expert_first_kernel, 2, filled, blocks, kinds),
         grid=(count,),
         in_specs=[
             SCALARS,
-            *[pl.BlockSpec(memory_space=pl.ANY)] * 6,
             whole(wr.shape),
-            pl.BlockSpec(memory_space=pl.ANY),
-        ],
-        out_specs=[slot_block(a, b) for a, b, _ in outs],
-        out_shape=[in_hbm((count * a, b), kind) for a, b, kind in outs],
+            *[anywhere] * (3 + len(kinds) + len(sums)),
+        ],
+        out_specs=[slot_block(a, b) for a, b, _ in outs] + more_specs,
+        out_shape=[in_hbm((count * a, b), kind) for a, b, kind in outs] + more,
         scratch_shapes=[
             pltpu.VMEM((width, ff), BF16),
             pltpu.VMEM((ff, width), BF16),
-            pltpu.SemaphoreType.DMA((2,)),
+            pltpu.SemaphoreType.DMA((4,)),
             pltpu.VMEM((4 * count, rows, width), BF16),
             pltpu.SemaphoreType.DMA((count,)),
-        ],
-        compiler_params=params(30),
+            pltpu.VMEM((rows, ff), BF16),
+            pltpu.VMEM((rows, ff), BF16),
+            pltpu.VMEM((width, ff), F32),
+            pltpu.VMEM((width, ff), F32),
+        ],
+        compiler_params=params(48),
         cost_estimate=TINY,
         name="expert_first",
-    )(*placed(at, *hidden, cots_m, cots_o, wr, parts))
+    )(*placed(at, wr, parts, *[hidden[k] for k in kinds], *cots, *sums))
 
 
 def expert_second_kernel(
-    splits, step_count, at_ref, pos_ref, xs_ref, cs_ref, g_ref, ret0_ref, dx0_ref, wr_ref,
+    splits, step_count, filled, at_ref, pos_ref, xs_ref, cs_ref, g_ref, ret0_ref, dx0_ref, wr_ref,
     parts_ref, *refs,
 ):
     step = pl.program_id(0)
@@ -419,7 +517,7 @@
     *refs, up_ref, down_ref, sem = refs
     early = step_count == EARLY
     if early:
-        act_ref, gp_ref, lg_ref, dh_m, dh_o, ret_m, ret_o, extra_m, extra_o = refs
+        act_ref, gp_ref, dh_m, dh_o, ret_m, ret_o, extra_m, extra_o = refs
         firsts = [((dh_m, ret_m), 0), ((dh_o, ret_o), 0)]
         targets = [[(dh, 0, back, 0), (dh, 1, back, 1)] for (dh, back), _ in firsts]
         targets += [
@@ -427,15 +525,8 @@
             for ((dh, back), _), extra in zip(firsts, (extra_m, extra_o))
         ]
     else:
-        extra_m, extra_o, act_ref, gp_ref, lg_ref, dh_m, dh_o, ret_m, ret_o = refs
+        act_ref, gp_ref, dh_m, dh_o, ret_m, ret_o = refs
         targets = [[(a, 0, b, 0), (a, 1, b, 1)] for a, b in ((dh_m, ret_m), (dh_o, ret_o))]
-
-        @pl.when(step == 0)
-        def _():
-            for extra, dh, back in ((extra_m, dh_m, ret_m), (extra_o, dh_o, ret_o)):
-                dh[2] = extra[0]
-                back[2] = extra[1]
-
 
     @pl.when(step == 0)
     def _():
@@ -447,12 +538,15 @@
 
     ret, dx = hidden_units(splits, xs_ref[...], g_ref, up_ref, down_ref, act_ref, gp_ref)
     ret = ret + ret0_ref[...].astype(F32)
-    router, sel, weight = routing(xs_ref[...], wr_ref, at_ref[2])
+    weight = weight_of(xs_ref[...], wr_ref, at_ref[2])
     gate = jnp.sum(cs_ref[...].astype(F32) * ret, axis=-1, keepdims=True)
-    high, low = two_parts(gate * weight * (sel - router))
-    lg = jnp.where(lax.broadcasted_iota(jnp.int32, (1, 128), 1) < 4 + E, high, low)
-    lg_ref[...] = lg
-    dxb = (dx + dx0_ref[...].astype(F32) + dot_nt(lg, wr_ref[...])).astype(BF16)
+    dxb = (dx + dx0_ref[...].astype(F32)).astype(BF16)
+    high, middle = two_parts(gate)
+    low = (gate - high.astype(F32) - middle.astype(F32)).astype(BF16)
+    lane = lax.broadcasted_iota(jnp.int32, (1, 128), 1) - filled % 16 - 3 * at_ref[2]
+    gates = jnp.where(lane == 0, high.astype(F32), 0.0)
+    gates = jnp.where(lane == 1, middle.astype(F32), gates)
+    gates = jnp.where(lane == 2, low.astype(F32), gates).astype(BF16)
     retb = (ret * weight).astype(BF16)
     slot = lax.broadcasted_iota(jnp.int32, (rows, rows), 0).astype(F32)
     picks = [(slot == pos_ref[k : k + 1, :]).astype(F32).astype(BF16) for k in range(2)]
@@ -461,36 +555,42 @@
         @pl.when(step == number)
         def _(target=target):
             for pick, (dh, i, back, j) in zip(picks, target):
-                dh[i] = dot_tn(pick, dxb).astype(BF16)
                 back[j] = dot_tn(pick, retb).astype(BF16)
-
-
-def expert_second(at, first, wr, parts, start, count, extras=()):
-    pos, xs, cs, g, _, _, ret, dx = first
-    rows, width = xs.shape[0] // len(BLOCKS), xs.shape[1]
+                out = dot_tn(pick, dxb)
+                dh[i] = out.astype(BF16)
+                tail = dot_tn(gates, pick)[:16]
+                tail = jnp.concatenate(
+                    [tail, jnp.zeros((16, out.shape[1] - rows), F32)], axis=1
+                )
+                start = filled // 16 * 16
+                dh[i, start : start + 16, :] = (out[start : start + 16] + tail).astype(BF16)
+
+
+def expert_second(at, first, wr, parts, filled):
+    pos, xs, cs, g, ret, dx = first
+    rows, width = pos.shape[1], xs.shape[1]
+    count = xs.shape[0] // rows
     ff = (parts.shape[1] - 2 * width // 8) * 8
-    sizes = (3, 3, 3, 3) if extras else (3, 3, 3, 3, 2, 2)
+    sizes = (3, 3, 3, 3, 2, 2) if count == EARLY else (2, 2, 2, 2)
     return pl.pallas_call(
-        functools.partial(expert_second_kernel, 2, count),
+        functools.partial(expert_second_kernel, 2, count, filled),
         grid=(count,),
         in_specs=[
             SCALARS,
-            slot_block(8, rows, start),
-            slot_block(rows, width, start),
-            slot_block(rows, width, start),
-            slot_block(rows, width, start),
-            slot_block(rows, width, start),
-            slot_block(rows, width, start),
+            slot_block(8, rows),
+            slot_block(rows, width),
+            slot_block(rows, width),
+            slot_block(rows, width),
+            slot_block(rows, width),
+            slot_block(rows, width),
             whole(wr.shape),
             pl.BlockSpec(memory_space=pl.ANY),
-            *[whole(e.shape) for e in extras],
-        ],
-        out_specs=[slot_block(rows, ff), slot_block(rows, ff), slot_block(rows, 128)]
+        ],
+        out_specs=[slot_block(rows, ff), slot_block(rows, ff)]
         + [whole((n, rows, width)) for n in sizes],
         out_shape=[
             in_hbm((count * rows, ff), BF16),
             in_hbm((count * rows, ff), BF16),
-            in_hbm((count * rows, 128), BF16),
         ]
         + [jax.ShapeDtypeStruct((n, rows, width), BF16) for n in sizes],
         scratch_shapes=[
@@ -501,14 +601,13 @@
         compiler_params=params(30),
         cost_estimate=TINY,
         name="expert_second",
-    )(*placed(at, pos, xs, cs, g, ret, dx, wr, parts, *extras))
+    )(*placed(at, pos, xs, cs, g, ret, dx, wr, parts))
 
 
 def weight_grad_kernel(ends, *refs):
     count = len(ends)
-    _, xs_ref, g_ref = refs[:3]
-    lgs, gps, acts = refs[3 : 3 + count], refs[3 + count : 3 + 2 * count], refs[3 + 2 * count : 3 + 3 * count]
-    out_ref, router_ref, xs_t, g_t, turned = refs[3 + 3 * count :]
+    xs, gs, gps, acts = (refs[i * count : (i + 1) * count] for i in range(4))
+    out_ref, xs_t, g_t, turned = refs[4 * count :]
     step = pl.program_id(0)
     width = xs_t.shape[0]
     part, cols = width // 8, gps[0].shape[1]
@@ -516,13 +615,9 @@
 
     @pl.when(step == 0)
     def _():
-        xs_t[...] = xs_ref[...].T
-        g_t[...] = g_ref[...].T
-        total = None
-        for (low, high), lg in zip(spans, lgs):
-            one = dot(xs_t[:, low:high], lg[...])
-            total = one if total is None else total + one
-        router_ref[...] = total
+        for (low, high), x_ref, g_ref in zip(spans, xs, gs):
+            xs_t[:, low:high] = x_ref[...].T
+            g_t[:, low:high] = g_ref[...].T
 
     up = down = None
     for (low, high), gp, act in zip(spans, gps, acts):
@@ -541,22 +636,21 @@
     out_ref[2 * step + 1, first:, :] = tall[half:]
 
 
-def weight_grad(at, xs, g, lgs, gps, acts):
-    slots, width = xs.shape
-    ff = gps[0].shape[1]
+def weight_grad(xs, g, gps, acts):
+    width, ff = xs[0].shape[1], gps[0].shape[1]
     cols = ff // 4
     out = (8, ff // width * (width // 8) + ff // 8, width)
     ends = []
     for gp in gps:
         ends.append(gp.shape[0] + (ends[-1] if ends else 0))
+    slots = ends[-1]
     return pl.pallas_call(
         functools.partial(weight_grad_kernel, tuple(ends)),
         grid=(4,),
-        in_specs=[SCALARS, whole(xs.shape), whole(g.shape)]
-        + [whole(a.shape) for a in lgs]
+        in_specs=[whole(a.shape) for a in (*xs, *g)]
         + [pl.BlockSpec((a.shape[0], cols), lambda i: (0, i)) for a in (*gps, *acts)],
-        out_specs=[whole(out), whole((width, 128))],
-        out_shape=[jax.ShapeDtypeStruct(out, BF16), in_hbm((width, 128), F32)],
+        out_specs=whole(out),
+        out_shape=in_hbm(out, BF16),
         scratch_shapes=[
             pltpu.VMEM((width, slots), BF16),
             pltpu.VMEM((width, slots), BF16),
@@ -565,7 +659,7 @@
         compiler_params=params(30),
         cost_estimate=TINY,
         name="weight_grad",
-    )(*placed(at, xs, g, *lgs, *gps, *acts))
+    )(*placed(*xs, *g, *gps, *acts))
 
 
 def settle_kernel(at_ref, zero_ref, one_ref, up_ref, down_ref):
@@ -605,10 +699,14 @@
     )(*placed(at, zero, one))
 
 
+def early_images(images, rows, width):
+    return pl.BlockSpec((1, rows, width), lambda i: (jnp.minimum(i, images - 2), 0, 0))
+
+
 def middle_back_kernel(
-    filled, at_ref, a_ref, ar_ref, xr_ref, mid_ref, cot_ref, vec_ref, am_ref,
-    got_ref, r0_ref, r1_ref,
-    gm_ref, low_ref, send_ref, keep_ref, sums_ref, proj_ref,
+    filled, at_ref, a_ref, ar_ref, b_ref, br_ref, xr_ref, mid_ref, cot_ref, vec_ref, am_ref,
+    got_ref, hidden_ref, wr_ref,
+    gm_ref, low_ref, parts_ref, sums_ref, proj_ref, router_ref,
 ):
     rows, width = mid_ref.shape[1:]
     group = am_ref.shape[2]
@@ -617,13 +715,29 @@
     def _():
         sums_ref[...] = jnp.zeros_like(sums_ref)
         proj_ref[...] = jnp.zeros_like(proj_ref)
-
-    grad = a_ref[0].astype(F32) + ar_ref[0].astype(F32) + xr_ref[0].astype(F32)
+        router_ref[...] = jnp.zeros_like(router_ref)
+
+    last = pl.program_id(0) == pl.num_programs(0) - 1
+    grad = jnp.where(
+        last,
+        b_ref[0].astype(F32) + br_ref[0].astype(F32),
+        a_ref[0].astype(F32) + ar_ref[0].astype(F32),
+    )
+    grad = grad + xr_ref[0].astype(F32)
+    gates = [grad[filled + 3 * e : filled + 3 * e + 3, :384] for e in range(E)]
+    gates = [jnp.sum(g, axis=0, keepdims=True) for g in gates]
+    gates = jnp.concatenate([jnp.zeros((4, 384), F32), *gates, jnp.zeros((120, 384), F32)], axis=0)
+    gates = gates.T[:rows]
+    router = routing(hidden_ref[0], wr_ref)
+    mean = jnp.sum(router * gates, axis=-1, keepdims=True)
+    logit_grad = (router * (gates - mean)).astype(BF16)
+    row = lax.broadcasted_iota(jnp.int32, (rows, 1), 0)
+    grad = jnp.where(row < filled, grad, 0.0) + dot_nt(logit_grad, wr_ref[...])
+    router_ref[...] += dot_tn(hidden_ref[0], logit_grad)
     xhat, rstd = norm_parts(mid_ref[0])
     sums_ref[2:3, :] += jnp.sum(grad * xhat, axis=0, keepdims=True)
     sums_ref[3:4, :] += jnp.sum(grad, axis=0, keepdims=True)
-    out = cot_ref[0, 0].astype(F32) + norm_back(grad * vec_ref[2:3, :], xhat, rstd)
-    row = lax.broadcasted_iota(jnp.int32, (rows, 1), 0)
+    out = cot_ref[0].astype(F32) + norm_back(grad * vec_ref[2:3, :], xhat, rstd)
     out = jnp.where(row < filled, out, 0.0)
     gm_ref[0] = out
     low = out.astype(BF16)
@@ -635,71 +749,81 @@
     @pl.when(pl.program_id(0) == pl.num_programs(0) - 1)
     def _():
         part = width // 8
-        router = (r0_ref[...] + r1_ref[...]).T
-        router = jnp.concatenate([jnp.zeros((4, width), F32), router[4:8] + router[8:12]], axis=0)
+        router = router_ref[...].T[:8]
         lines = jnp.concatenate(two_parts(sums_ref[...] + router), axis=0)
         row = lax.broadcasted_iota(jnp.int32, (width, 128), 0)
         col = lax.broadcasted_iota(jnp.int32, (width, 128), 1)
-        for ref, side in ((send_ref, 1 - at_ref[3]), (keep_ref, at_ref[3])):
-            for z in range(4):
-                base = (2 * z + side) * part
-                from_ = pl.multiple_of(base ^ (at_ref[1] * group), part)
-                ref[z, :part, :] = proj_ref[pl.ds(from_, part), :].astype(BF16)
-                pick = ((row == col + base) & (col < part)).astype(F32).astype(BF16)
-                ref[z, part:, :128] = dot(lines, pick).astype(BF16)
-                ref[z, part:, 128:] = jnp.zeros((16, width - 128), BF16)
-
-
-def middle_back(at, mine, near, from_x, middle, cots, vecs, att_m, got, routers, filled):
+        for index in range(8):
+            base = index * part
+            from_ = pl.multiple_of(base ^ (at_ref[1] * group), part)
+            parts_ref[index, :part, :] = proj_ref[pl.ds(from_, part), :].astype(BF16)
+            pick = ((row == col + base) & (col < part)).astype(F32).astype(BF16)
+            parts_ref[index, part:, :128] = dot(lines, pick).astype(BF16)
+            parts_ref[index, part:, 128:] = jnp.zeros((16, width - 128), BF16)
+
+
+def middle_back(at, mine, near, extra, extra_near, from_x, middle, cots, vecs, att_m, got, hidden, wr, filled):
     images, rows, width = middle.shape
     one = per_image(rows, width)
-    cot = pl.BlockSpec((1, 1, rows, width), lambda i: (0, i, 0, 0))
     group = att_m.shape[2]
-    piece = (4, width // 8 + 16, width)
+    piece = (8, width // 8 + 16, width)
     return pl.pallas_call(
         functools.partial(middle_back_kernel, filled),
         grid=(images,),
         in_specs=[SCALARS]
-        + [one] * 4
-        + [cot, whole(vecs.shape), per_image(rows, group), whole(got.shape)]
-        + [whole(routers[0].shape)] * 2,
-        out_specs=[one, one, whole(piece), whole(piece)],
+        + [early_images(images, rows, width)] * 2
+        + [pl.BlockSpec((1, rows, width), lambda i: (0, 0, 0))] * 2
+        + [one] * 2
+        + [one, whole(vecs.shape), per_image(rows, group), whole(got.shape)]
+        + [one, whole(wr.shape)],
+        out_specs=[one, one, whole(piece)],
         out_shape=[
             in_hbm(middle.shape, F32),
             jax.ShapeDtypeStruct(middle.shape, BF16),
             in_hbm(piece, BF16),
-            in_hbm(piece, BF16),
         ],
         scratch_shapes=[
             pltpu.VMEM((8, width), F32),
             pltpu.VMEM((width, width), F32),
+            pltpu.VMEM((width, 128), F32),
         ],
         compiler_params=params(32),
         cost_estimate=TINY,
         name="middle_back",
-    )(*placed(at, mine, near, from_x, middle, cots, vecs, att_m, got, *routers))
-
-
-def layer_kernel(mid_ref, a_ref, ar_ref, xr_ref, mine_ref, send_ref):
-    total = mid_ref[0] + a_ref[0].astype(F32) + ar_ref[0].astype(F32) + xr_ref[0].astype(F32)
+    )(*placed(at, mine, near, extra, extra_near, from_x, middle, cots, vecs, att_m, got, hidden, wr))
+
+
+def layer_kernel(mid_ref, a_ref, ar_ref, b_ref, br_ref, xr_ref, mine_ref, send_ref):
+    last = pl.program_id(0) == pl.num_programs(0) - 1
+    total = jnp.where(
+        last,
+        b_ref[0].astype(F32) + br_ref[0].astype(F32),
+        a_ref[0].astype(F32) + ar_ref[0].astype(F32),
+    )
+    total = total + mid_ref[0] + xr_ref[0].astype(F32)
     count = mine_ref.shape[1]
     mine_ref[0] = total[:count].astype(BF16)
     send_ref[0] = total[count : 2 * count].astype(BF16)
 
 
-def layer_sum(middle, mine, near, from_x, quarter):
+def layer_sum(middle, mine, near, extra, extra_near, from_x, quarter):
     images, rows, width = middle.shape
     one, part = per_image(rows, width), per_image(quarter, width)
     return pl.pallas_call(
         layer_kernel,
         grid=(images,),
-        in_specs=[one] * 4,
+        in_specs=[
+            one,
+            *[early_images(images, rows, width)] * 2,
+            *[pl.BlockSpec((1, rows, width), lambda i: (1, 0, 0))] * 2,
+            one,
+        ],
         out_specs=[part, part],
         out_shape=[jax.ShapeDtypeStruct((images, quarter, width), BF16)] * 2,
         compiler_params=params(24),
         cost_estimate=TINY,
         name="layer_sum",
-    )(*placed(middle, mine, near, from_x))
+    )(*placed(middle, mine, near, extra, extra_near, from_x))
 
 
 def attend_back_kernel(
@@ -794,7 +918,7 @@
 
 
 def input_back_kernel(
-    at_ref, x_ref, gm_ref, vec_ref, a_ref, ar_ref, gq_ref, r_send_ref, r_keep_ref,
+    at_ref, x_ref, gm_ref, vec_ref, a_ref, ar_ref, gq_ref,
     out_ref, go_ref, send_ref, keep_ref, sums_ref,
 ):
     step, images = pl.program_id(0), pl.num_programs(0)
@@ -828,11 +952,11 @@
             line = dot(lines, pick_line).astype(BF16)
             tail = jnp.concatenate([line, jnp.zeros((16, width - 128), BF16)], axis=1)
             block = jnp.concatenate([own[:, :width], half], axis=0)
-            last = part + block.shape[0]
+            last = block.shape[0]
 
             def put(ref, block=block, tail=tail, z=index // 2, last=last):
-                ref[z, part:last] = block
-                ref[z, last + 16 :] = tail
+                ref[z, :last] = block
+                ref[z, last:] = tail
 
             @pl.when(at_ref[3] == index % 2)
             def _(put=put):
@@ -842,22 +966,15 @@
             def _(put=put):
                 put(send_ref)
 
-        last = send_ref.shape[1] - 32
-        for ref, from_ in ((send_ref, r_send_ref), (keep_ref, r_keep_ref)):
-            ref[:, :part] = from_[:, :part]
-            ref[:, last : last + 16] = from_[:, part:]
-
-
-def input_back(at, x_own, grad_middle, vecs, mine, near, grads, r_parts, quarter):
+
+def input_back(at, x_own, grad_middle, vecs, mine, near, grads, quarter):
     images, rows, width = x_own.shape
     one, part = per_image(rows, width), per_image(quarter, width)
-    first = r_parts[0].shape[1]
-    more = (4, first + width // 8 + (grads.shape[1] - width) * (width // 8) // width + 16, width)
+    more = (4, width // 8 + (grads.shape[1] - width) * (width // 8) // width + 16, width)
     return pl.pallas_call(
         input_back_kernel,
         grid=(images,),
-        in_specs=[SCALARS, one, one, whole(vecs.shape), one, one, whole(grads.shape)]
-        + [whole(r.shape) for r in r_parts],
+        in_specs=[SCALARS, one, one, whole(vecs.shape), one, one, whole(grads.shape)],
         out_specs=[part, part, whole(more), whole(more)],
         out_shape=[
             jax.ShapeDtypeStruct((images, quarter, width), F32),
@@ -869,7 +986,7 @@
         compiler_params=params(32),
         cost_estimate=TINY,
         name="input_back",
-    )(*placed(at, x_own, grad_middle, vecs, mine, near, grads, *r_parts))
+    )(*placed(at, x_own, grad_middle, vecs, mine, near, grads))
 
 
 def shards(
@@ -892,7 +1009,7 @@
     head_dim = width // H
     group = width // 2
     filled = 2 * quarter
-    rows = -(-(filled + 1) // 16) * 16
+    rows = -(-(filled + 3 * E) // 16) * 16
     place = lax.axis_index("seq")
     chip, core = place // 2, place % 2
     direct = n_wide == 8
@@ -959,7 +1076,7 @@
         return jnp.concatenate([*blocks, down], axis=0)
 
     one_all = first_parts(wq, proj, lines)
-    one_all = jnp.broadcast_to(one_all[None], (8, *one_all.shape))
+    one_all = jnp.broadcast_to(one_all[None], (4, *one_all.shape))
     codes = (expert_ids[..., 0] * E + expert_ids[..., 1]).astype(BF16)
     codes = jnp.pad(codes, ((0, 0), (0, width - quarter)))[:, None, :]
     cot = jnp.concatenate([cotangent, codes], axis=1)
@@ -968,20 +1085,14 @@
     x_oth = over_core(after(x_own, bias, cot))
     cot_got = over_x(after(cot, x_got))
 
-    def cot_of(first, second):
-        code = jnp.concatenate(
-            [first[:, quarter:, :quarter], second[:, quarter:, :quarter]], axis=2
-        )
-        code = jnp.pad(code, ((0, 0), (0, rows - filled - 1), (0, width - filled)))
-        return jnp.concatenate([first[:, :quarter], second[:, :quarter], code], axis=1)
-
     z_groups = [[y + 2 * z for z in range(4)] for y in range(2)]
 
     def all_of(a, axis=0):
         return lax.all_gather(a, "wide", axis=axis, tiled=True)
 
     if direct:
-        ones = lax.all_to_all(one_all, "wide", 0, 0, tiled=True)
+        ones = lax.all_to_all(one_all, "wide", 0, 0, axis_index_groups=z_groups, tiled=True)
+        ones_y = over_wide(ones, 1)
         twos, threes = (
             lax.all_gather(after(half_of(up, down, half), ones, x_oth), "wide") for half in range(2)
         )
@@ -991,32 +1102,34 @@
             return jnp.split(a, 8, axis=axis)
 
         ones = jnp.stack([first_parts(*a) for a in zip(eight(all_of(wq)), eight(all_of(proj)), eight(all_of(lines, 1), 1))])
+        ones, ones_y = ones[::2], ones[1::2]
         ups, downs = eight(all_of(up)), eight(all_of(down))
         twos, threes = (
             jnp.stack([half_of(a, b, half) for a, b in zip(ups, downs)]) for half in range(2)
         )
 
     att_m, mail, qkv, hidden_one, lse, wq, small, vecs = attend(
-        at, x_own, x_oth, bias, ones, head_dim
+        at, x_own, x_oth, bias, ones, ones_y, head_dim
     )
     mail_got = over_core(mail)
     middle, hidden_two, proj_m = project(at, att_m, mail, mail_got, x_own, vecs)
     cot_got = after(cot_got, hidden_two)
-    cots_m = jnp.stack(
-        [
-            cot_of(images_of(cot, chip), images_of(cot_got, chip)),
-            cot_of(images_of(cot_got, 1 - chip), images_of(cot, 1 - chip)),
-        ]
-    )
+    cots_m = join_cots(at, cot, cot_got, rows)
     cots_o = over_core(cots_m)
+
     hidden_b = over_x(hidden_two)
-    hidden = (hidden_two, hidden_b, over_core(hidden_two), over_core(hidden_b))
-    first = expert_first(at, hidden, cots_m, cots_o, small, twos, filled)
-    _, xs, _, g_slots, act0, gp0, _, _ = first
-    no_lg = jnp.zeros((xs.shape[0], 128), BF16)
-    parts0, router0 = weight_grad(at, xs, g_slots, [no_lg], [gp0], [act0])
-    act1, gp1, lg1, dh_m, dh_o, ret_m, ret_o, *extras = expert_second(
-        after(at, parts0), first, small, threes, 0, EARLY
+    hidden_c = over_core(hidden_two)
+    ours = (hidden_two, None, hidden_c, None)
+    *first_a, gu_a, gd_a = expert_first(
+        at, ours, (cots_m, cots_o), small, twos, filled, EARLY, len(BLOCKS) - EARLY
+    )
+    hidden_d = over_core(after(hidden_b, gu_a))
+    hidden = (hidden_two, hidden_b, hidden_c, hidden_d)
+    *first_b, parts0 = expert_first(
+        at, hidden, (cots_m, cots_o), small, twos, filled, 0, EARLY, (gu_a, gd_a)
+    )
+    act1, gp1, dh_m, dh_o, ret_m, ret_o, extra_m, extra_o = expert_second(
+        after(at, parts0), first_b, small, threes, filled
     )
     dh_r = over_core(dh_o)
     dh_b = dh_m + dh_r
@@ -1046,59 +1159,59 @@
     def near_experts(pairs):
         return jnp.concatenate([pairs, over_x(pairs)], axis=0)
 
-    act2, gp2, lg2, late_m, late_o, late_ret_m, late_ret_o = expert_second(
-        after(at, dh_b), first, small, threes, EARLY, len(BLOCKS) - EARLY, extras
+    extra_r = over_core(extra_o)
+    act2, gp2, late_m, late_o, late_ret_m, late_ret_o = expert_second(
+        after(at, dh_b), first_a, small, threes, filled
     )
     late_r = over_core(late_o)
     late_ret_r = over_core(late_ret_o)
     if direct:
         sum0 = lax.all_to_all(parts0, "wide", 0, 0, tiled=True)
     ret_b = after(ret_m, act2) + ret_r
-    parts1, router1 = weight_grad(
-        after(at, ret_b), xs, g_slots, [lg1, lg2], [gp1, gp2], [act1, act2]
-    )
+    xs = (after(first_b[1], ret_b), first_a[1])
+    parts1 = weight_grad(xs, (first_b[3], first_a[3]), [gp1, gp2], [act1, act2])
     ret_x = over_x(after(ret_b, dh_x))
 
-    grad_middle, low_m, *r_parts = middle_back(
+    grad_middle, low_m, r_parts = middle_back(
         at,
         late_m,
         late_r,
+        extra_m,
+        extra_r,
         dh_x,
         middle,
         cots_m,
         vecs,
         att_m,
         mail_got,
-        (router0, router1),
+        hidden_two,
+        small,
         filled,
     )
     low_o = over_core(low_m)
-    hold = after(at, ret_x)
     if direct:
         sum1 = lax.all_to_all(after(parts1, dh_x, ret_b), "wide", 0, 0, tiled=True)
-        sum0 = jnp.sum(after(sum0, low_m).astype(F32), axis=0).astype(BF16)
-        pair0 = near_pair(sum0)
-        near0 = near_experts(pair0)
-        hold = after(hold, pair0)
-    layer_mine, layer_send = layer_sum(middle, late_ret_m, late_ret_r, ret_x, quarter)
-    layer_got = over_x(layer_send)
     dh1_m, dh1_o, grad_qkv = attend_back(
-        after(hold, layer_send), low_m, low_o, proj_m, qkv, lse, bias, hidden_one, wq, head_dim
-    )
-    dh1_o = after(dh1_o, layer_got)
-    if direct:
-        dh1_o = after(dh1_o, near0)
+        at, low_m, low_o, proj_m, qkv, lse, bias, hidden_one, wq, head_dim
+    )
+    dh1_o = after(dh1_o, ret_x)
     dh1_r = over_core(dh1_o)
     input_mine, input_send, q_send, q_keep = input_back(
-        at, x_own, grad_middle, vecs, dh1_m, dh1_r, grad_qkv, r_parts, quarter
+        at, x_own, grad_middle, vecs, dh1_m, dh1_r, grad_qkv, quarter
     )
     input_got = over_x(input_send)
+    layer_mine, layer_send = layer_sum(
+        middle, after(late_ret_m, q_send), late_ret_r, extra_m, extra_r, ret_x, quarter
+    )
+    layer_got = over_x(layer_send)
     if direct:
+        r_sum = lax.all_to_all(after(r_parts, q_send), "wide", 0, 0, tiled=True)
+        sum0 = jnp.sum(after(sum0, q_send).astype(F32), axis=0).astype(BF16)
         sum1 = jnp.sum(after(sum1, q_send).astype(F32), axis=0).astype(BF16)
-        pair1 = near_pair(sum1)
-        near1 = near_experts(pair1)
-        got = after(over_wide(q_send, 1), pair1)
-        last = q_send.shape[1] - 32
+        pair0, pair1 = near_pair(sum0), near_pair(sum1)
+        near0, near1 = near_experts(pair0), near_experts(pair1)
+        got = after(over_wide(q_send, 1), pair0, pair1, layer_send)
+        last = q_send.shape[1] - 16
         q_both = jnp.concatenate(
             [q_keep[:, :last] + got[:, :last], q_keep[:, last:], got[:, last:]], axis=1
         )
@@ -1145,17 +1258,20 @@
 
     owned = proj_weight.shape[0]
     if direct:
-        rest = jnp.sum(over_z(q_both).astype(F32), axis=0)
-        rows, lines = rest[:last], rest[last:].reshape(2, 2, 2, 8, width)
-        lines = jnp.sum(lines, axis=(0, 2)).reshape(16, width)
+        rest = jnp.sum(after(over_z(q_both), near0, near1).astype(F32), axis=0)
+        r_sum = jnp.sum(after(r_sum, q_both).astype(F32), axis=0)
+        rows = jnp.concatenate([r_sum[:part], rest[:last]])
+        lines = jnp.concatenate(
+            [r_sum[part : part + 8] + r_sum[part + 8 :], jnp.sum(rest[last:].reshape(4, 8, width), 0)]
+        )
     else:
-        both = q_both.reshape(8, -1, width).astype(F32)
-        last = both.shape[1] - 32
-        rows = [both[:, :part], both[:, part : 2 * part]]
-        halves = both[:, 2 * part : last].reshape(8, -1, 2, group)
+        q_all, r_all = q_both.reshape(8, -1, width).astype(F32), r_parts.astype(F32)
+        last = q_all.shape[1] - 16
+        rows = [r_all[:, :part], q_all[:, :part]]
+        halves = q_all[:, part:last].reshape(8, -1, 2, group)
         rows.append(jnp.moveaxis(halves, 2, 1).reshape(8, part, group))
-        lines = jnp.sum(both[:, last:, :part].reshape(8, 2, 2, 8, part), axis=2)
-        rows.append(jnp.moveaxis(lines.reshape(8, 16, part), 1, 2))
+        for a in (r_all[:, part:], q_all[:, last:]):
+            rows.append(jnp.moveaxis(a[:, :8, :part] + a[:, 8:, :part], 1, 2))
         rows = jnp.concatenate(rows, axis=2).reshape(width, -1)
         rows = lax.psum_scatter(rows, "wide", scatter_dimension=0, tiled=True)
         lines = jnp.pad(rows[:, -16:].T, ((0, 0), (0, width - owned)))
@@ -1164,8 +1280,8 @@
         rows = jnp.concatenate([rows[:, :width], rows[:, width : 2 * width], more])
     total, other, lines = over_seq_group(rows, lines)
     if direct:
-        grad_up, grad_down = settle_experts(after(at, total), near0, near1)
-    layer_out = settle(layer_mine, after(layer_got, total))
+        grad_up, grad_down = settle_experts(after(at, rows), near0, near1)
+    layer_out = settle(layer_mine, after(layer_got, rows))
     grad_proj = total[:owned] + other[:owned]
 
     def thirds(a):

time: 351 us -> 325 us (0.926)
  waiting for transfers between devices: 96.1 us -> 54.4 us
  Pallas kernels: 137 us -> 148 us
  local copies, waits for them, and re-layouts: 28.9 us -> 23.8 us
  other arithmetic: 26.2 us -> 30.7 us
    ppermute x24 -> x25, waiting for transfers between devices: 56.8 us -> 28.8 us  [over_seq(): return lax.ppermute(a, 'seq', [(i, i ^ turn) for i in range(n_seq)])]
    pallas_call x4 -> x6, Pallas kernels: 53.1 us -> 73.5 us  [the longest x2 38.1 us: expert_first(): pl.pallas_call(functools.partial(expert_first_kernel, 2, filled, blocks,...]
    all_to_all x1 -> x2, waiting for transfers between devices: 14.3 us -> 0.71 us  [the longest x1 0.71 us: shards(): lax.all_to_all(one_all, 'wide', 0, 0, axis_index_groups=z_groups, tiled=T...]
    pallas_call x2 -> x1, Pallas kernels: 22.4 us -> 11.2 us  [weight_grad(): pl.pallas_call(functools.partial(weight_grad_kernel, tuple(ends)), grid=(...]
    all_to_all x1, starting transfers between devices: 14.3 us -> 4.51 us  [shards(): sum1 = lax.all_to_all(after(parts1, dh_x, ret_b), 'wide', 0, 0, tiled=True)]
    all_to_all x1, waiting for transfers between devices: 7.08 us -> 0.01 us  [over_z(): lax.all_to_all(both, 'wide', 0, 0, axis_index_groups=z_groups, tiled=True)]
    ppermute x1 -> x2, waiting for transfers between devices: 13.5 us -> 19.8 us  [over_wide(): return lax.ppermute(a, 'wide', [(i, i ^ turn) for i in range(n_wide)])]
    all_to_all x1 -> x2, starting transfers between devices: 7.41 us -> 12.4 us  [the longest x1 6.45 us: shards(): lax.all_to_all(one_all, 'wide', 0, 0, axis_index_groups=z_groups, tiled=T...]
  transfers between devices with their start and end apart: 31 -> 34, of which waited for: 15 -> 17; matrix products, arithmetic and copies ran while one was open for 11% -> 13% of each run, Pallas kernels for 39% -> 46%
where the time goes in v3:
time: 325 us; the launch traced here: 320 us
  Pallas kernels  148 us (46%)
  waiting for transfers between devices  54.4 us (17%)
  starting transfers between devices  48.3 us (15%)
  other arithmetic  30.7 us (9%)
  local copies, waits for them, and re-layouts  23.8 us (7%)
  between operations  15.2 us (5%)
    pallas_call x2, Pallas kernels, expert_first(): pl.pallas_call(functools.partial(expert_first_kernel, 2, filled, blocks,...  38.1 us
    ppermute x25, waiting for transfers between devices, over_seq(): return lax.ppermute(a, 'seq', [(i, i ^ turn) for i in range(n_seq)])  28.8 us
    pallas_call x2, Pallas kernels, expert_second(): pl.pallas_call(functools.partial(expert_second_kernel, 2, count, filled),...  26.5 us
    pallas_call x1, Pallas kernels, attend_back(): pl.pallas_call(functools.partial(attend_back_kernel, head_dim), grid=(ima...  23.6 us
    ppermute x2, waiting for transfers between devices, over_wide(): return lax.ppermute(a, 'wide', [(i, i ^ turn) for i in range(n_wide)])  19.8 us
    ppermute x25, starting transfers between devices, over_seq(): return lax.ppermute(a, 'seq', [(i, i ^ turn) for i in range(n_seq)])  16.1 us
    pallas_call x1, Pallas kernels, attend(): pl.pallas_call(functools.partial(attend_kernel, images, head_dim), grid=(...  15.5 us
    pallas_call x1, Pallas kernels, weight_grad(): pl.pallas_call(functools.partial(weight_grad_kernel, tuple(ends)), grid=(...  11.2 us
  transfers between devices with their start and end apart: 34, of which 17 were waited for; matrix products, arithmetic and copies ran while one was open for 13% of the time, Pallas kernels for 46%

profile of v3, /device:TPU:0, one launch (start us, length us, event | category | flops | bytes accessed | tf_op | source)
XLA Modules:
  0.0 320.1 jit_solution(16149219075650477805)
XLA Ops:
  9.9 6.4 %all-to-all-start = ((bf16[4,80,1024]{2,1,0:T(8,128)(2,1)}), bf16[4,80,1024]{2,1,0:T(8,128)(2,1)}, u32[]{:S(2)}, u32[]{:S(2)}) async-start(bf16[4,80,1024]{2,1,0:T(8,128)(2,1)} %broadcast_in_dim.18), calls=%async_computation | async-start | bytes 1310720 | tf_op jit(solution)/shard_map/all_to_all | solution.py:1094
  22.8 6.9 %collective-permute-done = bf16[3,145,512]{2,1,0:T(8,128)(2,1)} collective-permute-done((bf16[3,145,512]{2,1,0:T(8,128)(2,1)}, bf16[3,145,512]{2,1,0:T(8,128)(2,1)}, u32[]{:S(2)}, u32[]{:S(2)}) %collective-permute-start) | collective-permute-done | bytes 445472 | tf_op jit(solution)/shard_map/ppermute | solution.py:1021
  37.2 16.6 %collective-permute-done.2.there_ref = bf16[4,80,1024]{2,1,0:T(8,128)(2,1)} collective-permute-done((bf16[4,80,1024]{2,1,0:T(8,128)(2,1)}, bf16[4,80,1024]{2,1,0:T(8,128)(2,1)}, u32[]{:S(2)}, u32[]{:S(2)}) %collective-permute-start.2) | collective-permute-done | bytes 655392 | tf_op jit(solution)/shard_map/ppermute | solution.py:1030
  53.8 15.5 %attend.1 = (bf16[3,304,256]{2,1,0:T(8,128)(2,1)S(1)}, bf16[1424,256]{1,0:T(8,128)(2,1)S(1)}, bf16[3,608,768]{2,1,0:T(8,128)(2,1)}, bf16[3,608,512]{2,1,0:T(8,12...) custom-call(s32[4]{0:T(128)S(1)} %pad_add_fusion.at_ref, ...), custom_call_target="tpu_custom_call" | custom-call | flops 1000 | bytes 1000 | tf_op jit(solution)/shard_map/attend/pallas_call | solution.py:136
  73.1 4.4 %project.1 = (f32[3,304,512]{2,1,0:T(8,128)}, bf16[3,304,512]{2,1,0:T(8,128)(2,1)S(1)}, bf16[256,512]{1,0:T(8,128)(2,1)}) custom-call(s32[4]{0:T(128)S(1)} %pad_add_fusion.at_ref, bf16[3,304,256]{2,1,0:T(8,128)(2,1)} %copy-done.4, bf16[1424,256]{1,0:T(8,128)(2,1)} %copy-done.6, bf16[1424,256]{1,0:T(8,128)(2,1)} %copy-done.15, ...), custom_call_target="tpu_custom_call" | custom-call | flops 1000 | bytes 1000 | tf_op jit(solution)/shard_map/project/pallas_call | solution.py:201
  77.5 5.6 %join_cots.1.refs_2_.refs_4_.cot_ref = bf16[6,304,512]{2,1,0:T(8,128)(2,1)} custom-call(s32[4]{0:T(128)S(1)} %pad_add_fusion.at_ref, bf16[6,146,512]{2,1,0:T(8,128)(2,1)} %copy-done.13, bf16[6,146,512]{2,1,0:T(8,128)(2,1)} %collective-permute-done.6.got_ref), custom_call_target="tpu_custom_call" | custom-call | flops 1000 | bytes 1000 | tf_op jit(solution)/shard_map/join_cots/pallas_call | solution.py:248
  85.2 3.1 collective-permute-done.5.refs_1_.refs_2_
  89.3 14.6 %expert_first.2 = (f32[16,304]{1,0:T(8,128)}, bf16[608,512]{1,0:T(8,128)(2,1)}, bf16[608,512]{1,0:T(8,128)(2,1)}, bf16[608,512]{1,0:T(8,128)(2,1)}, bf16[608,512...) custom-call(s32[4]{0:T(128)S(1)} %pad_add_fusion.at_ref, ...), custom_call_target="tpu_custom_call" | custom-call | flops 1000 | bytes 1000 | tf_op jit(solution)/shard_map/expert_first/pallas_call | solution.py:484
  106.5 2.7 collective-permute-done.8.refs_3_
  110.1 23.5 %expert_first.3 = (f32[32,304]{1,0:T(8,128)}, bf16[1216,512]{1,0:T(8,128)(2,1)}, bf16[1216,512]{1,0:T(8,128)(2,1)}, bf16[1216,512]{1,0:T(8,128)(2,1)}, bf16[1216...) custom-call(s32[4]{0:T(128)S(1)} %pad_add_fusion.at_ref, ...), custom_call_target="tpu_custom_call" | custom-call | flops 1000 | bytes 1000 | tf_op jit(solution)/shard_map/expert_first/pallas_call | solution.py:484
  133.6 6.4 %all-to-all-start.2 = ((bf16[8,256,512]{2,1,0:T(8,128)(2,1)}), bf16[8,256,512]{2,1,0:T(8,128)(2,1)}, u32[]{:S(2)}, u32[]{:S(2)}) async-start(bf16[8,256,512]{2,1,0:T(8,128)(2,1)} %get-tuple-element.103), calls=%async_computation.2 | async-start | bytes 4194304 | tf_op jit(solution)/shard_map/all_to_all | solution.py:1169
  140.0 16.4 %expert_second.2 = (bf16[1216,1024]{1,0:T(8,128)(2,1)}, bf16[1216,1024]{1,0:T(8,128)(2,1)}, bf16[3,304,512]{2,1,0:T(8,128)(2,1)S(1)}, bf16[3,304,512]{2,1,0:T(8,...) custom-call(s32[4]{0:T(128)S(1)} %pad_add_fusion.at_ref, ...), custom_call_target="tpu_custom_call" | custom-call | flops 1000 | bytes 1000 | tf_op jit(solution)/shard_map/expert_second/pallas_call | solution.py:575
  160.8 10.1 %expert_second.3 = (bf16[608,1024]{1,0:T(8,128)(2,1)}, bf16[608,1024]{1,0:T(8,128)(2,1)}, bf16[2,304,512]{2,1,0:T(8,128)(2,1)S(1)}, bf16[2,304,512]{2,1,0:T(8,12...) custom-call(s32[4]{0:T(128)S(1)} %pad_add_fusion.at_ref, f32[16,304]{1,0:T(8,128)S(1)} %copy-done.11, ...), custom_call_target="tpu_custom_call" | custom-call | flops 1000 | bytes 1000 | tf_op jit(solution)/shard_map/expert_second/pallas_call | solution.py:575
  172.3 11.2 %weight_grad.1 = bf16[8,256,512]{2,1,0:T(8,128)(2,1)} custom-call(bf16[1216,512]{1,0:T(8,128)(2,1)} %get-tuple-element.151.xs_ref.refs_0_, bf16[608,512]{1,0:T(8,128)(2,1)} %get-tuple-element.116.xs_ref.refs_1_, bf16[1216,512]{1,0:T(8,128)(2,1)} %get-tuple-element.108.g_ref.refs_2_, bf16[608,512]{1,0:T(8,128)(2,1)} %get-tuple-element.118.g_ref.refs_3_, ...), custom_call_target="tpu_custom_call" | custom-call | flops 1000 | bytes 1000 | tf_op jit(solution)/shard_map/weight_grad/pallas_call | solution.py:647
  183.5 5.0 %all-to-all-done.2 = bf16[8,256,512]{2,1,0:T(8,128)(2,1)} async-done(((bf16[8,256,512]{2,1,0:T(8,128)(2,1)}), bf16[8,256,512]{2,1,0:T(8,128)(2,1)}, u32[]{:S(2)}, u32[]{:S(2)}) %all-to-all-start.2) | async-done | bytes 2097184 | tf_op jit(solution)/shard_map/all_to_all | solution.py:1169
  188.6 4.5 %all-to-all-start.3 = ((bf16[8,256,512]{2,1,0:T(8,128)(2,1)}), bf16[8,256,512]{2,1,0:T(8,128)(2,1)}, u32[]{:S(2)}, u32[]{:S(2)}) async-start(bf16[8,256,512]{2,1,0:T(8,128)(2,1)} %weight_grad.1), calls=%async_computation.3 | async-start | bytes 4194304 | tf_op jit(solution)/shard_map/all_to_all | solution.py:1193
  196.9 8.8 %middle_back.1 = (f32[3,304,512]{2,1,0:T(8,128)}, bf16[3,304,512]{2,1,0:T(8,128)(2,1)S(1)}, bf16[8,80,512]{2,1,0:T(8,128)(2,1)}) custom-call(s32[4]{0:T(128)S(1)} %pad_add_fusion.at_ref, bf16[2,304,512]{2,1,0:T(8,128)(2,1)} %copy-done.7, bf16[2,304,512]{2,1,0:T(8,128)(2,1)} %copy-done.30, bf16[2,304,512]{2,1,0:T(8,128)(2,1)} %copy-done.3, ...), custom_call_target="tpu_custom_call" | custom-call | flops 1000 | bytes 1000 | tf_op jit(solution)/shard_map/middle_back/pallas_call | solution.py:770
  209.3 23.6 %attend_back.1 = (bf16[3,304,512]{2,1,0:T(8,128)(2,1)}, bf16[3,304,512]{2,1,0:T(8,128)(2,1)S(1)}, f32[512,768]{1,0:T(8,128)}) custom-call(s32[4]{0:T(128)S(1)} %pad_add_fusion.at_ref, bf16[3,304,512]{2,1,0:T(8,128)(2,1)} %copy-done.5, bf16[3,304,512]{2,1,0:T(8,128)(2,1)} %copy-done.24, bf16[256,512]{1,0:T(8,128)(2,1)} %get-tuple-element.128.pm_ref, ...), custom_call_target="tpu_custom_call" | custom-call | flops 1000 | bytes 1000 | tf_op jit(solution)/shard_map/attend_back/pallas_call | solution.py:886
  236.5 6.0 %input_back.1 = (f32[3,145,512]{2,1,0:T(8,128)S(1)}, bf16[3,145,512]{2,1,0:T(8,128)(2,1)S(1)}, bf16[4,112,512]{2,1,0:T(8,128)(2,1)S(1)}, bf16[4,112,512]{2,1,0:T(8,128)(2,1)S(1)}) custom-call(s32[4]{0:T(128)S(1)} %pad_add_fusion.at_ref, bf16[3,304,512]{2,1,0:T(8,128)(2,1)} %copy-done.12, f32[3,304,512]{2,1,0:T(8,128)} %get-tuple-element.126.gm_ref, ...), custom_call_target="tpu_custom_call" | custom-call | flops 1000 | bytes 1000 | tf_op jit(solution)/shard_map/input_back/pallas_call | solution.py:974
  242.4 6.0 %all-to-all-start.1 = ((bf16[8,80,512]{2,1,0:T(8,128)(2,1)}), bf16[8,80,512]{2,1,0:T(8,128)(2,1)}, u32[]{:S(2)}, u32[]{:S(2)}) async-start(bf16[8,80,512]{2,1,0:T(8,128)(2,1)} %get-tuple-element.148), calls=%async_computation.1 | async-start | bytes 1310720 | tf_op jit(solution)/shard_map/all_to_all | solution.py:1208
  257.5 3.4 %layer_sum.1 = (bf16[3,145,512]{2,1,0:T(8,128)(2,1)S(1)}, bf16[3,145,512]{2,1,0:T(8,128)(2,1)S(1)}) custom-call(f32[3,304,512]{2,1,0:T(8,128)} %get-tuple-element.94.mid_ref, bf16[2,304,512]{2,1,0:T(8,128)(2,1)} %copy-done.8, bf16[2,304,512]{2,1,0:T(8,128)(2,1)} %collective-permute-done.17.ar_ref, bf16[2,304,512]{2,1,0:T(8,128)(2,1)} %copy-done.3, ...), custom_call_target="tpu_custom_call" | custom-call | flops 1000 | bytes 1000 | tf_op jit(solution)/shard_map/layer_sum/pallas_call | solution.py:812
  265.2 3.2 collective-permute-done.19
  271.1 5.2 %all-to-all-start.4 = ((bf16[4,128,512]{2,1,0:T(8,128)(2,1)}), bf16[4,128,512]{2,1,0:T(8,128)(2,1)}, u32[]{:S(2)}, u32[]{:S(2)}) async-start(bf16[4,128,512]{2,1,0:T(8,128)(2,1)} %pad_maximum_fusion.5), calls=%async_computation.4 | async-start | bytes 1048576 | tf_op jit(solution)/shard_map/all_to_all | solution.py:1145
  299.8 4.7 %settle_experts.1 = (f32[4,64,2048]{2,1,0:T(8,128)}, f32[4,256,512]{2,1,0:T(8,128)}) custom-call(s32[4]{0:T(128)S(1)} %pad_add_fusion.at_ref, bf16[4,256,512]{2,1,0:T(8,128)(2,1)} %pad_maximum_fusion.zero_ref, bf16[4,256,512]{2,1,0:T(8,128)(2,1)} %pad_maximum_fusion.1.one_ref), custom_call_target="tpu_custom_call" | custom-call | flops 1000 | bytes 1000 | tf_op jit(solution)/shard_map/settle_experts/pallas_call | solution.py:681
  (220 shorter events, 91.4 us)
Async XLA Ops:
  9.9 23.9 %all-to-all-start = ((bf16[4,80,1024]{2,1,0:T(8,128)(2,1)}), bf16[4,80,1024]{2,1,0:T(8,128)(2,1)}, u32[]{:S(2)}, u32[]{:S(2)}) async-start(bf16[4,80,1024]{2,1,0:T(8,128)(2,1)} %broadcast_in_dim.18), calls=%async_computation | async-start | bytes 1310720 | tf_op jit(solution)/shard_map/all_to_all | solution.py:1094
  16.3 71.9 %all-gather.5.cloned.1.call-start = ((), (), s32[]{:S(2)}) async-start(), calls=%async_computation.5 | async-start | bytes 2359296 | tf_op jit(solution)/shard_map/all_gather | solution.py:1097
  17.2 12.5 %collective-permute-start = (bf16[3,145,512]{2,1,0:T(8,128)(2,1)}, bf16[3,145,512]{2,1,0:T(8,128)(2,1)}, u32[]{:S(2)}, u32[]{:S(2)}) collective-permute-start(bf16[3,145,512]{2,1,0:T(8,128)(2,1)} %pad_maximum_fusion.6), channel_id=1, source_target_pairs={{0,2},{1,3},{2,0},{3,1},{4,6},{5,7},{6,4},{7,5},{8,10},{9,11},{10,... | collective-permute-start | bytes 1336328 | tf_op jit(solution)/shard_map/ppermute | solution.py:1021
  33.8 106.2 %all-gather.7.cloned.1.call-start = ((), (), s32[]{:S(2)}) async-start(), calls=%async_computation.6 | async-start | bytes 2359296 | tf_op jit(solution)/shard_map/all_gather | solution.py:1097
  34.0 19.8 %collective-permute-start.2 = (bf16[4,80,1024]{2,1,0:T(8,128)(2,1)}, bf16[4,80,1024]{2,1,0:T(8,128)(2,1)}, u32[]{:S(2)}, u32[]{:S(2)}) collective-permute-start(bf16[4,80,1024]{2,1,0:T(8,128)(2,1)} %all-to-all-done.here_ref), channel_id=1, source_target_pairs={{0,4},{4,0},{8,12},{12,8},{16,20},{20,16},{24,28},{28,24},{1,5},{5... | collective-permute-start | bytes 1966088 | tf_op jit(solution)/shard_map/ppermute | solution.py:1030
  35.6 41.9 %collective-permute-start.6 = (bf16[6,146,512]{2,1,0:T(8,128)(2,1)S(1)}, bf16[6,146,512]{2,1,0:T(8,128)(2,1)}, u32[]{:S(2)}, u32[]{:S(2)}) collective-permute-start(bf16[6,146,512]{2,1,0:T(8,128)(2,1)S(1)} %pad_maximum_fusion.2.cot_ref), channel_id=1, source_target_pairs={{0,2},{1,3},{2,0},{3,1},{4,6},{5,7},{6,4},{7,5},{8,10},{9,11},{10,... | collective-permute-start | bytes 2691080 | tf_op jit(solution)/shard_map/ppermute | solution.py:1021
  83.1 5.2 %collective-permute-start.7 = (bf16[6,304,512]{2,1,0:T(8,128)(2,1)}, bf16[6,304,512]{2,1,0:T(8,128)(2,1)}, u32[]{:S(2)}, u32[]{:S(2)}) collective-permute-start(bf16[6,304,512]{2,1,0:T(8,128)(2,1)} %join_cots.1.refs_2_.refs_4_.cot_ref), channel_id=1, source_target_pairs={{0,1},{1,0},{2,3},{3,2},{4,5},{5,4},{6,7},{7,6},{8,9},{9,8},{10,11... | collective-permute-start | bytes 5603336 | tf_op jit(solution)/shard_map/ppermute | solution.py:1021
  83.7 22.8 %collective-permute-start.4 = (bf16[3,304,512]{2,1,0:T(8,128)(2,1)S(1)}, bf16[3,304,512]{2,1,0:T(8,128)(2,1)}, u32[]{:S(2)}, u32[]{:S(2)}) collective-permute-start(bf16[3,304,512]{2,1,0:T(8,128)(2,1)S(1)} %get-tuple-element.97.refs_0_.hidden_ref), channel_id=1, source_target_pairs={{0,2},{1,3},{2,0},{3,1},{4,6},{5,7},{6,4},{7,5},{8,10},{9,11},{10,... | collective-permute-start | bytes 2801672 | tf_op jit(solution)/shard_map/ppermute | solution.py:1021
  133.6 54.9 %all-to-all-start.2 = ((bf16[8,256,512]{2,1,0:T(8,128)(2,1)}), bf16[8,256,512]{2,1,0:T(8,128)(2,1)}, u32[]{:S(2)}, u32[]{:S(2)}) async-start(bf16[8,256,512]{2,1,0:T(8,128)(2,1)} %get-tuple-element.103), calls=%async_computation.2 | async-start | bytes 4194304 | tf_op jit(solution)/shard_map/all_to_all | solution.py:1169
  156.5 14.4 %collective-permute-start.14 = (bf16[3,304,512]{2,1,0:T(8,128)(2,1)S(1)}, bf16[3,304,512]{2,1,0:T(8,128)(2,1)S(1)}, u32[]{:S(2)}, u32[]{:S(2)}) collective-permute-start(bf16[3,304,512]{2,1,0:T(8,128)(2,1)S(1)} %get-tuple-element.138), channel_id=1, source_target_pairs={{0,1},{1,0},{2,3},{3,2},{4,5},{5,4},{6,7},{7,6},{8,9},{9,8},{10,11... | collective-permute-start | bytes 2801672 | tf_op jit(solution)/shard_map/ppermute | solution.py:1021
  159.3 24.2 %collective-permute-start.12 = (bf16[3,304,512]{2,1,0:T(8,128)(2,1)S(1)}, bf16[3,304,512]{2,1,0:T(8,128)(2,1)}, u32[]{:S(2)}, u32[]{:S(2)}) collective-permute-start(bf16[3,304,512]{2,1,0:T(8,128)(2,1)S(1)} %add.183), channel_id=1, source_target_pairs={{0,2},{1,3},{2,0},{3,1},{4,6},{5,7},{6,4},{7,5},{8,10},{9,11},{10,... | collective-permute-start | bytes 2801672 | tf_op jit(solution)/shard_map/ppermute | solution.py:1021
  188.6 53.9 %all-to-all-start.3 = ((bf16[8,256,512]{2,1,0:T(8,128)(2,1)}), bf16[8,256,512]{2,1,0:T(8,128)(2,1)}, u32[]{:S(2)}, u32[]{:S(2)}) async-start(bf16[8,256,512]{2,1,0:T(8,128)(2,1)} %weight_grad.1), calls=%async_computation.3 | async-start | bytes 4194304 | tf_op jit(solution)/shard_map/all_to_all | solution.py:1193
  205.9 26.9 %collective-permute-start.15 = (bf16[3,304,512]{2,1,0:T(8,128)(2,1)S(1)}, bf16[3,304,512]{2,1,0:T(8,128)(2,1)S(1)}, u32[]{:S(2)}, u32[]{:S(2)}) collective-permute-start(bf16[3,304,512]{2,1,0:T(8,128)(2,1)S(1)} %copy-done.28), channel_id=1, source_target_pairs={{0,2},{1,3},{2,0},{3,1},{4,6},{5,7},{6,4},{7,5},{8,10},{9,11},{10,... | collective-permute-start | bytes 2801672 | tf_op jit(solution)/shard_map/ppermute | solution.py:1021
  233.1 24.4 %collective-permute-start.17 = (bf16[2,304,512]{2,1,0:T(8,128)(2,1)S(1)}, bf16[2,304,512]{2,1,0:T(8,128)(2,1)}, u32[]{:S(2)}, u32[]{:S(2)}) collective-permute-start(bf16[2,304,512]{2,1,0:T(8,128)(2,1)S(1)} %get-tuple-element.144), channel_id=1, source_target_pairs={{0,1},{1,0},{2,3},{3,2},{4,5},{5,4},{6,7},{7,6},{8,9},{9,8},{10,11... | collective-permute-start | bytes 1867784 | tf_op jit(solution)/shard_map/ppermute | solution.py:1021
  242.4 28.7 %all-to-all-start.1 = ((bf16[8,80,512]{2,1,0:T(8,128)(2,1)}), bf16[8,80,512]{2,1,0:T(8,128)(2,1)}, u32[]{:S(2)}, u32[]{:S(2)}) async-start(bf16[8,80,512]{2,1,0:T(8,128)(2,1)} %get-tuple-element.148), calls=%async_computation.1 | async-start | bytes 1310720 | tf_op jit(solution)/shard_map/all_to_all | solution.py:1208
  251.1 9.8 %collective-permute-start.20 = (bf16[256,512]{1,0:T(8,128)(2,1)}, bf16[256,512]{1,0:T(8,128)(2,1)}, u32[]{:S(2)}, u32[]{:S(2)}) collective-permute-start(bf16[256,512]{1,0:T(8,128)(2,1)} %reduce_sum.51), channel_id=1, source_target_pairs={{0,1},{1,0},{2,3},{3,2},{4,5},{5,4},{6,7},{7,6},{8,9},{9,8},{10,11... | collective-permute-start | bytes 786440 | tf_op jit(solution)/shard_map/ppermute | solution.py:1021
  251.1 17.3 %collective-permute-start.19 = (bf16[4,112,512]{2,1,0:T(8,128)(2,1)S(1)}, bf16[4,112,512]{2,1,0:T(8,128)(2,1)}, u32[]{:S(2)}, u32[]{:S(2)}) collective-permute-start(bf16[4,112,512]{2,1,0:T(8,128)(2,1)S(1)} %get-tuple-element.142), channel_id=1, source_target_pairs={{0,4},{4,0},{8,12},{12,8},{16,20},{20,16},{24,28},{28,24},{1,5},{5... | collective-permute-start | bytes 1376264 | tf_op jit(solution)/shard_map/ppermute | solution.py:1030
  255.8 7.5 %collective-permute-start.21 = (bf16[256,512]{1,0:T(8,128)(2,1)}, bf16[256,512]{1,0:T(8,128)(2,1)S(1)}, u32[]{:S(2)}, u32[]{:S(2)}) collective-permute-start(bf16[256,512]{1,0:T(8,128)(2,1)} %reduce_sum.52), channel_id=1, source_target_pairs={{0,1},{1,0},{2,3},{3,2},{4,5},{5,4},{6,7},{7,6},{8,9},{9,8},{10,11... | collective-permute-start | bytes 786440 | tf_op jit(solution)/shard_map/ppermute | solution.py:1021
  256.0 27.1 %collective-permute-start.24 = (bf16[3,145,512]{2,1,0:T(8,128)(2,1)S(1)}, bf16[3,145,512]{2,1,0:T(8,128)(2,1)}, u32[]{:S(2)}, u32[]{:S(2)}) collective-permute-start(bf16[3,145,512]{2,1,0:T(8,128)(2,1)S(1)} %get-tuple-element.162), channel_id=1, source_target_pairs={{0,2},{1,3},{2,0},{3,1},{4,6},{5,7},{6,4},{7,5},{8,10},{9,11},{10,... | collective-permute-start | bytes 1336328 | tf_op jit(solution)/shard_map/ppermute | solution.py:1021
  262.8 18.1 %collective-permute-start.22 = (bf16[2,256,512]{2,1,0:T(8,128)(2,1)}, bf16[2,256,512]{2,1,0:T(8,128)(2,1)}, u32[]{:S(2)}, u32[]{:S(2)}) collective-permute-start(bf16[2,256,512]{2,1,0:T(8,128)(2,1)} %pad_maximum_fusion.3), channel_id=1, source_target_pairs={{0,2},{1,3},{2,0},{3,1},{4,6},{5,7},{6,4},{7,5},{8,10},{9,11},{10,... | collective-permute-start | bytes 1572872 | tf_op jit(solution)/shard_map/ppermute | solution.py:1021
  271.1 23.2 %all-to-all-start.4 = ((bf16[4,128,512]{2,1,0:T(8,128)(2,1)}), bf16[4,128,512]{2,1,0:T(8,128)(2,1)}, u32[]{:S(2)}, u32[]{:S(2)}) async-start(bf16[4,128,512]{2,1,0:T(8,128)(2,1)} %pad_maximum_fusion.5), calls=%async_computation.4 | async-start | bytes 1048576 | tf_op jit(solution)/shard_map/all_to_all | solution.py:1145
  276.3 15.8 %collective-permute-start.23 = (bf16[2,256,512]{2,1,0:T(8,128)(2,1)}, bf16[2,256,512]{2,1,0:T(8,128)(2,1)}, u32[]{:S(2)}, u32[]{:S(2)}) collective-permute-start(bf16[2,256,512]{2,1,0:T(8,128)(2,1)} %pad_maximum_fusion.4), channel_id=1, source_target_pairs={{0,2},{1,3},{2,0},{3,1},{4,6},{5,7},{6,4},{7,5},{8,10},{9,11},{10,... | collective-permute-start | bytes 1572872 | tf_op jit(solution)/shard_map/ppermute | solution.py:1021
  278.6 25.9 %collective-permute-start.18 = (bf16[3,145,512]{2,1,0:T(8,128)(2,1)S(1)}, bf16[3,145,512]{2,1,0:T(8,128)(2,1)}, u32[]{:S(2)}, u32[]{:S(2)}) collective-permute-start(bf16[3,145,512]{2,1,0:T(8,128)(2,1)S(1)} %get-tuple-element.146), channel_id=1, source_target_pairs={{0,2},{1,3},{2,0},{3,1},{4,6},{5,7},{6,4},{7,5},{8,10},{9,11},{10,... | collective-permute-start | bytes 1336328 | tf_op jit(solution)/shard_map/ppermute | solution.py:1021
  296.6 12.1 %collective-permute-start.25 = (bf16[192,512]{1,0:T(8,128)(2,1)S(1)}, bf16[192,512]{1,0:T(8,128)(2,1)S(1)}, u32[]{:S(2)}, u32[]{:S(2)}) collective-permute-start(bf16[192,512]{1,0:T(8,128)(2,1)S(1)} %pad_maximum_fusion.10), channel_id=1, source_target_pairs={{0,2},{1,3},{2,0},{3,1},{4,6},{5,7},{6,4},{7,5},{8,10},{9,11},{10,... | collective-permute-start | bytes 589832 | tf_op jit(solution)/shard_map/ppermute | solution.py:1021
  (45 other events, 243.8 us)
Sparse Core Ops, SparseCore 0:
  33.9 52.8 all-gather.4
  88.9 47.8 all-gather.6

commit v4 on v3

--- a/solution.py
+++ b/solution.py
@@ -793,37 +793,84 @@
     )(*placed(at, mine, near, extra, extra_near, from_x, middle, cots, vecs, att_m, got, hidden, wr))
 
 
-def layer_kernel(mid_ref, a_ref, ar_ref, b_ref, br_ref, xr_ref, mine_ref, send_ref):
+def mix_kernel(
+    mid_ref, a_ref, ar_ref, b_ref, br_ref, x_ref, xr_ref, mine_ref, theirs_ref, send_ref
+):
     last = pl.program_id(0) == pl.num_programs(0) - 1
     total = jnp.where(
         last,
         b_ref[0].astype(F32) + br_ref[0].astype(F32),
         a_ref[0].astype(F32) + ar_ref[0].astype(F32),
     )
-    total = total + mid_ref[0] + xr_ref[0].astype(F32)
+    total = total + mid_ref[0]
+    other = x_ref[0].astype(F32) + xr_ref[0].astype(F32)
     count = mine_ref.shape[1]
-    mine_ref[0] = total[:count].astype(BF16)
-    send_ref[0] = total[count : 2 * count].astype(BF16)
-
-
-def layer_sum(middle, mine, near, extra, extra_near, from_x, quarter):
+    mine_ref[0] = total[:count]
+    theirs_ref[0] = other[count : 2 * count]
+    send_ref[0, 0] = other[:count].astype(BF16)
+    send_ref[0, 1] = total[count : 2 * count].astype(BF16)
+
+
+def layer_mix(at, middle, mine, near, extra, extra_near, other, other_near, quarter):
     images, rows, width = middle.shape
     one, part = per_image(rows, width), per_image(quarter, width)
     return pl.pallas_call(
-        layer_kernel,
+        lambda at_ref, *refs: mix_kernel(*refs),
         grid=(images,),
         in_specs=[
+            SCALARS,
             one,
             *[early_images(images, rows, width)] * 2,
             *[pl.BlockSpec((1, rows, width), lambda i: (1, 0, 0))] * 2,
             one,
-        ],
-        out_specs=[part, part],
-        out_shape=[jax.ShapeDtypeStruct((images, quarter, width), BF16)] * 2,
+            one,
+        ],
+        out_specs=[part, part, per_image(2, quarter, width)],
+        out_shape=[
+            in_hbm((images, quarter, width), F32),
+            in_hbm((images, quarter, width), F32),
+            jax.ShapeDtypeStruct((images, 2, quarter, width), BF16),
+        ],
         compiler_params=params(24),
         cost_estimate=TINY,
-        name="layer_sum",
-    )(*placed(middle, mine, near, extra, extra_near, from_x))
+        name="layer_mix",
+    )(*placed(at, middle, mine, near, extra, extra_near, other, other_near))
+
+
+def combine_kernel(at_ref, mine_ref, theirs_ref, got_ref, out_ref):
+    ours = pl.program_id(0) // (pl.num_programs(0) // 2) == at_ref[2] // 2
+    value = jnp.where(
+        ours,
+        mine_ref[0] + got_ref[0, 0].astype(F32),
+        theirs_ref[0] + got_ref[0, 1].astype(F32),
+    )
+    out_ref[0] = value.astype(BF16)
+
+
+def layer_combine(at, mine, theirs, got):
+    half, quarter, width = mine.shape
+
+    def image(i, at):
+        return (jnp.where(i < half, i, (i + half - 1) % half), 0, 0)
+
+    part = pl.BlockSpec((1, quarter, width), image)
+    return pl.pallas_call(
+        combine_kernel,
+        grid_spec=pltpu.PrefetchScalarGridSpec(
+            num_scalar_prefetch=1,
+            grid=(2 * half,),
+            in_specs=[
+                part,
+                part,
+                pl.BlockSpec((1, 2, quarter, width), lambda i, at: (*image(i, at), 0)),
+            ],
+            out_specs=pl.BlockSpec((1, quarter, width), lambda i, at: (i, 0, 0)),
+        ),
+        out_shape=jax.ShapeDtypeStruct((2 * half, quarter, width), BF16),
+        compiler_params=params(24),
+        cost_estimate=TINY,
+        name="layer_combine",
+    )(*placed(at, mine, theirs, got))
 
 
 def attend_back_kernel(
@@ -918,8 +965,8 @@
 
 
 def input_back_kernel(
-    at_ref, x_ref, gm_ref, vec_ref, a_ref, ar_ref, gq_ref,
-    out_ref, go_ref, send_ref, keep_ref, sums_ref,
+    x_ref, gm_ref, vec_ref, a_ref, ar_ref, gq_ref, r_ref,
+    out_ref, go_ref, parts_ref, sums_ref,
 ):
     step, images = pl.program_id(0), pl.num_programs(0)
     grad = a_ref[0].astype(F32) + ar_ref[0].astype(F32)
@@ -952,41 +999,35 @@
             line = dot(lines, pick_line).astype(BF16)
             tail = jnp.concatenate([line, jnp.zeros((16, width - 128), BF16)], axis=1)
             block = jnp.concatenate([own[:, :width], half], axis=0)
-            last = block.shape[0]
-
-            def put(ref, block=block, tail=tail, z=index // 2, last=last):
-                ref[z, :last] = block
-                ref[z, last:] = tail
-
-            @pl.when(at_ref[3] == index % 2)
-            def _(put=put):
-                put(keep_ref)
-
-            @pl.when(at_ref[3] != index % 2)
-            def _(put=put):
-                put(send_ref)
-
-
-def input_back(at, x_own, grad_middle, vecs, mine, near, grads, quarter):
+            last = part + block.shape[0]
+            parts_ref[index, part:last] = block
+            parts_ref[index, last + 16 :] = tail
+
+        last = parts_ref.shape[1] - 32
+        parts_ref[:, :part] = r_ref[:, :part]
+        parts_ref[:, last : last + 16] = r_ref[:, part:]
+
+
+def input_back(x_own, grad_middle, vecs, mine, near, grads, r_parts, quarter):
     images, rows, width = x_own.shape
     one, part = per_image(rows, width), per_image(quarter, width)
-    more = (4, width // 8 + (grads.shape[1] - width) * (width // 8) // width + 16, width)
+    more = r_parts.shape[1] + width // 8 + (grads.shape[1] - width) * (width // 8) // width + 16
+    more = (8, more, width)
     return pl.pallas_call(
         input_back_kernel,
         grid=(images,),
-        in_specs=[SCALARS, one, one, whole(vecs.shape), one, one, whole(grads.shape)],
-        out_specs=[part, part, whole(more), whole(more)],
+        in_specs=[one, one, whole(vecs.shape), one, one, whole(grads.shape), whole(r_parts.shape)],
+        out_specs=[part, part, whole(more)],
         out_shape=[
             jax.ShapeDtypeStruct((images, quarter, width), F32),
             jax.ShapeDtypeStruct((images, quarter, width), BF16),
-            jax.ShapeDtypeStruct(more, BF16),
-            jax.ShapeDtypeStruct(more, BF16),
+            in_hbm(more, BF16),
         ],
         scratch_shapes=[pltpu.VMEM((8, width), F32)],
         compiler_params=params(32),
         cost_estimate=TINY,
         name="input_back",
-    )(*placed(at, x_own, grad_middle, vecs, mine, near, grads))
+    )(*placed(x_own, grad_middle, vecs, mine, near, grads, r_parts))
 
 
 def shards(
@@ -1113,10 +1154,8 @@
     )
     mail_got = over_core(mail)
     middle, hidden_two, proj_m = project(at, att_m, mail, mail_got, x_own, vecs)
-    cot_got = after(cot_got, hidden_two)
-    cots_m = join_cots(at, cot, cot_got, rows)
+    cots_m = join_cots(at, cot, after(cot_got, hidden_two), rows)
     cots_o = over_core(cots_m)
-
     hidden_b = over_x(hidden_two)
     hidden_c = over_core(hidden_two)
     ours = (hidden_two, None, hidden_c, None)
@@ -1167,10 +1206,13 @@
     late_ret_r = over_core(late_ret_o)
     if direct:
         sum0 = lax.all_to_all(parts0, "wide", 0, 0, tiled=True)
-    ret_b = after(ret_m, act2) + ret_r
-    xs = (after(first_b[1], ret_b), first_a[1])
+
+    xs = (first_b[1], first_a[1])
     parts1 = weight_grad(xs, (first_b[3], first_a[3]), [gp1, gp2], [act1, act2])
-    ret_x = over_x(after(ret_b, dh_x))
+    layer_mine, layer_theirs, layer_send = layer_mix(
+        after(at, parts1), middle, late_ret_m, late_ret_r, extra_m, extra_r, ret_m, ret_r, quarter
+    )
+    layer_got = over_x(after(layer_send, dh_x))
 
     grad_middle, low_m, r_parts = middle_back(
         at,
@@ -1190,33 +1232,24 @@
     )
     low_o = over_core(low_m)
     if direct:
-        sum1 = lax.all_to_all(after(parts1, dh_x, ret_b), "wide", 0, 0, tiled=True)
+        sum1 = lax.all_to_all(after(parts1, dh_x, layer_send), "wide", 0, 0, tiled=True)
     dh1_m, dh1_o, grad_qkv = attend_back(
         at, low_m, low_o, proj_m, qkv, lse, bias, hidden_one, wq, head_dim
     )
-    dh1_o = after(dh1_o, ret_x)
+    dh1_o = after(dh1_o, layer_got)
     dh1_r = over_core(dh1_o)
-    input_mine, input_send, q_send, q_keep = input_back(
-        at, x_own, grad_middle, vecs, dh1_m, dh1_r, grad_qkv, quarter
-    )
+    input_mine, input_send, q_parts = input_back(
+        x_own, grad_middle, vecs, dh1_m, dh1_r, grad_qkv, r_parts, quarter
+    )
+    last = q_parts.shape[1] - 32
     input_got = over_x(input_send)
-    layer_mine, layer_send = layer_sum(
-        middle, after(late_ret_m, q_send), late_ret_r, extra_m, extra_r, ret_x, quarter
-    )
-    layer_got = over_x(layer_send)
     if direct:
-        r_sum = lax.all_to_all(after(r_parts, q_send), "wide", 0, 0, tiled=True)
-        sum0 = jnp.sum(after(sum0, q_send).astype(F32), axis=0).astype(BF16)
-        sum1 = jnp.sum(after(sum1, q_send).astype(F32), axis=0).astype(BF16)
-        pair0, pair1 = near_pair(sum0), near_pair(sum1)
-        near0, near1 = near_experts(pair0), near_experts(pair1)
-        got = after(over_wide(q_send, 1), pair0, pair1, layer_send)
-        last = q_send.shape[1] - 16
-        q_both = jnp.concatenate(
-            [q_keep[:, :last] + got[:, :last], q_keep[:, last:], got[:, last:]], axis=1
+        rest = lax.all_to_all(q_parts, "wide", 0, 0, tiled=True)
+        sum0, sum1 = (
+            jnp.sum(after(a, q_parts).astype(F32), axis=0).astype(BF16) for a in (sum0, sum1)
         )
+        near0, near1 = near_experts(near_pair(sum0)), near_experts(after(near_pair(sum1), input_got))
     else:
-        q_both = over_y(q_send, q_keep)
         sum0 = expert_sum(parts0)
         sum1 = expert_sum(parts1)
 
@@ -1229,7 +1262,7 @@
             jnp.concatenate([got[pair], got[rest], mine[rest], mine[pair]], axis=0),
         )
 
-    input_grad = settle(input_mine, after(input_got, q_both))
+    input_grad = settle(input_mine, input_got)
     if not direct:
 
         def in_order(a):
@@ -1258,20 +1291,18 @@
 
     owned = proj_weight.shape[0]
     if direct:
-        rest = jnp.sum(after(over_z(q_both), near0, near1).astype(F32), axis=0)
-        r_sum = jnp.sum(after(r_sum, q_both).astype(F32), axis=0)
-        rows = jnp.concatenate([r_sum[:part], rest[:last]])
-        lines = jnp.concatenate(
-            [r_sum[part : part + 8] + r_sum[part + 8 :], jnp.sum(rest[last:].reshape(4, 8, width), 0)]
-        )
+        rest = after(rest, input_got)
+        rest = jnp.sum(rest.astype(F32), axis=0)
+        rows, lines = rest[:last], rest[last:].reshape(2, 2, 8, width)
+        lines = jnp.sum(lines, axis=1).reshape(16, width)
     else:
-        q_all, r_all = q_both.reshape(8, -1, width).astype(F32), r_parts.astype(F32)
-        last = q_all.shape[1] - 16
-        rows = [r_all[:, :part], q_all[:, :part]]
-        halves = q_all[:, part:last].reshape(8, -1, 2, group)
+        both = q_parts.astype(F32)
+        rows = [both[:, :part], both[:, part : 2 * part]]
+        halves = both[:, 2 * part : last].reshape(8, -1, 2, group)
         rows.append(jnp.moveaxis(halves, 2, 1).reshape(8, part, group))
-        for a in (r_all[:, part:], q_all[:, last:]):
-            rows.append(jnp.moveaxis(a[:, :8, :part] + a[:, 8:, :part], 1, 2))
+        for low in (last, last + 16):
+            two = both[:, low : low + 8, :part] + both[:, low + 8 : low + 16, :part]
+            rows.append(jnp.moveaxis(two, 1, 2))
         rows = jnp.concatenate(rows, axis=2).reshape(width, -1)
         rows = lax.psum_scatter(rows, "wide", scatter_dimension=0, tiled=True)
         lines = jnp.pad(rows[:, -16:].T, ((0, 0), (0, width - owned)))
@@ -1281,7 +1312,7 @@
     total, other, lines = over_seq_group(rows, lines)
     if direct:
         grad_up, grad_down = settle_experts(after(at, rows), near0, near1)
-    layer_out = settle(layer_mine, after(layer_got, rows))
+    layer_out = layer_combine(after(at, q_parts), layer_mine, layer_theirs, layer_got)
     grad_proj = total[:owned] + other[:owned]
 
     def thirds(a):

time: 325 us -> 318 us (0.978)
  other arithmetic: 30.7 us -> 16.9 us
  starting transfers between devices: 48.3 us -> 40 us
  Pallas kernels: 148 us -> 155 us
  waiting for transfers between devices: 54.4 us -> 61.2 us
    all_to_all x3 -> x2, waiting for transfers between devices: 0.01 us -> 15.1 us  [the longest x1 14.8 us: shards(): rest = lax.all_to_all(q_parts, 'wide', 0, 0, tiled=True)]
    pallas_call x2 -> x3, Pallas kernels: 9.33 us -> 16.6 us  [the longest x1 6.21 us: input_back(): pl.pallas_call(input_back_kernel, grid=(images,), in_specs=[one, one, who...]
    all_to_all x1, waiting for transfers between devices: 5.01 us -> 0.01 us  [shards(): sum0 = lax.all_to_all(parts0, 'wide', 0, 0, tiled=True)]
    all_to_all x3 -> x2, starting transfers between devices: 15.6 us -> 12.2 us  [the longest x1 6.25 us: shards(): lax.all_to_all(after(parts1, dh_x, layer_send), 'wide', 0, 0, tiled=True)]
    ppermute x2 -> x1, waiting for transfers between devices: 19.8 us -> 16.6 us  [over_wide(): return lax.ppermute(a, 'wide', [(i, i ^ turn) for i in range(n_wide)])]
    unnamed x76 -> x78, local copies, waits for them, and re-layouts: 7.36 us -> 10.4 us
    ppermute x25 -> x24, starting transfers between devices: 16.1 us -> 13.1 us  [over_seq(): return lax.ppermute(a, 'seq', [(i, i ^ turn) for i in range(n_seq)])]
    reduce_sum x5 -> x4, other arithmetic: 7.77 us -> 5.55 us  [the longest x2 5.32 us: shards(): jnp.sum(after(a, q_parts).astype(F32), axis=0).astype(BF16)]
  transfers between devices with their start and end apart: 34 -> 31, of which waited for: 17 -> 15; matrix products, arithmetic and copies ran while one was open for 13% -> 9% of each run, Pallas kernels for 46% -> 49%
where the time goes in v4:
time: 318 us; the launch traced here: 313 us
  Pallas kernels  155 us (49%)
  waiting for transfers between devices  61.2 us (19%)
  starting transfers between devices  40 us (13%)
  local copies, waits for them, and re-layouts  24.9 us (8%)
  other arithmetic  16.9 us (5%)
  between operations  15.1 us (5%)
    pallas_call x2, Pallas kernels, expert_first(): pl.pallas_call(functools.partial(expert_first_kernel, 2, filled, blocks,...  38.2 us
    ppermute x24, waiting for transfers between devices, over_seq(): return lax.ppermute(a, 'seq', [(i, i ^ turn) for i in range(n_seq)])  28.7 us
    pallas_call x2, Pallas kernels, expert_second(): pl.pallas_call(functools.partial(expert_second_kernel, 2, count, filled),...  26.5 us
    pallas_call x1, Pallas kernels, attend_back(): pl.pallas_call(functools.partial(attend_back_kernel, head_dim), grid=(ima...  23.6 us
    ppermute x1, waiting for transfers between devices, over_wide(): return lax.ppermute(a, 'wide', [(i, i ^ turn) for i in range(n_wide)])  16.6 us
    pallas_call x1, Pallas kernels, attend(): pl.pallas_call(functools.partial(attend_kernel, images, head_dim), grid=(...  15.5 us
    all_to_all x1, waiting for transfers between devices, shards(): rest = lax.all_to_all(q_parts, 'wide', 0, 0, tiled=True)  14.8 us
    ppermute x24, starting transfers between devices, over_seq(): return lax.ppermute(a, 'seq', [(i, i ^ turn) for i in range(n_seq)])  13.1 us
  transfers between devices with their start and end apart: 31, of which 15 were waited for; matrix products, arithmetic and copies ran while one was open for 9% of the time, Pallas kernels for 49%

profile of v4, /device:TPU:0, one launch (start us, length us, event | category | flops | bytes accessed | tf_op | source)
XLA Modules:
  0.0 313.1 jit_solution(9895593222168823481)
XLA Ops:
  9.9 6.4 %all-to-all-start = ((bf16[4,80,1024]{2,1,0:T(8,128)(2,1)}), bf16[4,80,1024]{2,1,0:T(8,128)(2,1)}, u32[]{:S(2)}, u32[]{:S(2)}) async-start(bf16[4,80,1024]{2,1,0:T(8,128)(2,1)} %broadcast_in_dim.18), calls=%async_computation | async-start | bytes 1310720 | tf_op jit(solution)/shard_map/all_to_all | solution.py:1135
  24.2 5.5 %collective-permute-done = bf16[3,145,512]{2,1,0:T(8,128)(2,1)} collective-permute-done((bf16[3,145,512]{2,1,0:T(8,128)(2,1)}, bf16[3,145,512]{2,1,0:T(8,128)(2,1)}, u32[]{:S(2)}, u32[]{:S(2)}) %collective-permute-start) | collective-permute-done | bytes 445472 | tf_op jit(solution)/shard_map/ppermute | solution.py:1062
  37.2 16.6 %collective-permute-done.2.there_ref = bf16[4,80,1024]{2,1,0:T(8,128)(2,1)} collective-permute-done((bf16[4,80,1024]{2,1,0:T(8,128)(2,1)}, bf16[4,80,1024]{2,1,0:T(8,128)(2,1)}, u32[]{:S(2)}, u32[]{:S(2)}) %collective-permute-start.2) | collective-permute-done | bytes 655392 | tf_op jit(solution)/shard_map/ppermute | solution.py:1071
  53.8 15.5 %attend.1 = (bf16[3,304,256]{2,1,0:T(8,128)(2,1)S(1)}, bf16[1424,256]{1,0:T(8,128)(2,1)S(1)}, bf16[3,608,768]{2,1,0:T(8,128)(2,1)}, bf16[3,608,512]{2,1,0:T(8,12...) custom-call(s32[4]{0:T(128)S(1)} %pad_add_fusion.at_ref, ...), custom_call_target="tpu_custom_call" | custom-call | flops 1000 | bytes 1000 | tf_op jit(solution)/shard_map/attend/pallas_call | solution.py:136
  73.1 4.3 %project.1 = (f32[3,304,512]{2,1,0:T(8,128)}, bf16[3,304,512]{2,1,0:T(8,128)(2,1)S(1)}, bf16[256,512]{1,0:T(8,128)(2,1)}) custom-call(s32[4]{0:T(128)S(1)} %pad_add_fusion.at_ref, bf16[3,304,256]{2,1,0:T(8,128)(2,1)} %copy-done.4, bf16[1424,256]{1,0:T(8,128)(2,1)} %copy-done.7, bf16[1424,256]{1,0:T(8,128)(2,1)} %copy-done.16, ...), custom_call_target="tpu_custom_call" | custom-call | flops 1000 | bytes 1000 | tf_op jit(solution)/shard_map/project/pallas_call | solution.py:201
  77.5 5.6 %join_cots.1.refs_2_.refs_4_.cot_ref = bf16[6,304,512]{2,1,0:T(8,128)(2,1)} custom-call(s32[4]{0:T(128)S(1)} %pad_add_fusion.at_ref, bf16[6,146,512]{2,1,0:T(8,128)(2,1)} %copy-done.14, bf16[6,146,512]{2,1,0:T(8,128)(2,1)} %collective-permute-done.6.got_ref), custom_call_target="tpu_custom_call" | custom-call | flops 1000 | bytes 1000 | tf_op jit(solution)/shard_map/join_cots/pallas_call | solution.py:248
  85.2 3.1 collective-permute-done.5.refs_1_.refs_2_
  89.3 14.6 %expert_first.2 = (f32[16,304]{1,0:T(8,128)}, bf16[608,512]{1,0:T(8,128)(2,1)}, bf16[608,512]{1,0:T(8,128)(2,1)}, bf16[608,512]{1,0:T(8,128)(2,1)}, bf16[608,512...) custom-call(s32[4]{0:T(128)S(1)} %pad_add_fusion.at_ref, ...), custom_call_target="tpu_custom_call" | custom-call | flops 1000 | bytes 1000 | tf_op jit(solution)/shard_map/expert_first/pallas_call | solution.py:484
  106.5 2.7 collective-permute-done.8.refs_3_
  110.2 23.6 %expert_first.3 = (f32[32,304]{1,0:T(8,128)}, bf16[1216,512]{1,0:T(8,128)(2,1)}, bf16[1216,512]{1,0:T(8,128)(2,1)}, bf16[1216,512]{1,0:T(8,128)(2,1)}, bf16[1216...) custom-call(s32[4]{0:T(128)S(1)} %pad_add_fusion.at_ref, ...), custom_call_target="tpu_custom_call" | custom-call | flops 1000 | bytes 1000 | tf_op jit(solution)/shard_map/expert_first/pallas_call | solution.py:484
  133.8 6.4 %all-to-all-start.2 = ((bf16[8,256,512]{2,1,0:T(8,128)(2,1)}), bf16[8,256,512]{2,1,0:T(8,128)(2,1)}, u32[]{:S(2)}, u32[]{:S(2)}) async-start(bf16[8,256,512]{2,1,0:T(8,128)(2,1)} %get-tuple-element.97), calls=%async_computation.2 | async-start | bytes 4194304 | tf_op jit(solution)/shard_map/all_to_all | solution.py:1208
  140.2 16.4 %expert_second.2 = (bf16[1216,1024]{1,0:T(8,128)(2,1)}, bf16[1216,1024]{1,0:T(8,128)(2,1)}, bf16[3,304,512]{2,1,0:T(8,128)(2,1)S(1)}, bf16[3,304,512]{2,1,0:T(8,...) custom-call(s32[4]{0:T(128)S(1)} %pad_add_fusion.at_ref, ...), custom_call_target="tpu_custom_call" | custom-call | flops 1000 | bytes 1000 | tf_op jit(solution)/shard_map/expert_second/pallas_call | solution.py:575
  161.9 10.1 %expert_second.3 = (bf16[608,1024]{1,0:T(8,128)(2,1)}, bf16[608,1024]{1,0:T(8,128)(2,1)}, bf16[2,304,512]{2,1,0:T(8,128)(2,1)S(1)}, bf16[2,304,512]{2,1,0:T(8,12...) custom-call(s32[4]{0:T(128)S(1)} %pad_add_fusion.at_ref, f32[16,304]{1,0:T(8,128)S(1)} %copy-done.12, ...), custom_call_target="tpu_custom_call" | custom-call | flops 1000 | bytes 1000 | tf_op jit(solution)/shard_map/expert_second/pallas_call | solution.py:575
  172.6 11.2 %weight_grad.1 = bf16[8,256,512]{2,1,0:T(8,128)(2,1)} custom-call(bf16[1216,512]{1,0:T(8,128)(2,1)} %get-tuple-element.100.xs_ref.refs_0_, bf16[608,512]{1,0:T(8,128)(2,1)} %get-tuple-element.110.xs_ref.refs_1_, bf16[1216,512]{1,0:T(8,128)(2,1)} %get-tuple-element.102.g_ref.refs_2_, bf16[608,512]{1,0:T(8,128)(2,1)} %get-tuple-element.112.g_ref.refs_3_, ...), custom_call_target="tpu_custom_call" | custom-call | flops 1000 | bytes 1000 | tf_op jit(solution)/shard_map/weight_grad/pallas_call | solution.py:647
  185.2 4.6 %layer_mix.1 = (f32[3,145,512]{2,1,0:T(8,128)}, f32[3,145,512]{2,1,0:T(8,128)}, bf16[3,2,145,512]{3,2,1,0:T(8,128)(2,1)S(1)}) custom-call(s32[4]{0:T(128)S(1)} %pad_add_fusion.at_ref, f32[3,304,512]{2,1,0:T(8,128)} %get-tuple-element.119.mid_ref.refs_0_, bf16[2,304,512]{2,1,0:T(8,128)(2,1)} %copy-done.9, bf16[2,304,512]{2,1,0:T(8,128)(2,1)} %copy-done.32, ...), custom_call_target="tpu_custom_call" | custom-call | flops 1000 | bytes 1000 | tf_op jit(solution)/shard_map/layer_mix/pallas_call | solution.py:817
  190.7 6.2 %all-to-all-start.3 = ((bf16[8,256,512]{2,1,0:T(8,128)(2,1)}), bf16[8,256,512]{2,1,0:T(8,128)(2,1)}, u32[]{:S(2)}, u32[]{:S(2)}) async-start(bf16[8,256,512]{2,1,0:T(8,128)(2,1)} %weight_grad.1), calls=%async_computation.3 | async-start | bytes 4194304 | tf_op jit(solution)/shard_map/all_to_all | solution.py:1235
  199.9 8.7 %middle_back.1 = (f32[3,304,512]{2,1,0:T(8,128)}, bf16[3,304,512]{2,1,0:T(8,128)(2,1)S(1)}, bf16[8,80,512]{2,1,0:T(8,128)(2,1)}) custom-call(s32[4]{0:T(128)S(1)} %pad_add_fusion.at_ref, bf16[2,304,512]{2,1,0:T(8,128)(2,1)} %copy-done.8, bf16[2,304,512]{2,1,0:T(8,128)(2,1)} %copy-done.30, bf16[2,304,512]{2,1,0:T(8,128)(2,1)} %copy-done.3, ...), custom_call_target="tpu_custom_call" | custom-call | flops 1000 | bytes 1000 | tf_op jit(solution)/shard_map/middle_back/pallas_call | solution.py:770
  212.1 23.6 %attend_back.1 = (bf16[3,304,512]{2,1,0:T(8,128)(2,1)}, bf16[3,304,512]{2,1,0:T(8,128)(2,1)S(1)}, f32[512,768]{1,0:T(8,128)}) custom-call(s32[4]{0:T(128)S(1)} %pad_add_fusion.at_ref, bf16[3,304,512]{2,1,0:T(8,128)(2,1)} %copy-done.5, bf16[3,304,512]{2,1,0:T(8,128)(2,1)} %copy-done.23, bf16[256,512]{1,0:T(8,128)(2,1)} %get-tuple-element.122.pm_ref, ...), custom_call_target="tpu_custom_call" | custom-call | flops 1000 | bytes 1000 | tf_op jit(solution)/shard_map/attend_back/pallas_call | solution.py:933
  239.2 6.2 %input_back.1 = (f32[3,145,512]{2,1,0:T(8,128)S(1)}, bf16[3,145,512]{2,1,0:T(8,128)(2,1)S(1)}, bf16[8,192,512]{2,1,0:T(8,128)(2,1)}) custom-call(bf16[3,304,512]{2,1,0:T(8,128)(2,1)} %copy-done.13, f32[3,304,512]{2,1,0:T(8,128)} %get-tuple-element.120.gm_ref, f32[8,512]{1,0:T(8,128)S(1)} %get-tuple-element.90.vec_ref, ...), custom_call_target="tpu_custom_call" | custom-call | flops 1000 | bytes 1000 | tf_op jit(solution)/shard_map/input_back/pallas_call | solution.py:1016
  245.7 6.0 %all-to-all-start.1 = ((bf16[8,192,512]{2,1,0:T(8,128)(2,1)}), bf16[8,192,512]{2,1,0:T(8,128)(2,1)S(1)}, u32[]{:S(2)}, u32[]{:S(2)}) async-start(bf16[8,192,512]{2,1,0:T(8,128)(2,1)} %get-tuple-element.143), calls=%async_computation.1 | async-start | bytes 3145728 | tf_op jit(solution)/shard_map/all_to_all | solution.py:1247
  257.2 5.8 %layer_combine.1 = bf16[6,145,512]{2,1,0:T(8,128)(2,1)} custom-call(s32[4]{0:T(128)S(1)} %pad_add_fusion.at_ref, f32[3,145,512]{2,1,0:T(8,128)} %get-tuple-element.145.mine_ref, f32[3,145,512]{2,1,0:T(8,128)} %get-tuple-element.146.theirs_ref, bf16[3,2,145,512]{3,2,1,0:T(8,128)(2,1)} %copy.56.got_ref), custom_call_target="tpu_custom_call" | custom-call | flops 1000 | bytes 1000 | tf_op jit(solution)/shard_map/layer_combine/pallas_call | solution.py:857
  274.1 14.8 %all-to-all-done.1 = bf16[8,192,512]{2,1,0:T(8,128)(2,1)S(1)} async-done(((bf16[8,192,512]{2,1,0:T(8,128)(2,1)}), bf16[8,192,512]{2,1,0:T(8,128)(2,1)S(1)}, u32[]{:S(2)}, u32[]{:S(2)}) %all-to-all-start.1) | async-done | bytes 1572896 | tf_op jit(solution)/shard_map/all_to_all | solution.py:1247
  292.1 3.8 %collective-permute-done.24 = bf16[2,256,512]{2,1,0:T(8,128)(2,1)S(1)} collective-permute-done((bf16[2,256,512]{2,1,0:T(8,128)(2,1)S(1)}, bf16[2,256,512]{2,1,0:T(8,128)(2,1)S(1)}, u32[]{:S(2)}, u32[]{:S(2)}) %collective-permute-start.24) | collective-permute-done | bytes 524320 | tf_op jit(solution)/shard_map/ppermute | solution.py:1062
  297.0 4.7 %settle_experts.1 = (f32[4,64,2048]{2,1,0:T(8,128)}, f32[4,256,512]{2,1,0:T(8,128)}) custom-call(s32[4]{0:T(128)S(1)} %pad_add_fusion.at_ref, bf16[4,256,512]{2,1,0:T(8,128)(2,1)} %pad_maximum_fusion.zero_ref, bf16[4,256,512]{2,1,0:T(8,128)(2,1)} %pad_maximum_fusion.1.one_ref), custom_call_target="tpu_custom_call" | custom-call | flops 1000 | bytes 1000 | tf_op jit(solution)/shard_map/settle_experts/pallas_call | solution.py:681
  (205 shorter events, 71.4 us)
Async XLA Ops:
  9.9 23.9 %all-to-all-start = ((bf16[4,80,1024]{2,1,0:T(8,128)(2,1)}), bf16[4,80,1024]{2,1,0:T(8,128)(2,1)}, u32[]{:S(2)}, u32[]{:S(2)}) async-start(bf16[4,80,1024]{2,1,0:T(8,128)(2,1)} %broadcast_in_dim.18), calls=%async_computation | async-start | bytes 1310720 | tf_op jit(solution)/shard_map/all_to_all | solution.py:1135
  16.3 71.9 %all-gather.5.cloned.1.call-start = ((), (), s32[]{:S(2)}) async-start(), calls=%async_computation.4 | async-start | bytes 2359296 | tf_op jit(solution)/shard_map/all_gather | solution.py:1138
  17.2 12.5 %collective-permute-start = (bf16[3,145,512]{2,1,0:T(8,128)(2,1)}, bf16[3,145,512]{2,1,0:T(8,128)(2,1)}, u32[]{:S(2)}, u32[]{:S(2)}) collective-permute-start(bf16[3,145,512]{2,1,0:T(8,128)(2,1)} %pad_maximum_fusion.5), channel_id=1, source_target_pairs={{0,2},{1,3},{2,0},{3,1},{4,6},{5,7},{6,4},{7,5},{8,10},{9,11},{10,... | collective-permute-start | bytes 1336328 | tf_op jit(solution)/shard_map/ppermute | solution.py:1062
  30.9 2.9 collective-permute-start.1
  33.8 106.4 %all-gather.7.cloned.1.call-start = ((), (), s32[]{:S(2)}) async-start(), calls=%async_computation.5 | async-start | bytes 2359296 | tf_op jit(solution)/shard_map/all_gather | solution.py:1138
  34.0 19.8 %collective-permute-start.2 = (bf16[4,80,1024]{2,1,0:T(8,128)(2,1)}, bf16[4,80,1024]{2,1,0:T(8,128)(2,1)}, u32[]{:S(2)}, u32[]{:S(2)}) collective-permute-start(bf16[4,80,1024]{2,1,0:T(8,128)(2,1)} %all-to-all-done.here_ref), channel_id=1, source_target_pairs={{0,4},{4,0},{8,12},{12,8},{16,20},{20,16},{24,28},{28,24},{1,5},{5... | collective-permute-start | bytes 1966088 | tf_op jit(solution)/shard_map/ppermute | solution.py:1071
  35.6 41.9 %collective-permute-start.6 = (bf16[6,146,512]{2,1,0:T(8,128)(2,1)S(1)}, bf16[6,146,512]{2,1,0:T(8,128)(2,1)}, u32[]{:S(2)}, u32[]{:S(2)}) collective-permute-start(bf16[6,146,512]{2,1,0:T(8,128)(2,1)S(1)} %pad_maximum_fusion.2.cot_ref), channel_id=1, source_target_pairs={{0,2},{1,3},{2,0},{3,1},{4,6},{5,7},{6,4},{7,5},{8,10},{9,11},{10,... | collective-permute-start | bytes 2691080 | tf_op jit(solution)/shard_map/ppermute | solution.py:1062
  83.1 5.2 %collective-permute-start.7 = (bf16[6,304,512]{2,1,0:T(8,128)(2,1)}, bf16[6,304,512]{2,1,0:T(8,128)(2,1)}, u32[]{:S(2)}, u32[]{:S(2)}) collective-permute-start(bf16[6,304,512]{2,1,0:T(8,128)(2,1)} %join_cots.1.refs_2_.refs_4_.cot_ref), channel_id=1, source_target_pairs={{0,1},{1,0},{2,3},{3,2},{4,5},{5,4},{6,7},{7,6},{8,9},{9,8},{10,11... | collective-permute-start | bytes 5603336 | tf_op jit(solution)/shard_map/ppermute | solution.py:1062
  83.2 5.0 %collective-permute-start.5 = (bf16[3,304,512]{2,1,0:T(8,128)(2,1)S(1)}, bf16[3,304,512]{2,1,0:T(8,128)(2,1)S(1)}, u32[]{:S(2)}, u32[]{:S(2)}) collective-permute-start(bf16[3,304,512]{2,1,0:T(8,128)(2,1)S(1)} %get-tuple-element.91.refs_0_.hidden_ref), channel_id=1, source_target_pairs={{0,1},{1,0},{2,3},{3,2},{4,5},{5,4},{6,7},{7,6},{8,9},{9,8},{10,11... | collective-permute-start | bytes 2801672 | tf_op jit(solution)/shard_map/ppermute | solution.py:1062
  83.7 22.8 %collective-permute-start.4 = (bf16[3,304,512]{2,1,0:T(8,128)(2,1)S(1)}, bf16[3,304,512]{2,1,0:T(8,128)(2,1)}, u32[]{:S(2)}, u32[]{:S(2)}) collective-permute-start(bf16[3,304,512]{2,1,0:T(8,128)(2,1)S(1)} %get-tuple-element.91.refs_0_.hidden_ref), channel_id=1, source_target_pairs={{0,2},{1,3},{2,0},{3,1},{4,6},{5,7},{6,4},{7,5},{8,10},{9,11},{10,... | collective-permute-start | bytes 2801672 | tf_op jit(solution)/shard_map/ppermute | solution.py:1062
  133.8 56.0 %all-to-all-start.2 = ((bf16[8,256,512]{2,1,0:T(8,128)(2,1)}), bf16[8,256,512]{2,1,0:T(8,128)(2,1)}, u32[]{:S(2)}, u32[]{:S(2)}) async-start(bf16[8,256,512]{2,1,0:T(8,128)(2,1)} %get-tuple-element.97), calls=%async_computation.2 | async-start | bytes 4194304 | tf_op jit(solution)/shard_map/all_to_all | solution.py:1208
  157.5 26.3 %collective-permute-start.15 = (bf16[3,304,512]{2,1,0:T(8,128)(2,1)S(1)}, bf16[3,304,512]{2,1,0:T(8,128)(2,1)S(1)}, u32[]{:S(2)}, u32[]{:S(2)}) collective-permute-start(bf16[3,304,512]{2,1,0:T(8,128)(2,1)S(1)} %get-tuple-element.137), channel_id=1, source_target_pairs={{0,1},{1,0},{2,3},{3,2},{4,5},{5,4},{6,7},{7,6},{8,9},{9,8},{10,11... | collective-permute-start | bytes 2801672 | tf_op jit(solution)/shard_map/ppermute | solution.py:1062
  160.3 29.4 %collective-permute-start.12 = (bf16[3,304,512]{2,1,0:T(8,128)(2,1)S(1)}, bf16[3,304,512]{2,1,0:T(8,128)(2,1)S(1)}, u32[]{:S(2)}, u32[]{:S(2)}) collective-permute-start(bf16[3,304,512]{2,1,0:T(8,128)(2,1)S(1)} %add.174), channel_id=1, source_target_pairs={{0,2},{1,3},{2,0},{3,1},{4,6},{5,7},{6,4},{7,5},{8,10},{9,11},{10,... | collective-permute-start | bytes 2801672 | tf_op jit(solution)/shard_map/ppermute | solution.py:1062
  161.9 21.9 %collective-permute-start.11 = (bf16[2,304,512]{2,1,0:T(8,128)(2,1)S(1)}, bf16[2,304,512]{2,1,0:T(8,128)(2,1)S(1)}, u32[]{:S(2)}, u32[]{:S(2)}) collective-permute-start(bf16[2,304,512]{2,1,0:T(8,128)(2,1)S(1)} %get-tuple-element.118), channel_id=1, source_target_pairs={{0,1},{1,0},{2,3},{3,2},{4,5},{5,4},{6,7},{7,6},{8,9},{9,8},{10,11... | collective-permute-start | bytes 1867784 | tf_op jit(solution)/shard_map/ppermute | solution.py:1062
  172.0 11.8 %collective-permute-start.14 = (bf16[2,304,512]{2,1,0:T(8,128)(2,1)S(1)}, bf16[2,304,512]{2,1,0:T(8,128)(2,1)S(1)}, u32[]{:S(2)}, u32[]{:S(2)}) collective-permute-start(bf16[2,304,512]{2,1,0:T(8,128)(2,1)S(1)} %get-tuple-element.135), channel_id=1, source_target_pairs={{0,1},{1,0},{2,3},{3,2},{4,5},{5,4},{6,7},{7,6},{8,9},{9,8},{10,11... | collective-permute-start | bytes 1867784 | tf_op jit(solution)/shard_map/ppermute | solution.py:1062
  190.7 55.0 %all-to-all-start.3 = ((bf16[8,256,512]{2,1,0:T(8,128)(2,1)}), bf16[8,256,512]{2,1,0:T(8,128)(2,1)}, u32[]{:S(2)}, u32[]{:S(2)}) async-start(bf16[8,256,512]{2,1,0:T(8,128)(2,1)} %weight_grad.1), calls=%async_computation.3 | async-start | bytes 4194304 | tf_op jit(solution)/shard_map/all_to_all | solution.py:1235
  209.5 26.2 %collective-permute-start.16 = (bf16[3,2,145,512]{3,1,2,0:T(2,128)(2,1)S(1)}, bf16[3,2,145,512]{3,1,2,0:T(2,128)(2,1)S(1)}, u32[]{:S(2)}, u32[]{:S(2)}) collective-permute-start(bf16[3,2,145,512]{3,1,2,0:T(2,128)(2,1)S(1)} %copy.55), channel_id=1, source_target_pairs={{0,2},{1,3},{2,0},{3,1},{4,6},{5,7},{6,4},{7,5},{8,10},{9,11},{10,... | collective-permute-start | bytes 2672648 | tf_op jit(solution)/shard_map/ppermute | solution.py:1062
  245.7 43.2 %all-to-all-start.1 = ((bf16[8,192,512]{2,1,0:T(8,128)(2,1)}), bf16[8,192,512]{2,1,0:T(8,128)(2,1)S(1)}, u32[]{:S(2)}, u32[]{:S(2)}) async-start(bf16[8,192,512]{2,1,0:T(8,128)(2,1)} %get-tuple-element.143), calls=%async_computation.1 | async-start | bytes 3145728 | tf_op jit(solution)/shard_map/all_to_all | solution.py:1247
  251.7 19.5 %collective-permute-start.18 = (bf16[3,145,512]{2,1,0:T(8,128)(2,1)S(1)}, bf16[3,145,512]{2,1,0:T(8,128)(2,1)S(1)}, u32[]{:S(2)}, u32[]{:S(2)}) collective-permute-start(bf16[3,145,512]{2,1,0:T(8,128)(2,1)S(1)} %get-tuple-element.148), channel_id=1, source_target_pairs={{0,2},{1,3},{2,0},{3,1},{4,6},{5,7},{6,4},{7,5},{8,10},{9,11},{10,... | collective-permute-start | bytes 1336328 | tf_op jit(solution)/shard_map/ppermute | solution.py:1062
  255.0 12.8 %collective-permute-start.21 = (bf16[256,512]{1,0:T(8,128)(2,1)}, bf16[256,512]{1,0:T(8,128)(2,1)}, u32[]{:S(2)}, u32[]{:S(2)}) collective-permute-start(bf16[256,512]{1,0:T(8,128)(2,1)} %reduce_sum.44), channel_id=1, source_target_pairs={{0,1},{1,0},{2,3},{3,2},{4,5},{5,4},{6,7},{7,6},{8,9},{9,8},{10,11... | collective-permute-start | bytes 786440 | tf_op jit(solution)/shard_map/ppermute | solution.py:1062
  267.3 5.8 %collective-permute-start.23 = (bf16[256,512]{1,0:T(8,128)(2,1)}, bf16[256,512]{1,0:T(8,128)(2,1)S(1)}, u32[]{:S(2)}, u32[]{:S(2)}) collective-permute-start(bf16[256,512]{1,0:T(8,128)(2,1)} %reduce_sum.45), channel_id=1, source_target_pairs={{0,1},{1,0},{2,3},{3,2},{4,5},{5,4},{6,7},{7,6},{8,9},{9,8},{10,11... | collective-permute-start | bytes 786440 | tf_op jit(solution)/shard_map/ppermute | solution.py:1062
  269.6 20.2 %collective-permute-start.22 = (bf16[2,256,512]{2,1,0:T(8,128)(2,1)}, bf16[2,256,512]{2,1,0:T(8,128)(2,1)}, u32[]{:S(2)}, u32[]{:S(2)}) collective-permute-start(bf16[2,256,512]{2,1,0:T(8,128)(2,1)} %pad_maximum_fusion.3), channel_id=1, source_target_pairs={{0,2},{1,3},{2,0},{3,1},{4,6},{5,7},{6,4},{7,5},{8,10},{9,11},{10,... | collective-permute-start | bytes 1572872 | tf_op jit(solution)/shard_map/ppermute | solution.py:1062
  273.1 22.8 %collective-permute-start.24 = (bf16[2,256,512]{2,1,0:T(8,128)(2,1)S(1)}, bf16[2,256,512]{2,1,0:T(8,128)(2,1)S(1)}, u32[]{:S(2)}, u32[]{:S(2)}) collective-permute-start(bf16[2,256,512]{2,1,0:T(8,128)(2,1)S(1)} %pad_maximum_fusion.4), channel_id=1, source_target_pairs={{0,2},{1,3},{2,0},{3,1},{4,6},{5,7},{6,4},{7,5},{8,10},{9,11},{10,... | collective-permute-start | bytes 1572872 | tf_op jit(solution)/shard_map/ppermute | solution.py:1062
  289.3 12.4 %collective-permute-start.19 = (bf16[192,512]{1,0:T(8,128)(2,1)S(1)}, bf16[192,512]{1,0:T(8,128)(2,1)S(1)}, u32[]{:S(2)}, u32[]{:S(2)}) collective-permute-start(bf16[192,512]{1,0:T(8,128)(2,1)S(1)} %pad_maximum_fusion.8), channel_id=1, source_target_pairs={{0,2},{1,3},{2,0},{3,1},{4,6},{5,7},{6,4},{7,5},{8,10},{9,11},{10,... | collective-permute-start | bytes 589832 | tf_op jit(solution)/shard_map/ppermute | solution.py:1062
  (43 other events, 205.2 us)
Sparse Core Ops, SparseCore 0:
  33.9 52.8 all-gather.4
  88.9 47.8 all-gather.6

commit v5 on v4

--- a/solution.py
+++ b/solution.py
@@ -51,9 +51,12 @@
     return pltpu.CompilerParams(vmem_limit_bytes=limit * MIB, **more)
 
 
-def placed(*arrays):
+def placed(*arrays, free=()):
     return [
-        pltpu.with_memory_space_constraint(a, pltpu.HBM) if a.size > 1 << 15 else a for a in arrays
+        pltpu.with_memory_space_constraint(a, pltpu.HBM)
+        if a.size > 1 << 15 and not any(a is f for f in free)
+        else a
+        for a in arrays
     ]
 
 
@@ -167,7 +170,7 @@
         compiler_params=params(40),
         cost_estimate=TINY,
         name="attend",
-    )(*placed(at, x_own, x_oth, bias, here, there))
+    )(*placed(at, x_own, x_oth, bias, here, there, free=(x_oth, there)))
 
 
 def project_kernel(
@@ -218,46 +221,46 @@
         compiler_params=params(24),
         cost_estimate=TINY,
         name="project",
-    )(*placed(at, att_m, sent, got, x_own, vecs))
+    )(*placed(at, att_m, sent, got, x_own, vecs, free=(got,)))
 
 
 def join_kernel(at_ref, cot_ref, got_ref, out_ref):
-    ours = pl.program_id(0) < pl.num_programs(0) // 2
-    first = jnp.where(ours, cot_ref[0], got_ref[0])
-    second = jnp.where(ours, got_ref[0], cot_ref[0])
-    count = first.shape[0] - 1
-    rows, width = out_ref.shape[1:]
-    codes = jnp.concatenate(
-        [first[count:, :count], second[count:, :count], jnp.zeros((1, width - 2 * count), BF16)],
-        axis=1,
-    )
-    fill = jnp.zeros((rows - 2 * count - 1, width), BF16)
-    out_ref[0] = jnp.concatenate([first[:count], second[:count], codes, fill], axis=0)
+    images, rows, width = out_ref.shape
+    half, count = images // 2, cot_ref.shape[1] - 1
+    start = count // 16 * 16
+    for index in range(images):
+        chip = (at_ref[2] // 2 + index // half) % 2
+        k = index % half
+        image = chip * (images - 2) + k if k < half - 1 else half - 1 + chip
+        refs = (cot_ref, got_ref) if index < half else (got_ref, cot_ref)
+        first, second = (ref[image] for ref in refs)
+        second = second.astype(F32)
+        out_ref[index, :start, :] = first[:start]
+        tail = first[start:].astype(F32)
+        codes = jnp.concatenate(
+            [
+                tail[count - start :, :count],
+                second[count:, :count],
+                jnp.zeros((1, width - 2 * count), F32),
+            ],
+            axis=1,
+        )
+        fill = jnp.zeros((rows - 2 * count - 1, width), F32)
+        rest = jnp.concatenate([tail[: count - start], second[:count], codes, fill], axis=0)
+        out_ref[index, start:, :] = rest.astype(BF16)
 
 
 def join_cots(at, cot, got, rows):
     images, _, width = cot.shape
-    half = images // 2
-
-    def image(i, at):
-        chip = (at[2] // 2 + i // half) % 2
-        k = i % half
-        return (jnp.where(k < half - 1, chip * (images - 2) + k, half - 1 + chip), 0, 0)
-
-    one = pl.BlockSpec((1, *cot.shape[1:]), image)
     return pl.pallas_call(
         join_kernel,
-        grid_spec=pltpu.PrefetchScalarGridSpec(
-            num_scalar_prefetch=1,
-            grid=(images,),
-            in_specs=[one, one],
-            out_specs=pl.BlockSpec((1, rows, width), lambda i, at: (i, 0, 0)),
-        ),
-        out_shape=in_hbm((images, rows, width), BF16),
-        compiler_params=params(24),
+        in_specs=[SCALARS, *[pl.BlockSpec(memory_space=pltpu.VMEM)] * 2],
+        out_specs=pl.BlockSpec(memory_space=pltpu.VMEM),
+        out_shape=jax.ShapeDtypeStruct((images, rows, width), BF16),
+        compiler_params=params(16),
         cost_estimate=TINY,
         name="join_cots",
-    )(*placed(at, cot, got))
+    )(at, cot, got)
 
 
 BLOCKS = (
@@ -505,7 +508,7 @@
         compiler_params=params(48),
         cost_estimate=TINY,
         name="expert_first",
-    )(*placed(at, wr, parts, *[hidden[k] for k in kinds], *cots, *sums))
+    )(*placed(at, wr, parts, *[hidden[k] for k in kinds], *cots, *sums, free=(*hidden, cots[1])))
 
 
 def expert_second_kernel(
@@ -548,17 +551,21 @@
     gates = jnp.where(lane == 1, middle.astype(F32), gates)
     gates = jnp.where(lane == 2, low.astype(F32), gates).astype(BF16)
     retb = (ret * weight).astype(BF16)
-    slot = lax.broadcasted_iota(jnp.int32, (rows, rows), 0).astype(F32)
-    picks = [(slot == pos_ref[k : k + 1, :]).astype(F32).astype(BF16) for k in range(2)]
+    slot = lax.broadcasted_iota(jnp.int32, (rows, rows), 1).astype(F32)
+    lanes = -(-rows // 128) * 128
+    tall = jnp.concatenate([pos_ref[...], jnp.zeros((8, lanes - rows), F32)], axis=1)
+    tall = jnp.concatenate([tall, jnp.zeros((120, lanes), F32)], axis=0).T
+    picks = [(slot == tall[:rows, k : k + 1]).astype(F32).astype(BF16) for k in range(2)]
     for number, target in enumerate(targets):
 
         @pl.when(step == number)
         def _(target=target):
             for pick, (dh, i, back, j) in zip(picks, target):
-                back[j] = dot_tn(pick, retb).astype(BF16)
-                out = dot_tn(pick, dxb)
+                back[j] = dot(pick, retb).astype(BF16)
+                out = dot(pick, dxb)
                 dh[i] = out.astype(BF16)
-                tail = dot_tn(gates, pick)[:16]
+                tail = dot(pick, gates)
+                tail = jnp.concatenate([tail, jnp.zeros((lanes - rows, 128), F32)], axis=0).T[:16, :rows]
                 tail = jnp.concatenate(
                     [tail, jnp.zeros((16, out.shape[1] - rows), F32)], axis=1
                 )
@@ -790,7 +797,7 @@
         compiler_params=params(32),
         cost_estimate=TINY,
         name="middle_back",
-    )(*placed(at, mine, near, extra, extra_near, from_x, middle, cots, vecs, att_m, got, hidden, wr))
+    )(*placed(at, mine, near, extra, extra_near, from_x, middle, cots, vecs, att_m, got, hidden, wr, free=(near, extra_near, from_x)))
 
 
 def mix_kernel(
@@ -834,7 +841,7 @@
         compiler_params=params(24),
         cost_estimate=TINY,
         name="layer_mix",
-    )(*placed(at, middle, mine, near, extra, extra_near, other, other_near))
+    )(*placed(at, middle, mine, near, extra, extra_near, other, other_near, free=(near, extra_near, other_near)))
 
 
 def combine_kernel(at_ref, mine_ref, theirs_ref, got_ref, out_ref):
@@ -961,7 +968,7 @@
         compiler_params=params(48),
         cost_estimate=TINY,
         name="attend_back",
-    )(*placed(at, low_m, low_o, proj_m, qkv, lse, bias, hidden_one, wq))
+    )(*placed(at, low_m, low_o, proj_m, qkv, lse, bias, hidden_one, wq, free=(low_m, low_o)))
 
 
 def input_back_kernel(
@@ -995,23 +1002,22 @@
             base = index * part
             own = total[base : base + part].astype(BF16)
             half = jnp.concatenate([own[: part // 2, width:], own[part // 2 :, width:]], axis=1)
-            pick_line = ((row == col + base) & (col < part)).astype(F32).astype(BF16)
+            into = (col >= part) & (col < 2 * part)
+            pick_line = ((row == col - part + base) & into).astype(F32).astype(BF16)
             line = dot(lines, pick_line).astype(BF16)
             tail = jnp.concatenate([line, jnp.zeros((16, width - 128), BF16)], axis=1)
             block = jnp.concatenate([own[:, :width], half], axis=0)
             last = part + block.shape[0]
             parts_ref[index, part:last] = block
-            parts_ref[index, last + 16 :] = tail
-
-        last = parts_ref.shape[1] - 32
+            parts_ref[index, last:] = r_ref[index, part:] + tail
+
         parts_ref[:, :part] = r_ref[:, :part]
-        parts_ref[:, last : last + 16] = r_ref[:, part:]
 
 
 def input_back(x_own, grad_middle, vecs, mine, near, grads, r_parts, quarter):
     images, rows, width = x_own.shape
     one, part = per_image(rows, width), per_image(quarter, width)
-    more = r_parts.shape[1] + width // 8 + (grads.shape[1] - width) * (width // 8) // width + 16
+    more = r_parts.shape[1] + width // 8 + (grads.shape[1] - width) * (width // 8) // width
     more = (8, more, width)
     return pl.pallas_call(
         input_back_kernel,
@@ -1027,7 +1033,7 @@
         compiler_params=params(32),
         cost_estimate=TINY,
         name="input_back",
-    )(*placed(x_own, grad_middle, vecs, mine, near, grads, r_parts))
+    )(*placed(x_own, grad_middle, vecs, mine, near, grads, r_parts, free=(near,)))
 
 
 def shards(
@@ -1241,7 +1247,7 @@
     input_mine, input_send, q_parts = input_back(
         x_own, grad_middle, vecs, dh1_m, dh1_r, grad_qkv, r_parts, quarter
     )
-    last = q_parts.shape[1] - 32
+    last = q_parts.shape[1] - 16
     input_got = over_x(input_send)
     if direct:
         rest = lax.all_to_all(q_parts, "wide", 0, 0, tiled=True)
@@ -1293,16 +1299,17 @@
     if direct:
         rest = after(rest, input_got)
         rest = jnp.sum(rest.astype(F32), axis=0)
-        rows, lines = rest[:last], rest[last:].reshape(2, 2, 8, width)
-        lines = jnp.sum(lines, axis=1).reshape(16, width)
+        rows, lines = rest[:last], rest[last : last + 8] + rest[last + 8 :]
+        lines = jnp.concatenate([lines[:, :part], lines[:, part : 2 * part]])
+        lines = jnp.pad(lines, ((0, 0), (0, width - part)))
     else:
         both = q_parts.astype(F32)
         rows = [both[:, :part], both[:, part : 2 * part]]
         halves = both[:, 2 * part : last].reshape(8, -1, 2, group)
         rows.append(jnp.moveaxis(halves, 2, 1).reshape(8, part, group))
-        for low in (last, last + 16):
-            two = both[:, low : low + 8, :part] + both[:, low + 8 : low + 16, :part]
-            rows.append(jnp.moveaxis(two, 1, 2))
+        two = both[:, last : last + 8] + both[:, last + 8 :]
+        for low in (0, part):
+            rows.append(jnp.moveaxis(two[:, :, low : low + part], 1, 2))
         rows = jnp.concatenate(rows, axis=2).reshape(width, -1)
         rows = lax.psum_scatter(rows, "wide", scatter_dimension=0, tiled=True)
         lines = jnp.pad(rows[:, -16:].T, ((0, 0), (0, width - owned)))

time: 318 us -> 309 us (0.972)
  local copies, waits for them, and re-layouts: 24.9 us -> 19.4 us
  Pallas kernels: 155 us -> 150 us
  waiting for transfers between devices: 61.2 us -> 66 us
  starting transfers between devices: 40 us -> 35.6 us
    unnamed x78 -> x70, local copies, waits for them, and re-layouts: 10.4 us -> 4.98 us
    pallas_call x1, Pallas kernels: 5.59 us -> 1.83 us  [join_cots(): pl.pallas_call(join_kernel, in_specs=[SCALARS, *[pl.BlockSpec(memory_spac...]
    all_to_all x1, waiting for transfers between devices: 0.27 us -> 3.57 us  [shards(): lax.all_to_all(after(parts1, dh_x, layer_send), 'wide', 0, 0, tiled=True)]
  transfers between devices with their start and end apart: 31 -> 31, of which waited for: 15 -> 18; matrix products, arithmetic and copies ran while one was open for 9% -> 9% of each run, Pallas kernels for 49% -> 49%
where the time goes in v5:
time: 309 us; the launch traced here: 304 us
  Pallas kernels  150 us (49%)
  waiting for transfers between devices  66 us (21%)
  starting transfers between devices  35.6 us (12%)
  local copies, waits for them, and re-layouts  19.4 us (6%)
  other arithmetic  17.9 us (6%)
  between operations  15.1 us (5%)
    pallas_call x2, Pallas kernels, expert_first(): pl.pallas_call(functools.partial(expert_first_kernel, 2, filled, blocks,...  38.6 us
    ppermute x24, waiting for transfers between devices, over_seq(): return lax.ppermute(a, 'seq', [(i, i ^ turn) for i in range(n_seq)])  29.9 us
    pallas_call x2, Pallas kernels, expert_second(): pl.pallas_call(functools.partial(expert_second_kernel, 2, count, filled),...  26.5 us
    pallas_call x1, Pallas kernels, attend_back(): pl.pallas_call(functools.partial(attend_back_kernel, head_dim), grid=(ima...  23.3 us
    ppermute x1, waiting for transfers between devices, over_wide(): return lax.ppermute(a, 'wide', [(i, i ^ turn) for i in range(n_wide)])  16.8 us
    pallas_call x1, Pallas kernels, attend(): pl.pallas_call(functools.partial(attend_kernel, images, head_dim), grid=(...  15.4 us
    ppermute x24, starting transfers between devices, over_seq(): return lax.ppermute(a, 'seq', [(i, i ^ turn) for i in range(n_seq)])  14 us
    all_to_all x1, waiting for transfers between devices, shards(): rest = lax.all_to_all(q_parts, 'wide', 0, 0, tiled=True)  11.9 us
  transfers between devices with their start and end apart: 31, of which 18 were waited for; matrix products, arithmetic and copies ran while one was open for 9% of the time, Pallas kernels for 49%

profile of v5, /device:TPU:0, one launch (start us, length us, event | category | flops | bytes accessed | tf_op | source)
XLA Modules:
  0.0 304.1 jit_solution(15668516977528581645)
XLA Ops:
  9.9 6.4 %all-to-all-start = ((bf16[4,80,1024]{2,1,0:T(8,128)(2,1)}), bf16[4,80,1024]{2,1,0:T(8,128)(2,1)}, u32[]{:S(2)}, u32[]{:S(2)}) async-start(bf16[4,80,1024]{2,1,0:T(8,128)(2,1)} %broadcast_in_dim.18), calls=%async_computation | async-start | bytes 1310720 | tf_op jit(solution)/shard_map/all_to_all | solution.py:1141
  24.2 5.5 %collective-permute-done = bf16[3,145,512]{2,1,0:T(8,128)(2,1)} collective-permute-done((bf16[3,145,512]{2,1,0:T(8,128)(2,1)}, bf16[3,145,512]{2,1,0:T(8,128)(2,1)}, u32[]{:S(2)}, u32[]{:S(2)}) %collective-permute-start) | collective-permute-done | bytes 445472 | tf_op jit(solution)/shard_map/ppermute | solution.py:1068
  37.9 16.8 %collective-permute-done.2.there_ref = bf16[4,80,1024]{2,1,0:T(8,128)(2,1)} collective-permute-done((bf16[4,80,1024]{2,1,0:T(8,128)(2,1)}, bf16[4,80,1024]{2,1,0:T(8,128)(2,1)}, u32[]{:S(2)}, u32[]{:S(2)}) %collective-permute-start.2) | collective-permute-done | bytes 655392 | tf_op jit(solution)/shard_map/ppermute | solution.py:1077
  54.7 15.4 %attend.1 = (bf16[3,304,256]{2,1,0:T(8,128)(2,1)S(1)}, bf16[1424,256]{1,0:T(8,128)(2,1)S(1)}, bf16[3,608,768]{2,1,0:T(8,128)(2,1)}, bf16[3,608,512]{2,1,0:T(8,12...) custom-call(s32[4]{0:T(128)S(1)} %pad_add_fusion.at_ref, ...), custom_call_target="tpu_custom_call" | custom-call | flops 1000 | bytes 1000 | tf_op jit(solution)/shard_map/attend/pallas_call | solution.py:139
  73.1 4.4 %project.1 = (f32[3,304,512]{2,1,0:T(8,128)}, bf16[3,304,512]{2,1,0:T(8,128)(2,1)S(1)}, bf16[256,512]{1,0:T(8,128)(2,1)}) custom-call(s32[4]{0:T(128)S(1)} %pad_add_fusion.at_ref, bf16[3,304,256]{2,1,0:T(8,128)(2,1)} %copy-done.12, bf16[1424,256]{1,0:T(8,128)(2,1)} %copy-done.14, bf16[1424,256]{1,0:T(8,128)(2,1)S(1)} %collective-permute-done.3.got_ref, ...), custom_call_target="tpu_custom_call" | custom-call | flops 1000 | bytes 1000 | tf_op jit(solution)/shard_map/project/pallas_call | solution.py:204
  81.5 3.3 %collective-permute-done.5.refs_1_.refs_2_ = bf16[3,304,512]{2,1,0:T(8,128)(2,1)S(1)} collective-permute-done((bf16[3,304,512]{2,1,0:T(8,128)(2,1)}, bf16[3,304,512]{2,1,0:T(8,128)(2,1)S(1)}, u32[]{:S(2)}, u32[]{:S(2)}) %collective-permute-start.5) | collective-permute-done | bytes 933920 | tf_op jit(solution)/shard_map/ppermute | solution.py:1068
  90.2 14.7 %expert_first.2 = (f32[16,304]{1,0:T(8,128)}, bf16[608,512]{1,0:T(8,128)(2,1)}, bf16[608,512]{1,0:T(8,128)(2,1)}, bf16[608,512]{1,0:T(8,128)(2,1)}, bf16[608,512...) custom-call(s32[4]{0:T(128)S(1)} %pad_add_fusion.at_ref, ...), custom_call_target="tpu_custom_call" | custom-call | flops 1000 | bytes 1000 | tf_op jit(solution)/shard_map/expert_first/pallas_call | solution.py:487
  105.0 2.7 collective-permute-done.8.refs_3_
  107.7 23.9 %expert_first.3 = (f32[32,304]{1,0:T(8,128)}, bf16[1216,512]{1,0:T(8,128)(2,1)}, bf16[1216,512]{1,0:T(8,128)(2,1)}, bf16[1216,512]{1,0:T(8,128)(2,1)}, bf16[1216...) custom-call(s32[4]{0:T(128)S(1)} %pad_add_fusion.at_ref, ...), custom_call_target="tpu_custom_call" | custom-call | flops 1000 | bytes 1000 | tf_op jit(solution)/shard_map/expert_first/pallas_call | solution.py:487
  131.6 4.9 %all-to-all-start.2 = ((bf16[8,256,512]{2,1,0:T(8,128)(2,1)}), bf16[8,256,512]{2,1,0:T(8,128)(2,1)}, u32[]{:S(2)}, u32[]{:S(2)}) async-start(bf16[8,256,512]{2,1,0:T(8,128)(2,1)} %get-tuple-element.97), calls=%async_computation.2 | async-start | bytes 4194304 | tf_op jit(solution)/shard_map/all_to_all | solution.py:1214
  137.4 16.3 %expert_second.2 = (bf16[1216,1024]{1,0:T(8,128)(2,1)}, bf16[1216,1024]{1,0:T(8,128)(2,1)}, bf16[3,304,512]{2,1,0:T(8,128)(2,1)S(1)}, bf16[3,304,512]{2,1,0:T(8,...) custom-call(s32[4]{0:T(128)S(1)} %pad_add_fusion.at_ref, ...), custom_call_target="tpu_custom_call" | custom-call | flops 1000 | bytes 1000 | tf_op jit(solution)/shard_map/expert_second/pallas_call | solution.py:582
  158.1 10.2 %expert_second.3 = (bf16[608,1024]{1,0:T(8,128)(2,1)}, bf16[608,1024]{1,0:T(8,128)(2,1)}, bf16[2,304,512]{2,1,0:T(8,128)(2,1)S(1)}, bf16[2,304,512]{2,1,0:T(8,12...) custom-call(s32[4]{0:T(128)S(1)} %pad_add_fusion.at_ref, f32[16,304]{1,0:T(8,128)S(1)} %copy-done.19, ...), custom_call_target="tpu_custom_call" | custom-call | flops 1000 | bytes 1000 | tf_op jit(solution)/shard_map/expert_second/pallas_call | solution.py:582
  168.9 11.3 %weight_grad.1 = bf16[8,256,512]{2,1,0:T(8,128)(2,1)} custom-call(bf16[1216,512]{1,0:T(8,128)(2,1)} %get-tuple-element.100.xs_ref.refs_0_, bf16[608,512]{1,0:T(8,128)(2,1)} %get-tuple-element.110.xs_ref.refs_1_, bf16[1216,512]{1,0:T(8,128)(2,1)} %get-tuple-element.102.g_ref.refs_2_, bf16[608,512]{1,0:T(8,128)(2,1)} %get-tuple-element.112.g_ref.refs_3_, ...), custom_call_target="tpu_custom_call" | custom-call | flops 1000 | bytes 1000 | tf_op jit(solution)/shard_map/weight_grad/pallas_call | solution.py:654
  180.2 4.2 %layer_mix.1 = (f32[3,145,512]{2,1,0:T(8,128)}, f32[3,145,512]{2,1,0:T(8,128)}, bf16[3,2,145,512]{3,2,1,0:T(8,128)(2,1)S(1)}) custom-call(s32[4]{0:T(128)S(1)} %pad_add_fusion.at_ref, f32[3,304,512]{2,1,0:T(8,128)} %get-tuple-element.119.mid_ref.refs_0_, bf16[2,304,512]{2,1,0:T(8,128)(2,1)} %copy-done.16, ...), custom_call_target="tpu_custom_call" | custom-call | flops 1000 | bytes 1000 | tf_op jit(solution)/shard_map/layer_mix/pallas_call | solution.py:824
  185.3 4.5 %all-to-all-start.3 = ((bf16[8,256,512]{2,1,0:T(8,128)(2,1)}), bf16[8,256,512]{2,1,0:T(8,128)(2,1)}, u32[]{:S(2)}, u32[]{:S(2)}) async-start(bf16[8,256,512]{2,1,0:T(8,128)(2,1)} %weight_grad.1), calls=%async_computation.3 | async-start | bytes 4194304 | tf_op jit(solution)/shard_map/all_to_all | solution.py:1241
  192.1 8.2 %middle_back.1 = (f32[3,304,512]{2,1,0:T(8,128)}, bf16[3,304,512]{2,1,0:T(8,128)(2,1)S(1)}, bf16[8,80,512]{2,1,0:T(8,128)(2,1)}) custom-call(s32[4]{0:T(128)S(1)} %pad_add_fusion.at_ref, bf16[2,304,512]{2,1,0:T(8,128)(2,1)} %copy-done.15, bf16[2,304,512]{2,1,0:T(8,128)(2,1)S(1)} %collective-permute-done.10.ar_ref, bf16[2,304,512]{2,1,0:T(8,128)(2,1)} %copy-done.11, ...), custom_call_target="tpu_custom_call" | custom-call | flops 1000 | bytes 1000 | tf_op jit(solution)/shard_map/middle_back/pallas_call | solution.py:777
  203.0 23.3 %attend_back.1 = (bf16[3,304,512]{2,1,0:T(8,128)(2,1)}, bf16[3,304,512]{2,1,0:T(8,128)(2,1)S(1)}, f32[512,768]{1,0:T(8,128)}) custom-call(s32[4]{0:T(128)S(1)} %pad_add_fusion.at_ref, bf16[3,304,512]{2,1,0:T(8,128)(2,1)S(1)} %get-tuple-element.121.lm_ref, bf16[3,304,512]{2,1,0:T(8,128)(2,1)S(1)} %collective-permute-done.13.lo_ref, ...), custom_call_target="tpu_custom_call" | custom-call | flops 1000 | bytes 1000 | tf_op jit(solution)/shard_map/attend_back/pallas_call | solution.py:940
  228.8 6.0 %input_back.1 = (f32[3,145,512]{2,1,0:T(8,128)S(1)}, bf16[3,145,512]{2,1,0:T(8,128)(2,1)S(1)}, bf16[8,176,512]{2,1,0:T(8,128)(2,1)}) custom-call(bf16[3,304,512]{2,1,0:T(8,128)(2,1)} %fusion.4.own_ref.x_ref, f32[3,304,512]{2,1,0:T(8,128)} %get-tuple-element.120.gm_ref, f32[8,512]{1,0:T(8,128)S(1)} %get-tuple-element.90.vec_ref, ...), custom_call_target="tpu_custom_call" | custom-call | flops 1000 | bytes 1000 | tf_op jit(solution)/shard_map/input_back/pallas_call | solution.py:1022
  234.8 3.6 %all-to-all-done.3 = bf16[8,256,512]{2,1,0:T(8,128)(2,1)} async-done(((bf16[8,256,512]{2,1,0:T(8,128)(2,1)}), bf16[8,256,512]{2,1,0:T(8,128)(2,1)}, u32[]{:S(2)}, u32[]{:S(2)}) %all-to-all-start.3) | async-done | bytes 2097184 | tf_op jit(solution)/shard_map/all_to_all | solution.py:1241
  238.4 3.9 %all-to-all-start.1 = ((bf16[8,176,512]{2,1,0:T(8,128)(2,1)}), bf16[8,176,512]{2,1,0:T(8,128)(2,1)S(1)}, u32[]{:S(2)}, u32[]{:S(2)}) async-start(bf16[8,176,512]{2,1,0:T(8,128)(2,1)} %get-tuple-element.143), calls=%async_computation.1 | async-start | bytes 2883584 | tf_op jit(solution)/shard_map/all_to_all | solution.py:1253
  248.2 5.8 %layer_combine.1 = bf16[6,145,512]{2,1,0:T(8,128)(2,1)} custom-call(s32[4]{0:T(128)S(1)} %pad_add_fusion.at_ref, f32[3,145,512]{2,1,0:T(8,128)} %get-tuple-element.145.mine_ref, f32[3,145,512]{2,1,0:T(8,128)} %get-tuple-element.146.theirs_ref, bf16[3,2,145,512]{3,2,1,0:T(8,128)(2,1)} %copy.56.got_ref), custom_call_target="tpu_custom_call" | custom-call | flops 1000 | bytes 1000 | tf_op jit(solution)/shard_map/layer_combine/pallas_call | solution.py:864
  264.7 11.9 %all-to-all-done.1 = bf16[8,176,512]{2,1,0:T(8,128)(2,1)S(1)} async-done(((bf16[8,176,512]{2,1,0:T(8,128)(2,1)}), bf16[8,176,512]{2,1,0:T(8,128)(2,1)S(1)}, u32[]{:S(2)}, u32[]{:S(2)}) %all-to-all-start.1) | async-done | bytes 1441824 | tf_op jit(solution)/shard_map/all_to_all | solution.py:1253
  280.2 6.7 %collective-permute-done.24 = bf16[2,256,512]{2,1,0:T(8,128)(2,1)S(1)} collective-permute-done((bf16[2,256,512]{2,1,0:T(8,128)(2,1)S(1)}, bf16[2,256,512]{2,1,0:T(8,128)(2,1)S(1)}, u32[]{:S(2)}, u32[]{:S(2)}) %collective-permute-start.24) | collective-permute-done | bytes 524320 | tf_op jit(solution)/shard_map/ppermute | solution.py:1068
  288.0 4.7 %settle_experts.1 = (f32[4,64,2048]{2,1,0:T(8,128)}, f32[4,256,512]{2,1,0:T(8,128)}) custom-call(s32[4]{0:T(128)S(1)} %pad_add_fusion.at_ref, bf16[4,256,512]{2,1,0:T(8,128)(2,1)} %pad_maximum_fusion.zero_ref, bf16[4,256,512]{2,1,0:T(8,128)(2,1)} %pad_maximum_fusion.1.one_ref), custom_call_target="tpu_custom_call" | custom-call | flops 1000 | bytes 1000 | tf_op jit(solution)/shard_map/settle_experts/pallas_call | solution.py:688
  (198 shorter events, 70.4 us)
Async XLA Ops:
  9.9 23.9 %all-to-all-start = ((bf16[4,80,1024]{2,1,0:T(8,128)(2,1)}), bf16[4,80,1024]{2,1,0:T(8,128)(2,1)}, u32[]{:S(2)}, u32[]{:S(2)}) async-start(bf16[4,80,1024]{2,1,0:T(8,128)(2,1)} %broadcast_in_dim.18), calls=%async_computation | async-start | bytes 1310720 | tf_op jit(solution)/shard_map/all_to_all | solution.py:1141
  16.3 71.4 %all-gather.5.cloned.1.call-start = ((), (), s32[]{:S(2)}) async-start(), calls=%async_computation.4 | async-start | bytes 2359296 | tf_op jit(solution)/shard_map/all_gather | solution.py:1144
  17.2 12.5 %collective-permute-start = (bf16[3,145,512]{2,1,0:T(8,128)(2,1)}, bf16[3,145,512]{2,1,0:T(8,128)(2,1)}, u32[]{:S(2)}, u32[]{:S(2)}) collective-permute-start(bf16[3,145,512]{2,1,0:T(8,128)(2,1)} %pad_maximum_fusion.5), channel_id=1, source_target_pairs={{0,2},{1,3},{2,0},{3,1},{4,6},{5,7},{6,4},{7,5},{8,10},{9,11},{10,... | collective-permute-start | bytes 1336328 | tf_op jit(solution)/shard_map/ppermute | solution.py:1068
  34.5 102.8 %all-gather.7.cloned.1.call-start = ((), (), s32[]{:S(2)}) async-start(), calls=%async_computation.5 | async-start | bytes 2359296 | tf_op jit(solution)/shard_map/all_gather | solution.py:1144
  34.8 20.0 %collective-permute-start.2 = (bf16[4,80,1024]{2,1,0:T(8,128)(2,1)}, bf16[4,80,1024]{2,1,0:T(8,128)(2,1)}, u32[]{:S(2)}, u32[]{:S(2)}) collective-permute-start(bf16[4,80,1024]{2,1,0:T(8,128)(2,1)} %all-to-all-done.here_ref), channel_id=1, source_target_pairs={{0,4},{4,0},{8,12},{12,8},{16,20},{20,16},{24,28},{28,24},{1,5},{5... | collective-permute-start | bytes 1966088 | tf_op jit(solution)/shard_map/ppermute | solution.py:1077
  36.3 41.1 %collective-permute-start.6 = (bf16[6,146,512]{2,1,0:T(8,128)(2,1)S(1)}, bf16[6,146,512]{2,1,0:T(8,128)(2,1)}, u32[]{:S(2)}, u32[]{:S(2)}) collective-permute-start(bf16[6,146,512]{2,1,0:T(8,128)(2,1)S(1)} %pad_maximum_fusion.2.cot_ref), channel_id=1, source_target_pairs={{0,2},{1,3},{2,0},{3,1},{4,6},{5,7},{6,4},{7,5},{8,10},{9,11},{10,... | collective-permute-start | bytes 2691080 | tf_op jit(solution)/shard_map/ppermute | solution.py:1068
  79.4 6.4 %collective-permute-start.7 = (bf16[6,304,512]{2,1,0:T(8,128)(2,1)S(1)}, bf16[6,304,512]{2,1,0:T(8,128)(2,1)}, u32[]{:S(2)}, u32[]{:S(2)}) collective-permute-start(bf16[6,304,512]{2,1,0:T(8,128)(2,1)S(1)} %join_cots.1.refs_2_.refs_4_.cot_ref), channel_id=1, source_target_pairs={{0,1},{1,0},{2,3},{3,2},{4,5},{5,4},{6,7},{7,6},{8,9},{9,8},{10,11... | collective-permute-start | bytes 5603336 | tf_op jit(solution)/shard_map/ppermute | solution.py:1068
  79.6 5.2 %collective-permute-start.5 = (bf16[3,304,512]{2,1,0:T(8,128)(2,1)}, bf16[3,304,512]{2,1,0:T(8,128)(2,1)S(1)}, u32[]{:S(2)}, u32[]{:S(2)}) collective-permute-start(bf16[3,304,512]{2,1,0:T(8,128)(2,1)} %copy-done.3), channel_id=1, source_target_pairs={{0,1},{1,0},{2,3},{3,2},{4,5},{5,4},{6,7},{7,6},{8,9},{9,8},{10,11... | collective-permute-start | bytes 2801672 | tf_op jit(solution)/shard_map/ppermute | solution.py:1068
  80.0 24.9 %collective-permute-start.4 = (bf16[3,304,512]{2,1,0:T(8,128)(2,1)}, bf16[3,304,512]{2,1,0:T(8,128)(2,1)}, u32[]{:S(2)}, u32[]{:S(2)}) collective-permute-start(bf16[3,304,512]{2,1,0:T(8,128)(2,1)} %copy-done.3), channel_id=1, source_target_pairs={{0,2},{1,3},{2,0},{3,1},{4,6},{5,7},{6,4},{7,5},{8,10},{9,11},{10,... | collective-permute-start | bytes 2801672 | tf_op jit(solution)/shard_map/ppermute | solution.py:1068
  104.9 2.8 collective-permute-start.8
  131.6 53.7 %all-to-all-start.2 = ((bf16[8,256,512]{2,1,0:T(8,128)(2,1)}), bf16[8,256,512]{2,1,0:T(8,128)(2,1)}, u32[]{:S(2)}, u32[]{:S(2)}) async-start(bf16[8,256,512]{2,1,0:T(8,128)(2,1)} %get-tuple-element.97), calls=%async_computation.2 | async-start | bytes 4194304 | tf_op jit(solution)/shard_map/all_to_all | solution.py:1214
  153.8 26.4 %collective-permute-start.15 = (bf16[3,304,512]{2,1,0:T(8,128)(2,1)S(1)}, bf16[3,304,512]{2,1,0:T(8,128)(2,1)S(1)}, u32[]{:S(2)}, u32[]{:S(2)}) collective-permute-start(bf16[3,304,512]{2,1,0:T(8,128)(2,1)S(1)} %get-tuple-element.137), channel_id=1, source_target_pairs={{0,1},{1,0},{2,3},{3,2},{4,5},{5,4},{6,7},{7,6},{8,9},{9,8},{10,11... | collective-permute-start | bytes 2801672 | tf_op jit(solution)/shard_map/ppermute | solution.py:1068
  156.5 28.0 %collective-permute-start.12 = (bf16[3,304,512]{2,1,0:T(8,128)(2,1)S(1)}, bf16[3,304,512]{2,1,0:T(8,128)(2,1)S(1)}, u32[]{:S(2)}, u32[]{:S(2)}) collective-permute-start(bf16[3,304,512]{2,1,0:T(8,128)(2,1)S(1)} %add.179), channel_id=1, source_target_pairs={{0,2},{1,3},{2,0},{3,1},{4,6},{5,7},{6,4},{7,5},{8,10},{9,11},{10,... | collective-permute-start | bytes 2801672 | tf_op jit(solution)/shard_map/ppermute | solution.py:1068
  158.1 22.1 %collective-permute-start.11 = (bf16[2,304,512]{2,1,0:T(8,128)(2,1)S(1)}, bf16[2,304,512]{2,1,0:T(8,128)(2,1)S(1)}, u32[]{:S(2)}, u32[]{:S(2)}) collective-permute-start(bf16[2,304,512]{2,1,0:T(8,128)(2,1)S(1)} %get-tuple-element.118), channel_id=1, source_target_pairs={{0,1},{1,0},{2,3},{3,2},{4,5},{5,4},{6,7},{7,6},{8,9},{9,8},{10,11... | collective-permute-start | bytes 1867784 | tf_op jit(solution)/shard_map/ppermute | solution.py:1068
  168.4 11.9 %collective-permute-start.14 = (bf16[2,304,512]{2,1,0:T(8,128)(2,1)S(1)}, bf16[2,304,512]{2,1,0:T(8,128)(2,1)S(1)}, u32[]{:S(2)}, u32[]{:S(2)}) collective-permute-start(bf16[2,304,512]{2,1,0:T(8,128)(2,1)S(1)} %get-tuple-element.135), channel_id=1, source_target_pairs={{0,1},{1,0},{2,3},{3,2},{4,5},{5,4},{6,7},{7,6},{8,9},{9,8},{10,11... | collective-permute-start | bytes 1867784 | tf_op jit(solution)/shard_map/ppermute | solution.py:1068
  185.3 53.1 %all-to-all-start.3 = ((bf16[8,256,512]{2,1,0:T(8,128)(2,1)}), bf16[8,256,512]{2,1,0:T(8,128)(2,1)}, u32[]{:S(2)}, u32[]{:S(2)}) async-start(bf16[8,256,512]{2,1,0:T(8,128)(2,1)} %weight_grad.1), calls=%async_computation.3 | async-start | bytes 4194304 | tf_op jit(solution)/shard_map/all_to_all | solution.py:1241
  201.3 24.9 %collective-permute-start.16 = (bf16[3,2,145,512]{3,1,2,0:T(2,128)(2,1)S(1)}, bf16[3,2,145,512]{3,1,2,0:T(2,128)(2,1)S(1)}, u32[]{:S(2)}, u32[]{:S(2)}) collective-permute-start(bf16[3,2,145,512]{3,1,2,0:T(2,128)(2,1)S(1)} %copy.55), channel_id=1, source_target_pairs={{0,2},{1,3},{2,0},{3,1},{4,6},{5,7},{6,4},{7,5},{8,10},{9,11},{10,... | collective-permute-start | bytes 2672648 | tf_op jit(solution)/shard_map/ppermute | solution.py:1068
  238.4 38.2 %all-to-all-start.1 = ((bf16[8,176,512]{2,1,0:T(8,128)(2,1)}), bf16[8,176,512]{2,1,0:T(8,128)(2,1)S(1)}, u32[]{:S(2)}, u32[]{:S(2)}) async-start(bf16[8,176,512]{2,1,0:T(8,128)(2,1)} %get-tuple-element.143), calls=%async_computation.1 | async-start | bytes 2883584 | tf_op jit(solution)/shard_map/all_to_all | solution.py:1253
  242.3 19.5 %collective-permute-start.18 = (bf16[3,145,512]{2,1,0:T(8,128)(2,1)S(1)}, bf16[3,145,512]{2,1,0:T(8,128)(2,1)S(1)}, u32[]{:S(2)}, u32[]{:S(2)}) collective-permute-start(bf16[3,145,512]{2,1,0:T(8,128)(2,1)S(1)} %get-tuple-element.148), channel_id=1, source_target_pairs={{0,2},{1,3},{2,0},{3,1},{4,6},{5,7},{6,4},{7,5},{8,10},{9,11},{10,... | collective-permute-start | bytes 1336328 | tf_op jit(solution)/shard_map/ppermute | solution.py:1068
  246.0 12.8 %collective-permute-start.21 = (bf16[256,512]{1,0:T(8,128)(2,1)}, bf16[256,512]{1,0:T(8,128)(2,1)}, u32[]{:S(2)}, u32[]{:S(2)}) collective-permute-start(bf16[256,512]{1,0:T(8,128)(2,1)} %reduce_sum.34), channel_id=1, source_target_pairs={{0,1},{1,0},{2,3},{3,2},{4,5},{5,4},{6,7},{7,6},{8,9},{9,8},{10,11... | collective-permute-start | bytes 786440 | tf_op jit(solution)/shard_map/ppermute | solution.py:1068
  258.3 5.4 %collective-permute-start.23 = (bf16[256,512]{1,0:T(8,128)(2,1)}, bf16[256,512]{1,0:T(8,128)(2,1)S(1)}, u32[]{:S(2)}, u32[]{:S(2)}) collective-permute-start(bf16[256,512]{1,0:T(8,128)(2,1)} %reduce_sum.35), channel_id=1, source_target_pairs={{0,1},{1,0},{2,3},{3,2},{4,5},{5,4},{6,7},{7,6},{8,9},{9,8},{10,11... | collective-permute-start | bytes 786440 | tf_op jit(solution)/shard_map/ppermute | solution.py:1068
  260.7 17.3 %collective-permute-start.22 = (bf16[2,256,512]{2,1,0:T(8,128)(2,1)}, bf16[2,256,512]{2,1,0:T(8,128)(2,1)}, u32[]{:S(2)}, u32[]{:S(2)}) collective-permute-start(bf16[2,256,512]{2,1,0:T(8,128)(2,1)} %pad_maximum_fusion.3), channel_id=1, source_target_pairs={{0,2},{1,3},{2,0},{3,1},{4,6},{5,7},{6,4},{7,5},{8,10},{9,11},{10,... | collective-permute-start | bytes 1572872 | tf_op jit(solution)/shard_map/ppermute | solution.py:1068
  263.7 23.2 %collective-permute-start.24 = (bf16[2,256,512]{2,1,0:T(8,128)(2,1)S(1)}, bf16[2,256,512]{2,1,0:T(8,128)(2,1)S(1)}, u32[]{:S(2)}, u32[]{:S(2)}) collective-permute-start(bf16[2,256,512]{2,1,0:T(8,128)(2,1)S(1)} %pad_maximum_fusion.4), channel_id=1, source_target_pairs={{0,2},{1,3},{2,0},{3,1},{4,6},{5,7},{6,4},{7,5},{8,10},{9,11},{10,... | collective-permute-start | bytes 1572872 | tf_op jit(solution)/shard_map/ppermute | solution.py:1068
  277.0 15.7 %collective-permute-start.19 = (bf16[192,512]{1,0:T(8,128)(2,1)S(1)}, bf16[192,512]{1,0:T(8,128)(2,1)S(1)}, u32[]{:S(2)}, u32[]{:S(2)}) collective-permute-start(bf16[192,512]{1,0:T(8,128)(2,1)S(1)} %pad_maximum_fusion.8), channel_id=1, source_target_pairs={{0,2},{1,3},{2,0},{3,1},{4,6},{5,7},{6,4},{7,5},{8,10},{9,11},{10,... | collective-permute-start | bytes 589832 | tf_op jit(solution)/shard_map/ppermute | solution.py:1068
  (39 other events, 219.7 us)
Sparse Core Ops, SparseCore 0:
  34.7 53.0 all-gather.4
  89.9 47.4 all-gather.6

commit v6 on v5

--- a/solution.py
+++ b/solution.py
@@ -1254,7 +1254,9 @@
         sum0, sum1 = (
             jnp.sum(after(a, q_parts).astype(F32), axis=0).astype(BF16) for a in (sum0, sum1)
         )
-        near0, near1 = near_experts(near_pair(sum0)), near_experts(after(near_pair(sum1), input_got))
+        pair0, pair1 = near_pair(sum0), near_pair(sum1)
+        near0, near1 = near_experts(pair0), near_experts(pair1)
+        at = after(at, pair0, pair1)
     else:
         sum0 = expert_sum(parts0)
         sum1 = expert_sum(parts1)
@@ -1269,6 +1271,7 @@
         )
 
     input_grad = settle(input_mine, input_got)
+    layer_out = layer_combine(after(at, q_parts), layer_mine, layer_theirs, layer_got)
     if not direct:
 
         def in_order(a):
@@ -1297,7 +1300,7 @@
 
     owned = proj_weight.shape[0]
     if direct:
-        rest = after(rest, input_got)
+        rest = after(rest, layer_out, input_grad)
         rest = jnp.sum(rest.astype(F32), axis=0)
         rows, lines = rest[:last], rest[last : last + 8] + rest[last + 8 :]
         lines = jnp.concatenate([lines[:, :part], lines[:, part : 2 * part]])
@@ -1319,7 +1322,6 @@
     total, other, lines = over_seq_group(rows, lines)
     if direct:
         grad_up, grad_down = settle_experts(after(at, rows), near0, near1)
-    layer_out = layer_combine(after(at, q_parts), layer_mine, layer_theirs, layer_got)
     grad_proj = total[:owned] + other[:owned]
 
     def thirds(a):

time: 309 us -> 304 us (0.984)
  waiting for transfers between devices: 66 us -> 60.9 us
    ppermute x24, waiting for transfers between devices: 29.9 us -> 24.2 us  [over_seq(): return lax.ppermute(a, 'seq', [(i, i ^ turn) for i in range(n_seq)])]
  transfers between devices with their start and end apart: 31 -> 31, of which waited for: 18 -> 17; matrix products, arithmetic and copies ran while one was open for 9% -> 10% of each run, Pallas kernels for 49% -> 50%
where the time goes in v6:
time: 304 us; the launch traced here: 300 us
  Pallas kernels  150 us (49%)
  waiting for transfers between devices  60.9 us (20%)
  starting transfers between devices  35 us (12%)
  local copies, waits for them, and re-layouts  19.4 us (6%)
  other arithmetic  19 us (6%)
  between operations  15.2 us (5%)
    pallas_call x2, Pallas kernels, expert_first(): pl.pallas_call(functools.partial(expert_first_kernel, 2, filled, blocks,...  38.6 us
    pallas_call x2, Pallas kernels, expert_second(): pl.pallas_call(functools.partial(expert_second_kernel, 2, count, filled),...  26.5 us
    ppermute x24, waiting for transfers between devices, over_seq(): return lax.ppermute(a, 'seq', [(i, i ^ turn) for i in range(n_seq)])  24.2 us
    pallas_call x1, Pallas kernels, attend_back(): pl.pallas_call(functools.partial(attend_back_kernel, head_dim), grid=(ima...  23.2 us
    ppermute x1, waiting for transfers between devices, over_wide(): return lax.ppermute(a, 'wide', [(i, i ^ turn) for i in range(n_wide)])  16.8 us
    pallas_call x1, Pallas kernels, attend(): pl.pallas_call(functools.partial(attend_kernel, images, head_dim), grid=(...  15.4 us
    ppermute x24, starting transfers between devices, over_seq(): return lax.ppermute(a, 'seq', [(i, i ^ turn) for i in range(n_seq)])  13.4 us
    all_to_all x1, waiting for transfers between devices, shards(): rest = lax.all_to_all(q_parts, 'wide', 0, 0, tiled=True)  11.9 us
  transfers between devices with their start and end apart: 31, of which 17 were waited for; matrix products, arithmetic and copies ran while one was open for 10% of the time, Pallas kernels for 50%

profile of v6, /device:TPU:0, one launch (start us, length us, event | category | flops | bytes accessed | tf_op | source)
XLA Modules:
  0.0 299.5 jit_solution(11762534963671107235)
XLA Ops:
  9.9 6.4 %all-to-all-start = ((bf16[4,80,1024]{2,1,0:T(8,128)(2,1)}), bf16[4,80,1024]{2,1,0:T(8,128)(2,1)}, u32[]{:S(2)}, u32[]{:S(2)}) async-start(bf16[4,80,1024]{2,1,0:T(8,128)(2,1)} %broadcast_in_dim.18), calls=%async_computation | async-start | bytes 1310720 | tf_op jit(solution)/shard_map/all_to_all | solution.py:1141
  24.2 5.5 %collective-permute-done = bf16[3,145,512]{2,1,0:T(8,128)(2,1)} collective-permute-done((bf16[3,145,512]{2,1,0:T(8,128)(2,1)}, bf16[3,145,512]{2,1,0:T(8,128)(2,1)}, u32[]{:S(2)}, u32[]{:S(2)}) %collective-permute-start) | collective-permute-done | bytes 445472 | tf_op jit(solution)/shard_map/ppermute | solution.py:1068
  37.9 16.8 %collective-permute-done.2.there_ref = bf16[4,80,1024]{2,1,0:T(8,128)(2,1)} collective-permute-done((bf16[4,80,1024]{2,1,0:T(8,128)(2,1)}, bf16[4,80,1024]{2,1,0:T(8,128)(2,1)}, u32[]{:S(2)}, u32[]{:S(2)}) %collective-permute-start.2) | collective-permute-done | bytes 655392 | tf_op jit(solution)/shard_map/ppermute | solution.py:1077
  54.7 15.4 %attend.1 = (bf16[3,304,256]{2,1,0:T(8,128)(2,1)S(1)}, bf16[1424,256]{1,0:T(8,128)(2,1)S(1)}, bf16[3,608,768]{2,1,0:T(8,128)(2,1)}, bf16[3,608,512]{2,1,0:T(8,12...) custom-call(s32[4]{0:T(128)S(1)} %pad_add_fusion.at_ref, ...), custom_call_target="tpu_custom_call" | custom-call | flops 1000 | bytes 1000 | tf_op jit(solution)/shard_map/attend/pallas_call | solution.py:139
  73.1 4.4 %project.1 = (f32[3,304,512]{2,1,0:T(8,128)}, bf16[3,304,512]{2,1,0:T(8,128)(2,1)S(1)}, bf16[256,512]{1,0:T(8,128)(2,1)}) custom-call(s32[4]{0:T(128)S(1)} %pad_add_fusion.at_ref, bf16[3,304,256]{2,1,0:T(8,128)(2,1)} %copy-done.12, bf16[1424,256]{1,0:T(8,128)(2,1)} %copy-done.14, bf16[1424,256]{1,0:T(8,128)(2,1)S(1)} %collective-permute-done.3.got_ref, ...), custom_call_target="tpu_custom_call" | custom-call | flops 1000 | bytes 1000 | tf_op jit(solution)/shard_map/project/pallas_call | solution.py:204
  81.5 3.3 %collective-permute-done.5.refs_1_.refs_2_ = bf16[3,304,512]{2,1,0:T(8,128)(2,1)S(1)} collective-permute-done((bf16[3,304,512]{2,1,0:T(8,128)(2,1)}, bf16[3,304,512]{2,1,0:T(8,128)(2,1)S(1)}, u32[]{:S(2)}, u32[]{:S(2)}) %collective-permute-start.5) | collective-permute-done | bytes 933920 | tf_op jit(solution)/shard_map/ppermute | solution.py:1068
  90.2 14.7 %expert_first.2 = (f32[16,304]{1,0:T(8,128)}, bf16[608,512]{1,0:T(8,128)(2,1)}, bf16[608,512]{1,0:T(8,128)(2,1)}, bf16[608,512]{1,0:T(8,128)(2,1)}, bf16[608,512...) custom-call(s32[4]{0:T(128)S(1)} %pad_add_fusion.at_ref, ...), custom_call_target="tpu_custom_call" | custom-call | flops 1000 | bytes 1000 | tf_op jit(solution)/shard_map/expert_first/pallas_call | solution.py:487
  105.0 2.7 collective-permute-done.8.refs_3_
  107.7 23.9 %expert_first.3 = (f32[32,304]{1,0:T(8,128)}, bf16[1216,512]{1,0:T(8,128)(2,1)}, bf16[1216,512]{1,0:T(8,128)(2,1)}, bf16[1216,512]{1,0:T(8,128)(2,1)}, bf16[1216...) custom-call(s32[4]{0:T(128)S(1)} %pad_add_fusion.at_ref, ...), custom_call_target="tpu_custom_call" | custom-call | flops 1000 | bytes 1000 | tf_op jit(solution)/shard_map/expert_first/pallas_call | solution.py:487
  131.6 4.9 %all-to-all-start.1 = ((bf16[8,256,512]{2,1,0:T(8,128)(2,1)}), bf16[8,256,512]{2,1,0:T(8,128)(2,1)}, u32[]{:S(2)}, u32[]{:S(2)}) async-start(bf16[8,256,512]{2,1,0:T(8,128)(2,1)} %get-tuple-element.97), calls=%async_computation.1 | async-start | bytes 4194304 | tf_op jit(solution)/shard_map/all_to_all | solution.py:1214
  138.0 16.3 %expert_second.2 = (bf16[1216,1024]{1,0:T(8,128)(2,1)}, bf16[1216,1024]{1,0:T(8,128)(2,1)}, bf16[3,304,512]{2,1,0:T(8,128)(2,1)S(1)}, bf16[3,304,512]{2,1,0:T(8,...) custom-call(s32[4]{0:T(128)S(1)} %pad_add_fusion.at_ref, ...), custom_call_target="tpu_custom_call" | custom-call | flops 1000 | bytes 1000 | tf_op jit(solution)/shard_map/expert_second/pallas_call | solution.py:582
  158.1 10.2 %expert_second.3 = (bf16[608,1024]{1,0:T(8,128)(2,1)}, bf16[608,1024]{1,0:T(8,128)(2,1)}, bf16[2,304,512]{2,1,0:T(8,128)(2,1)S(1)}, bf16[2,304,512]{2,1,0:T(8,12...) custom-call(s32[4]{0:T(128)S(1)} %pad_add_fusion.at_ref, f32[16,304]{1,0:T(8,128)S(1)} %copy-done.19, ...), custom_call_target="tpu_custom_call" | custom-call | flops 1000 | bytes 1000 | tf_op jit(solution)/shard_map/expert_second/pallas_call | solution.py:582
  169.0 11.2 %weight_grad.1 = bf16[8,256,512]{2,1,0:T(8,128)(2,1)} custom-call(bf16[1216,512]{1,0:T(8,128)(2,1)} %get-tuple-element.100.xs_ref.refs_0_, bf16[608,512]{1,0:T(8,128)(2,1)} %get-tuple-element.110.xs_ref.refs_1_, bf16[1216,512]{1,0:T(8,128)(2,1)} %get-tuple-element.102.g_ref.refs_2_, bf16[608,512]{1,0:T(8,128)(2,1)} %get-tuple-element.112.g_ref.refs_3_, ...), custom_call_target="tpu_custom_call" | custom-call | flops 1000 | bytes 1000 | tf_op jit(solution)/shard_map/weight_grad/pallas_call | solution.py:654
  180.3 4.3 %layer_mix.1 = (f32[3,145,512]{2,1,0:T(8,128)}, f32[3,145,512]{2,1,0:T(8,128)}, bf16[3,2,145,512]{3,2,1,0:T(8,128)(2,1)S(1)}) custom-call(s32[4]{0:T(128)S(1)} %pad_add_fusion.at_ref, f32[3,304,512]{2,1,0:T(8,128)} %get-tuple-element.119.mid_ref.refs_0_, bf16[2,304,512]{2,1,0:T(8,128)(2,1)} %copy-done.16, ...), custom_call_target="tpu_custom_call" | custom-call | flops 1000 | bytes 1000 | tf_op jit(solution)/shard_map/layer_mix/pallas_call | solution.py:824
  185.3 4.5 %all-to-all-start.2 = ((bf16[8,256,512]{2,1,0:T(8,128)(2,1)}), bf16[8,256,512]{2,1,0:T(8,128)(2,1)}, u32[]{:S(2)}, u32[]{:S(2)}) async-start(bf16[8,256,512]{2,1,0:T(8,128)(2,1)} %weight_grad.1), calls=%async_computation.2 | async-start | bytes 4194304 | tf_op jit(solution)/shard_map/all_to_all | solution.py:1241
  192.1 8.2 %middle_back.1 = (f32[3,304,512]{2,1,0:T(8,128)}, bf16[3,304,512]{2,1,0:T(8,128)(2,1)S(1)}, bf16[8,80,512]{2,1,0:T(8,128)(2,1)}) custom-call(s32[4]{0:T(128)S(1)} %pad_add_fusion.at_ref, bf16[2,304,512]{2,1,0:T(8,128)(2,1)} %copy-done.15, bf16[2,304,512]{2,1,0:T(8,128)(2,1)S(1)} %collective-permute-done.10.ar_ref, bf16[2,304,512]{2,1,0:T(8,128)(2,1)} %copy-done.11, ...), custom_call_target="tpu_custom_call" | custom-call | flops 1000 | bytes 1000 | tf_op jit(solution)/shard_map/middle_back/pallas_call | solution.py:777
  202.9 23.2 %attend_back.1 = (bf16[3,304,512]{2,1,0:T(8,128)(2,1)}, bf16[3,304,512]{2,1,0:T(8,128)(2,1)S(1)}, f32[512,768]{1,0:T(8,128)}) custom-call(s32[4]{0:T(128)S(1)} %pad_add_fusion.at_ref, bf16[3,304,512]{2,1,0:T(8,128)(2,1)S(1)} %get-tuple-element.121.lm_ref, bf16[3,304,512]{2,1,0:T(8,128)(2,1)S(1)} %collective-permute-done.13.lo_ref, ...), custom_call_target="tpu_custom_call" | custom-call | flops 1000 | bytes 1000 | tf_op jit(solution)/shard_map/attend_back/pallas_call | solution.py:940
  228.8 6.0 %input_back.1 = (f32[3,145,512]{2,1,0:T(8,128)S(1)}, bf16[3,145,512]{2,1,0:T(8,128)(2,1)S(1)}, bf16[8,176,512]{2,1,0:T(8,128)(2,1)}) custom-call(bf16[3,304,512]{2,1,0:T(8,128)(2,1)} %fusion.4.own_ref.x_ref, f32[3,304,512]{2,1,0:T(8,128)} %get-tuple-element.120.gm_ref, f32[8,512]{1,0:T(8,128)S(1)} %get-tuple-element.90.vec_ref, ...), custom_call_target="tpu_custom_call" | custom-call | flops 1000 | bytes 1000 | tf_op jit(solution)/shard_map/input_back/pallas_call | solution.py:1022
  234.8 3.7 %all-to-all-done.2 = bf16[8,256,512]{2,1,0:T(8,128)(2,1)} async-done(((bf16[8,256,512]{2,1,0:T(8,128)(2,1)}), bf16[8,256,512]{2,1,0:T(8,128)(2,1)}, u32[]{:S(2)}, u32[]{:S(2)}) %all-to-all-start.2) | async-done | bytes 2097184 | tf_op jit(solution)/shard_map/all_to_all | solution.py:1241
  238.5 3.9 %all-to-all-start.3 = ((bf16[8,176,512]{2,1,0:T(8,128)(2,1)}), bf16[8,176,512]{2,1,0:T(8,128)(2,1)S(1)}, u32[]{:S(2)}, u32[]{:S(2)}) async-start(bf16[8,176,512]{2,1,0:T(8,128)(2,1)} %get-tuple-element.143), calls=%async_computation.3 | async-start | bytes 2883584 | tf_op jit(solution)/shard_map/all_to_all | solution.py:1253
  243.3 2.7 reduce_sum.33
  259.0 5.8 %layer_combine.1 = bf16[6,145,512]{2,1,0:T(8,128)(2,1)} custom-call(s32[4]{0:T(128)S(1)} %pad_add_fusion.at_ref, f32[3,145,512]{2,1,0:T(8,128)} %get-tuple-element.149.mine_ref, f32[3,145,512]{2,1,0:T(8,128)} %get-tuple-element.150.theirs_ref, bf16[3,2,145,512]{3,2,1,0:T(8,128)(2,1)} %copy.56.got_ref), custom_call_target="tpu_custom_call" | custom-call | flops 1000 | bytes 1000 | tf_op jit(solution)/shard_map/layer_combine/pallas_call | solution.py:864
  264.8 11.9 %all-to-all-done.3 = bf16[8,176,512]{2,1,0:T(8,128)(2,1)S(1)} async-done(((bf16[8,176,512]{2,1,0:T(8,128)(2,1)}), bf16[8,176,512]{2,1,0:T(8,128)(2,1)S(1)}, u32[]{:S(2)}, u32[]{:S(2)}) %all-to-all-start.3) | async-done | bytes 1441824 | tf_op jit(solution)/shard_map/all_to_all | solution.py:1253
  283.4 4.7 %settle_experts.1 = (f32[4,64,2048]{2,1,0:T(8,128)}, f32[4,256,512]{2,1,0:T(8,128)}) custom-call(s32[4]{0:T(128)S(1)} %pad_add_fusion.at_ref, bf16[4,256,512]{2,1,0:T(8,128)(2,1)} %pad_maximum_fusion.zero_ref, bf16[4,256,512]{2,1,0:T(8,128)(2,1)} %pad_maximum_fusion.1.one_ref), custom_call_target="tpu_custom_call" | custom-call | flops 1000 | bytes 1000 | tf_op jit(solution)/shard_map/settle_experts/pallas_call | solution.py:688
  (202 shorter events, 69.8 us)
Async XLA Ops:
  9.9 23.9 %all-to-all-start = ((bf16[4,80,1024]{2,1,0:T(8,128)(2,1)}), bf16[4,80,1024]{2,1,0:T(8,128)(2,1)}, u32[]{:S(2)}, u32[]{:S(2)}) async-start(bf16[4,80,1024]{2,1,0:T(8,128)(2,1)} %broadcast_in_dim.18), calls=%async_computation | async-start | bytes 1310720 | tf_op jit(solution)/shard_map/all_to_all | solution.py:1141
  16.3 71.4 %all-gather.5.cloned.1.call-start = ((), (), s32[]{:S(2)}) async-start(), calls=%async_computation.4 | async-start | bytes 2359296 | tf_op jit(solution)/shard_map/all_gather | solution.py:1144
  17.2 12.5 %collective-permute-start = (bf16[3,145,512]{2,1,0:T(8,128)(2,1)}, bf16[3,145,512]{2,1,0:T(8,128)(2,1)}, u32[]{:S(2)}, u32[]{:S(2)}) collective-permute-start(bf16[3,145,512]{2,1,0:T(8,128)(2,1)} %pad_maximum_fusion.5), channel_id=1, source_target_pairs={{0,2},{1,3},{2,0},{3,1},{4,6},{5,7},{6,4},{7,5},{8,10},{9,11},{10,... | collective-permute-start | bytes 1336328 | tf_op jit(solution)/shard_map/ppermute | solution.py:1068
  34.5 103.4 %all-gather.7.cloned.1.call-start = ((), (), s32[]{:S(2)}) async-start(), calls=%async_computation.5 | async-start | bytes 2359296 | tf_op jit(solution)/shard_map/all_gather | solution.py:1144
  34.8 20.0 %collective-permute-start.2 = (bf16[4,80,1024]{2,1,0:T(8,128)(2,1)}, bf16[4,80,1024]{2,1,0:T(8,128)(2,1)}, u32[]{:S(2)}, u32[]{:S(2)}) collective-permute-start(bf16[4,80,1024]{2,1,0:T(8,128)(2,1)} %all-to-all-done.here_ref), channel_id=1, source_target_pairs={{0,4},{4,0},{8,12},{12,8},{16,20},{20,16},{24,28},{28,24},{1,5},{5... | collective-permute-start | bytes 1966088 | tf_op jit(solution)/shard_map/ppermute | solution.py:1077
  36.3 41.1 %collective-permute-start.6 = (bf16[6,146,512]{2,1,0:T(8,128)(2,1)S(1)}, bf16[6,146,512]{2,1,0:T(8,128)(2,1)}, u32[]{:S(2)}, u32[]{:S(2)}) collective-permute-start(bf16[6,146,512]{2,1,0:T(8,128)(2,1)S(1)} %pad_maximum_fusion.2.cot_ref), channel_id=1, source_target_pairs={{0,2},{1,3},{2,0},{3,1},{4,6},{5,7},{6,4},{7,5},{8,10},{9,11},{10,... | collective-permute-start | bytes 2691080 | tf_op jit(solution)/shard_map/ppermute | solution.py:1068
  79.3 6.4 %collective-permute-start.7 = (bf16[6,304,512]{2,1,0:T(8,128)(2,1)S(1)}, bf16[6,304,512]{2,1,0:T(8,128)(2,1)}, u32[]{:S(2)}, u32[]{:S(2)}) collective-permute-start(bf16[6,304,512]{2,1,0:T(8,128)(2,1)S(1)} %join_cots.1.refs_2_.refs_4_.cot_ref), channel_id=1, source_target_pairs={{0,1},{1,0},{2,3},{3,2},{4,5},{5,4},{6,7},{7,6},{8,9},{9,8},{10,11... | collective-permute-start | bytes 5603336 | tf_op jit(solution)/shard_map/ppermute | solution.py:1068
  79.6 5.2 %collective-permute-start.5 = (bf16[3,304,512]{2,1,0:T(8,128)(2,1)}, bf16[3,304,512]{2,1,0:T(8,128)(2,1)S(1)}, u32[]{:S(2)}, u32[]{:S(2)}) collective-permute-start(bf16[3,304,512]{2,1,0:T(8,128)(2,1)} %copy-done.3), channel_id=1, source_target_pairs={{0,1},{1,0},{2,3},{3,2},{4,5},{5,4},{6,7},{7,6},{8,9},{9,8},{10,11... | collective-permute-start | bytes 2801672 | tf_op jit(solution)/shard_map/ppermute | solution.py:1068
  80.0 24.9 %collective-permute-start.4 = (bf16[3,304,512]{2,1,0:T(8,128)(2,1)}, bf16[3,304,512]{2,1,0:T(8,128)(2,1)}, u32[]{:S(2)}, u32[]{:S(2)}) collective-permute-start(bf16[3,304,512]{2,1,0:T(8,128)(2,1)} %copy-done.3), channel_id=1, source_target_pairs={{0,2},{1,3},{2,0},{3,1},{4,6},{5,7},{6,4},{7,5},{8,10},{9,11},{10,... | collective-permute-start | bytes 2801672 | tf_op jit(solution)/shard_map/ppermute | solution.py:1068
  104.9 2.8 collective-permute-start.8
  131.6 53.7 %all-to-all-start.1 = ((bf16[8,256,512]{2,1,0:T(8,128)(2,1)}), bf16[8,256,512]{2,1,0:T(8,128)(2,1)}, u32[]{:S(2)}, u32[]{:S(2)}) async-start(bf16[8,256,512]{2,1,0:T(8,128)(2,1)} %get-tuple-element.97), calls=%async_computation.1 | async-start | bytes 4194304 | tf_op jit(solution)/shard_map/all_to_all | solution.py:1214
  154.4 25.9 %collective-permute-start.15 = (bf16[3,304,512]{2,1,0:T(8,128)(2,1)S(1)}, bf16[3,304,512]{2,1,0:T(8,128)(2,1)S(1)}, u32[]{:S(2)}, u32[]{:S(2)}) collective-permute-start(bf16[3,304,512]{2,1,0:T(8,128)(2,1)S(1)} %get-tuple-element.137), channel_id=1, source_target_pairs={{0,1},{1,0},{2,3},{3,2},{4,5},{5,4},{6,7},{7,6},{8,9},{9,8},{10,11... | collective-permute-start | bytes 2801672 | tf_op jit(solution)/shard_map/ppermute | solution.py:1068
  157.1 27.4 %collective-permute-start.12 = (bf16[3,304,512]{2,1,0:T(8,128)(2,1)S(1)}, bf16[3,304,512]{2,1,0:T(8,128)(2,1)S(1)}, u32[]{:S(2)}, u32[]{:S(2)}) collective-permute-start(bf16[3,304,512]{2,1,0:T(8,128)(2,1)S(1)} %add.179), channel_id=1, source_target_pairs={{0,2},{1,3},{2,0},{3,1},{4,6},{5,7},{6,4},{7,5},{8,10},{9,11},{10,... | collective-permute-start | bytes 2801672 | tf_op jit(solution)/shard_map/ppermute | solution.py:1068
  158.1 22.1 %collective-permute-start.11 = (bf16[2,304,512]{2,1,0:T(8,128)(2,1)S(1)}, bf16[2,304,512]{2,1,0:T(8,128)(2,1)S(1)}, u32[]{:S(2)}, u32[]{:S(2)}) collective-permute-start(bf16[2,304,512]{2,1,0:T(8,128)(2,1)S(1)} %get-tuple-element.118), channel_id=1, source_target_pairs={{0,1},{1,0},{2,3},{3,2},{4,5},{5,4},{6,7},{7,6},{8,9},{9,8},{10,11... | collective-permute-start | bytes 1867784 | tf_op jit(solution)/shard_map/ppermute | solution.py:1068
  168.4 11.9 %collective-permute-start.14 = (bf16[2,304,512]{2,1,0:T(8,128)(2,1)S(1)}, bf16[2,304,512]{2,1,0:T(8,128)(2,1)S(1)}, u32[]{:S(2)}, u32[]{:S(2)}) collective-permute-start(bf16[2,304,512]{2,1,0:T(8,128)(2,1)S(1)} %get-tuple-element.135), channel_id=1, source_target_pairs={{0,1},{1,0},{2,3},{3,2},{4,5},{5,4},{6,7},{7,6},{8,9},{9,8},{10,11... | collective-permute-start | bytes 1867784 | tf_op jit(solution)/shard_map/ppermute | solution.py:1068
  185.3 53.2 %all-to-all-start.2 = ((bf16[8,256,512]{2,1,0:T(8,128)(2,1)}), bf16[8,256,512]{2,1,0:T(8,128)(2,1)}, u32[]{:S(2)}, u32[]{:S(2)}) async-start(bf16[8,256,512]{2,1,0:T(8,128)(2,1)} %weight_grad.1), calls=%async_computation.2 | async-start | bytes 4194304 | tf_op jit(solution)/shard_map/all_to_all | solution.py:1241
  201.3 24.9 %collective-permute-start.16 = (bf16[3,2,145,512]{3,1,2,0:T(2,128)(2,1)S(1)}, bf16[3,2,145,512]{3,1,2,0:T(2,128)(2,1)S(1)}, u32[]{:S(2)}, u32[]{:S(2)}) collective-permute-start(bf16[3,2,145,512]{3,1,2,0:T(2,128)(2,1)S(1)} %copy.55), channel_id=1, source_target_pairs={{0,2},{1,3},{2,0},{3,1},{4,6},{5,7},{6,4},{7,5},{8,10},{9,11},{10,... | collective-permute-start | bytes 2672648 | tf_op jit(solution)/shard_map/ppermute | solution.py:1068
  238.5 38.2 %all-to-all-start.3 = ((bf16[8,176,512]{2,1,0:T(8,128)(2,1)}), bf16[8,176,512]{2,1,0:T(8,128)(2,1)S(1)}, u32[]{:S(2)}, u32[]{:S(2)}) async-start(bf16[8,176,512]{2,1,0:T(8,128)(2,1)} %get-tuple-element.143), calls=%async_computation.3 | async-start | bytes 2883584 | tf_op jit(solution)/shard_map/all_to_all | solution.py:1253
  242.4 13.7 %collective-permute-start.20 = (bf16[3,145,512]{2,1,0:T(8,128)(2,1)S(1)}, bf16[3,145,512]{2,1,0:T(8,128)(2,1)S(1)}, u32[]{:S(2)}, u32[]{:S(2)}) collective-permute-start(bf16[3,145,512]{2,1,0:T(8,128)(2,1)S(1)} %get-tuple-element.152), channel_id=1, source_target_pairs={{0,2},{1,3},{2,0},{3,1},{4,6},{5,7},{6,4},{7,5},{8,10},{9,11},{10,... | collective-permute-start | bytes 1336328 | tf_op jit(solution)/shard_map/ppermute | solution.py:1068
  246.0 7.0 %collective-permute-start.18 = (bf16[256,512]{1,0:T(8,128)(2,1)}, bf16[256,512]{1,0:T(8,128)(2,1)}, u32[]{:S(2)}, u32[]{:S(2)}) collective-permute-start(bf16[256,512]{1,0:T(8,128)(2,1)} %reduce_sum.33), channel_id=1, source_target_pairs={{0,1},{1,0},{2,3},{3,2},{4,5},{5,4},{6,7},{7,6},{8,9},{9,8},{10,11... | collective-permute-start | bytes 786440 | tf_op jit(solution)/shard_map/ppermute | solution.py:1068
  252.5 5.4 %collective-permute-start.19 = (bf16[256,512]{1,0:T(8,128)(2,1)}, bf16[256,512]{1,0:T(8,128)(2,1)S(1)}, u32[]{:S(2)}, u32[]{:S(2)}) collective-permute-start(bf16[256,512]{1,0:T(8,128)(2,1)} %reduce_sum.34), channel_id=1, source_target_pairs={{0,1},{1,0},{2,3},{3,2},{4,5},{5,4},{6,7},{7,6},{8,9},{9,8},{10,11... | collective-permute-start | bytes 786440 | tf_op jit(solution)/shard_map/ppermute | solution.py:1068
  254.9 23.1 %collective-permute-start.23 = (bf16[2,256,512]{2,1,0:T(8,128)(2,1)}, bf16[2,256,512]{2,1,0:T(8,128)(2,1)}, u32[]{:S(2)}, u32[]{:S(2)}) collective-permute-start(bf16[2,256,512]{2,1,0:T(8,128)(2,1)} %pad_maximum_fusion.3), channel_id=1, source_target_pairs={{0,2},{1,3},{2,0},{3,1},{4,6},{5,7},{6,4},{7,5},{8,10},{9,11},{10,... | collective-permute-start | bytes 1572872 | tf_op jit(solution)/shard_map/ppermute | solution.py:1068
  258.0 23.2 %collective-permute-start.24 = (bf16[2,256,512]{2,1,0:T(8,128)(2,1)S(1)}, bf16[2,256,512]{2,1,0:T(8,128)(2,1)}, u32[]{:S(2)}, u32[]{:S(2)}) collective-permute-start(bf16[2,256,512]{2,1,0:T(8,128)(2,1)S(1)} %pad_maximum_fusion.4), channel_id=1, source_target_pairs={{0,2},{1,3},{2,0},{3,1},{4,6},{5,7},{6,4},{7,5},{8,10},{9,11},{10,... | collective-permute-start | bytes 1572872 | tf_op jit(solution)/shard_map/ppermute | solution.py:1068
  277.1 11.0 %collective-permute-start.21 = (bf16[192,512]{1,0:T(8,128)(2,1)S(1)}, bf16[192,512]{1,0:T(8,128)(2,1)S(1)}, u32[]{:S(2)}, u32[]{:S(2)}) collective-permute-start(bf16[192,512]{1,0:T(8,128)(2,1)S(1)} %pad_maximum_fusion.8), channel_id=1, source_target_pairs={{0,2},{1,3},{2,0},{3,1},{4,6},{5,7},{6,4},{7,5},{8,10},{9,11},{10,... | collective-permute-start | bytes 589832 | tf_op jit(solution)/shard_map/ppermute | solution.py:1068
  (41 other events, 222.9 us)
Sparse Core Ops, SparseCore 0:
  34.7 53.0 all-gather.4
  89.9 48.0 all-gather.6
